TPU v7x, 32 devices: a whole 2x2x4 slice. The times are simulated.
32 devices in a mesh: dp: 8 (over z, x), tp: 4 (over y, core).
Axes of the slice: x: 2, y: 2, z: 4, core: 2. Of those that a mesh axis runs over, the one named last changes fastest.
Arguments:
- block_input: bfloat16 [2, 16384, 1152], P(None, ('dp', 'tp')), may hold values from -6 to 6
- segment_ids: int32 [2, 16384], P(None, 'dp'), may hold values from 0 to 3, as said below
- conditioning: bfloat16 [2, 64, 1152], P(None, 'dp'), may hold values from -6 to 6
- w_qkv: bfloat16 [3, 1152, 1152], P(None, 'dp', 'tp'), may hold values from -0.1875 to 0.1875
- qv_bias: bfloat16 [2, 1152], replicated, may hold values from -3 to 3
- w_out: bfloat16 [1152, 1152], P('tp', 'dp'), may hold values from -1.5 to 1.5
- out_bias: bfloat16 [1152], replicated, may hold values from -3 to 3
- w_fc1: bfloat16 [1152, 4608], P('dp', 'tp'), may hold values from -0.1875 to 0.1875
- fc1_bias: bfloat16 [4608], replicated, may hold values from -3 to 3
- w_fc2: bfloat16 [4608, 1152], P('tp', 'dp'), may hold values from -0.09375 to 0.09375
- fc2_bias: bfloat16 [1152], replicated, may hold values from -3 to 3
- w_ada: bfloat16 [1152, 6912], P('dp', 'tp'), may hold values from -0.1875 to 0.1875
- ada_bias: bfloat16 [6912], replicated, may hold values from -3 to 3
- cotangent: bfloat16 [2, 16384, 1152], P(None, ('dp', 'tp')), may hold values from -6 to 6
Outputs:
- block_output: bfloat16 [2, 16384, 1152], P(None, ('dp', 'tp'))
- input_grad: bfloat16 [2, 16384, 1152], P(None, ('dp', 'tp'))
- w_qkv_grad: float32 [3, 1152, 1152], P(None, 'dp', 'tp')
- qv_bias_grad: float32 [2, 1152], replicated
- w_out_grad: float32 [1152, 1152], P('tp', 'dp')
- out_bias_grad: float32 [1152], replicated
- w_fc1_grad: float32 [1152, 4608], P('dp', 'tp')
- fc1_bias_grad: float32 [4608], replicated
- w_fc2_grad: float32 [4608, 1152], P('tp', 'dp')
- fc2_bias_grad: float32 [1152], replicated
- w_ada_grad: float32 [1152, 6912], P('dp', 'tp')
- ada_bias_grad: float32 [6912], replicated
Inputs may be any that keep to these rules, and one draw needn't show every extreme that they name: `segment_ids`: within each packed row of 1024 tokens the ids never fall, and every image of the row holds at least one token.
All inputs are finite; a program needn't handle non-finite values.
Results may differ from a plain program's by a relative error of at most 0.02.
The roundings to bfloat16 on the way count: a program that leaves them out, or rounds other values in their place, can miss the bound.
Values may be sent and summed in bfloat16 or wider, within the bound.
No kernel may reach another device: no remote copies, remote signals or barrier semaphores. Data moves between devices by JAX's collectives and lax.ppermute only.
A program may use at most 320 MiB of HBM per device.

v0:
```python
import math

import jax
import jax.numpy as jnp
from jax import lax
from jax.sharding import PartitionSpec as P

HD = 72
PACK = 1024
IMG_ROW = 4


highest = lax.Precision.HIGHEST
epsilon = 1e-06
masked_score = -1e30


def layer_norm(values):
    centred = values - jnp.mean(values, axis=-1, keepdims=True)
    return centred * lax.rsqrt(jnp.mean(centred * centred, axis=-1, keepdims=True) + epsilon)


def gelu_tanh(values):
    return (
        0.5
        * values
        * (1.0 + jnp.tanh(0.7978845608028654 * (values + 0.044715 * values * values * values)))
    )


def smooth_gate(values):
    return values / (1.0 + jnp.exp(-values))


def to_blocks(values, local_heads):
    shaped = values.reshape(values.shape[0] // PACK, PACK, local_heads, HD)
    return shaped.transpose(0, 2, 1, 3).reshape(-1, PACK, HD)


def from_blocks(blocks, local_heads):
    shaped = blocks.reshape(-1, local_heads, PACK, HD).transpose(0, 2, 1, 3)
    return shaped.reshape(-1, local_heads * HD)


def block_segments(segment_group, local_heads):
    shaped = segment_group.reshape(-1, 1, PACK)
    return jnp.broadcast_to(shaped, (shaped.shape[0], local_heads, PACK)).reshape(-1, PACK)


def project_heads(activations, full_qkv, bias_pair):
    projected = jnp.einsum("gd,cde->cge", activations, full_qkv, preferred_element_type=jnp.float32)
    bias_rows = jnp.stack([bias_pair[0], jnp.zeros_like(bias_pair[0]), bias_pair[1]])
    return (projected + bias_rows[:, None, :]).astype(jnp.bfloat16)


def masked_scores(query_rows, key_rows, segment_row):
    raw_scores = lax.dot_general(
        query_rows, key_rows, (((1,), (1,)), ((), ())), preferred_element_type=jnp.float32
    ) / math.sqrt(HD)
    same_image = segment_row[:, None] == segment_row[None, :]
    return (same_image, jnp.where(same_image, raw_scores, masked_score))


def attend_forward(block_items):
    query_rows, key_rows, value_rows, segment_row = block_items
    same_image, scores = masked_scores(query_rows, key_rows, segment_row)
    row_max = jnp.max(scores, axis=-1, keepdims=True)
    exponents = jnp.exp(scores - row_max)
    row_sums = jnp.sum(exponents, axis=-1, keepdims=True)
    probs_low = (exponents / row_sums).astype(jnp.bfloat16)
    attended = jnp.dot(probs_low, value_rows, preferred_element_type=jnp.float32).astype(
        jnp.bfloat16
    )
    return (attended, (row_max + jnp.log(row_sums))[:, 0])


def attend_backward(block_items):
    query_rows, key_rows, value_rows, segment_row, log_total, attended_grad = block_items
    same_image, scores = masked_scores(query_rows, key_rows, segment_row)
    attn_probs = jnp.where(same_image, jnp.exp(scores - log_total[:, None]), 0.0)
    value_grad = lax.dot_general(
        attn_probs.astype(jnp.bfloat16),
        attended_grad,
        (((0,), (0,)), ((), ())),
        preferred_element_type=jnp.float32,
    )
    probs_grad = lax.dot_general(
        attended_grad, value_rows, (((1,), (1,)), ((), ())), preferred_element_type=jnp.float32
    )
    centred = probs_grad - jnp.sum(attn_probs * probs_grad, axis=-1, keepdims=True)
    scores_grad = (attn_probs * centred).astype(jnp.bfloat16)
    query_grad = jnp.dot(scores_grad, key_rows, preferred_element_type=jnp.float32) / math.sqrt(HD)
    key_grad = lax.dot_general(
        scores_grad, query_rows, (((0,), (0,)), ((), ())), preferred_element_type=jnp.float32
    ) / math.sqrt(HD)
    return (
        query_grad.astype(jnp.bfloat16),
        key_grad.astype(jnp.bfloat16),
        value_grad.astype(jnp.bfloat16),
    )


def body(
    block_input,
    segment_ids,
    conditioning,
    w_qkv,
    qv_bias,
    w_out,
    out_bias,
    w_fc1,
    fc1_bias,
    w_fc2,
    fc2_bias,
    w_ada,
    ada_bias,
    cotangent,
):
    micro_count, tok_dev, model_width = block_input.shape
    tp_size = lax.axis_size("tp")
    tp_rank = lax.axis_index("tp")
    heads_dev = w_qkv.shape[2]
    hidden_dev = w_fc1.shape[1]
    mod_dev = w_ada.shape[1]
    cond_width = conditioning.shape[2]
    images = conditioning.shape[1]
    local_heads = heads_dev // HD
    qv_local = lax.dynamic_slice_in_dim(
        qv_bias.astype(jnp.float32), tp_rank * heads_dev, heads_dev, 1
    )
    fc1_local = lax.dynamic_slice_in_dim(
        fc1_bias.astype(jnp.float32), tp_rank * hidden_dev, hidden_dev, 0
    )
    ada_local = lax.dynamic_slice_in_dim(
        ada_bias.astype(jnp.float32), tp_rank * mod_dev, mod_dev, 0
    )
    out_bias_f = out_bias.astype(jnp.float32)
    fc2_bias_f = fc2_bias.astype(jnp.float32)
    positions = tp_rank * tok_dev + jnp.arange(tok_dev, dtype=jnp.int32)
    grad_qkv = jnp.zeros((3, model_width, heads_dev), jnp.float32)
    grad_out_w = jnp.zeros((heads_dev, model_width), jnp.float32)
    grad_fc1 = jnp.zeros((model_width, hidden_dev), jnp.float32)
    grad_fc2 = jnp.zeros((hidden_dev, model_width), jnp.float32)
    grad_ada = jnp.zeros((cond_width, mod_dev), jnp.float32)
    sum_qv = jnp.zeros((2, heads_dev), jnp.float32)
    sum_out_bias = jnp.zeros((model_width,), jnp.float32)
    sum_fc1 = jnp.zeros((hidden_dev,), jnp.float32)
    sum_fc2 = jnp.zeros((model_width,), jnp.float32)
    sum_ada = jnp.zeros((mod_dev,), jnp.float32)
    outputs = []
    input_grads = []
    for micro_step in range(micro_count):
        full_qkv, full_out, full_fc1, full_fc2, full_ada = (
            lax.all_gather(w_qkv, "dp", axis=1, tiled=True),
            lax.all_gather(w_out, "dp", axis=1, tiled=True),
            lax.all_gather(w_fc1, "dp", axis=0, tiled=True),
            lax.all_gather(w_fc2, "dp", axis=1, tiled=True),
            lax.all_gather(w_ada, "dp", axis=0, tiled=True),
        )
        lifted = smooth_gate(conditioning[micro_step].astype(jnp.float32)).astype(jnp.bfloat16)
        mod_part = jnp.dot(lifted, full_ada, preferred_element_type=jnp.float32) + ada_local
        modulation = lax.all_gather(mod_part, "tp", axis=1, tiled=True)
        segment_group = segment_ids[micro_step]
        segment_local = lax.dynamic_slice_in_dim(segment_group, tp_rank * tok_dev, tok_dev, 0)
        image_index = positions // PACK * IMG_ROW + segment_local
        onehot = (image_index[:, None] == jnp.arange(images, dtype=jnp.int32)[None, :]).astype(
            jnp.float32
        )
        token_mod = jnp.dot(onehot, modulation, precision=highest)
        shift_one, scale_one, gate_one, shift_two, scale_two, gate_two = jnp.split(
            token_mod, 6, axis=1
        )
        inputs = block_input[micro_step].astype(jnp.float32)
        normed_one = layer_norm(inputs)
        attn_in = (normed_one * (1.0 + scale_one) + shift_one).astype(jnp.bfloat16)
        attn_full = lax.all_gather(attn_in, "tp", axis=0, tiled=True)
        projected = project_heads(attn_full, full_qkv, qv_local)
        segment_blocks = block_segments(segment_group, local_heads)
        attended_blocks, log_totals = lax.map(
            attend_forward,
            (
                to_blocks(projected[0], local_heads),
                to_blocks(projected[1], local_heads),
                to_blocks(projected[2], local_heads),
                segment_blocks,
            ),
        )
        attended = from_blocks(attended_blocks, local_heads)
        branch_one = lax.psum_scatter(
            jnp.dot(attended, full_out, preferred_element_type=jnp.float32).astype(jnp.bfloat16),
            "tp",
            scatter_dimension=0,
            tiled=True,
        ).astype(jnp.float32)
        hidden = inputs + gate_one * (branch_one + out_bias_f)
        normed_two = layer_norm(hidden)
        mlp_in = (normed_two * (1.0 + scale_two) + shift_two).astype(jnp.bfloat16)
        mlp_full = lax.all_gather(mlp_in, "tp", axis=0, tiled=True)
        pre_act = jnp.dot(mlp_full, full_fc1, preferred_element_type=jnp.float32) + fc1_local
        activated = gelu_tanh(pre_act).astype(jnp.bfloat16)
        branch_two = lax.psum_scatter(
            jnp.dot(activated, full_fc2, preferred_element_type=jnp.float32).astype(jnp.bfloat16),
            "tp",
            scatter_dimension=0,
            tiled=True,
        ).astype(jnp.float32)
        outputs.append((hidden + gate_two * (branch_two + fc2_bias_f)).astype(jnp.bfloat16))
        grad_y = cotangent[micro_step].astype(jnp.float32)
        sum_fc2 = sum_fc2 + jnp.sum(gate_two * grad_y, axis=0)
        grad_gate_two = grad_y * (branch_two + fc2_bias_f)
        grad_branch_two = (gate_two * grad_y).astype(jnp.bfloat16)
        grad_two_full = lax.all_gather(grad_branch_two, "tp", axis=0, tiled=True)
        attn_back, mlp_back = (
            lax.all_gather(attn_in, "tp", axis=0, tiled=True),
            lax.all_gather(mlp_in, "tp", axis=0, tiled=True),
        )
        proj_back = project_heads(attn_back, full_qkv, qv_local)
        pre_back = jnp.dot(mlp_back, full_fc1, preferred_element_type=jnp.float32) + fc1_local
        act_back, gelu_pull = jax.vjp(gelu_tanh, pre_back)
        grad_fc2 = grad_fc2 + lax.dot_general(
            act_back.astype(jnp.bfloat16),
            grad_two_full,
            (((0,), (0,)), ((), ())),
            preferred_element_type=jnp.float32,
        )
        grad_act = lax.dot_general(
            grad_two_full, full_fc2, (((1,), (1,)), ((), ())), preferred_element_type=jnp.float32
        )
        grad_pre = gelu_pull(grad_act)[0].astype(jnp.bfloat16)
        sum_fc1 = sum_fc1 + jnp.sum(grad_pre.astype(jnp.float32), axis=0)
        grad_fc1 = grad_fc1 + lax.dot_general(
            mlp_back, grad_pre, (((0,), (0,)), ((), ())), preferred_element_type=jnp.float32
        )
        grad_mlp_in = lax.psum_scatter(
            lax.dot_general(
                grad_pre, full_fc1, (((1,), (1,)), ((), ())), preferred_element_type=jnp.float32
            ).astype(jnp.bfloat16),
            "tp",
            scatter_dimension=0,
            tiled=True,
        ).astype(jnp.float32)
        norm_two_pull = jax.vjp(layer_norm, hidden)[1]
        grad_hidden = grad_y + norm_two_pull(grad_mlp_in * (1.0 + scale_two))[0]
        sum_out_bias = sum_out_bias + jnp.sum(gate_one * grad_hidden, axis=0)
        grad_gate_one = grad_hidden * (branch_one + out_bias_f)
        grad_branch_one = (gate_one * grad_hidden).astype(jnp.bfloat16)
        grad_one_full = lax.all_gather(grad_branch_one, "tp", axis=0, tiled=True)
        grad_out_w = grad_out_w + lax.dot_general(
            attended, grad_one_full, (((0,), (0,)), ((), ())), preferred_element_type=jnp.float32
        )
        grad_attended = lax.dot_general(
            grad_one_full, full_out, (((1,), (1,)), ((), ())), preferred_element_type=jnp.float32
        ).astype(jnp.bfloat16)
        query_blocks, key_blocks, value_blocks = lax.map(
            attend_backward,
            (
                to_blocks(proj_back[0], local_heads),
                to_blocks(proj_back[1], local_heads),
                to_blocks(proj_back[2], local_heads),
                segment_blocks,
                log_totals,
                to_blocks(grad_attended, local_heads),
            ),
        )
        grad_proj = jnp.stack(
            [
                from_blocks(query_blocks, local_heads),
                from_blocks(key_blocks, local_heads),
                from_blocks(value_blocks, local_heads),
            ]
        )
        sum_qv = sum_qv + jnp.stack(
            [
                jnp.sum(grad_proj[0].astype(jnp.float32), axis=0),
                jnp.sum(grad_proj[2].astype(jnp.float32), axis=0),
            ]
        )
        grad_qkv = grad_qkv + jnp.einsum(
            "gd,cge->cde", attn_back, grad_proj, preferred_element_type=jnp.float32
        )
        grad_attn_in = lax.psum_scatter(
            jnp.einsum(
                "cge,cde->gd", grad_proj, full_qkv, preferred_element_type=jnp.float32
            ).astype(jnp.bfloat16),
            "tp",
            scatter_dimension=0,
            tiled=True,
        ).astype(jnp.float32)
        norm_one_pull = jax.vjp(layer_norm, inputs)[1]
        input_grads.append(
            (grad_hidden + norm_one_pull(grad_attn_in * (1.0 + scale_one))[0]).astype(jnp.bfloat16)
        )
        grad_token_mod = jnp.concatenate(
            [
                grad_attn_in,
                grad_attn_in * normed_one,
                grad_gate_one,
                grad_mlp_in,
                grad_mlp_in * normed_two,
                grad_gate_two,
            ],
            axis=1,
        )
        mod_grad_part = lax.dot_general(
            onehot, grad_token_mod, (((0,), (0,)), ((), ())), precision=highest
        )
        grad_mod = lax.psum_scatter(
            mod_grad_part.astype(jnp.bfloat16), "tp", scatter_dimension=1, tiled=True
        ).astype(jnp.float32)
        sum_ada = sum_ada + jnp.sum(grad_mod, axis=0)
        grad_ada = grad_ada + lax.dot_general(
            lifted.astype(jnp.float32), grad_mod, (((0,), (0,)), ((), ())), precision=highest
        )
    qkv_shard, out_shard, fc1_shard, fc2_shard, ada_shard = (
        lax.psum_scatter(
            grad_qkv.astype(jnp.bfloat16), "dp", scatter_dimension=1, tiled=True
        ).astype(jnp.float32),
        lax.psum_scatter(
            grad_out_w.astype(jnp.bfloat16), "dp", scatter_dimension=1, tiled=True
        ).astype(jnp.float32),
        lax.psum_scatter(
            grad_fc1.astype(jnp.bfloat16), "dp", scatter_dimension=0, tiled=True
        ).astype(jnp.float32),
        lax.psum_scatter(
            grad_fc2.astype(jnp.bfloat16), "dp", scatter_dimension=1, tiled=True
        ).astype(jnp.float32),
        lax.psum_scatter(
            grad_ada.astype(jnp.bfloat16), "dp", scatter_dimension=0, tiled=True
        ).astype(jnp.float32),
    )
    qv_full = lax.dynamic_update_slice_in_dim(
        jnp.zeros((2, model_width), jnp.float32), sum_qv, tp_rank * heads_dev, 1
    )
    fc1_full = lax.dynamic_update_slice_in_dim(
        jnp.zeros((hidden_dev * tp_size,), jnp.float32), sum_fc1, tp_rank * hidden_dev, 0
    )
    ada_full = lax.dynamic_update_slice_in_dim(
        jnp.zeros((mod_dev * tp_size,), jnp.float32), sum_ada, tp_rank * mod_dev, 0
    )
    qv_total, out_total, fc1_total, fc2_total, ada_total = lax.psum(
        (qv_full, sum_out_bias, fc1_full, sum_fc2, ada_full), ("dp", "tp")
    )
    return (
        jnp.stack(outputs),
        jnp.stack(input_grads),
        qkv_shard,
        qv_total,
        out_shard,
        out_total,
        fc1_shard,
        fc1_total,
        fc2_shard,
        fc2_total,
        ada_shard,
        ada_total,
    )


def solution(mesh):
    placed = (
        P(None, ("dp", "tp"), None),
        P(None, "dp"),
        P(None, "dp", None),
        P(None, "dp", "tp"),
        P(),
        P("tp", "dp"),
        P(),
        P("dp", "tp"),
        P(),
        P("tp", "dp"),
        P(),
        P("dp", "tp"),
        P(),
        P(None, ("dp", "tp"), None),
    )
    return jax.shard_map(
        body,
        mesh=mesh,
        in_specs=placed,
        out_specs=(
            P(None, ("dp", "tp"), None),
            P(None, ("dp", "tp"), None),
            P(None, "dp", "tp"),
            P(),
            P("tp", "dp"),
            P(),
            P("dp", "tp"),
            P(),
            P("tp", "dp"),
            P(),
            P("dp", "tp"),
            P(),
        ),
        check_vma=False,
    )
```

profile of v0, /device:TPU:0, one launch (start us, length us, event | category | flops | bytes accessed | tf_op | source)
XLA Modules:
  0.0 1956.4 jit_solution(10573483748032254643)
XLA Ops:
  14.6 70.9 %all-gather.15.cloned.1.call-done = bf16[1152,1728]{1,0:T(8,128)(2,1)} async-done(((bf16[144,1728]{1,0:T(8,128)(2,1)}), bf16[1152,1728]{1,0:T(8,128)(2,1)}) %all-gather.15.cloned.1.call-update) | async-done | bytes 3981328 | tf_op jit(solution)/shard_map/all_gather | solution.py:158
  107.7 47.6 %all_gather.58 = bf16[288,1152]{0,1:T(8,128)(2,1)} all-gather(bf16[288,144]{0,1:T(8,128)(2,1)S(1)} %copy-done.61), channel_id=1, replica_groups=mesh['dp'=8,'tp'=4] {'dp'}, dimensions={1}, use_global_device_ids=true | all-gather | bytes 746496 | tf_op jit(solution)/shard_map/all_gather | solution.py:155
  155.3 37.5 %all-gather.17.cloned.1.call-done = bf16[2048,1152]{1,0:T(8,128)(2,1)} async-done(((bf16[512,1152]{1,0:T(8,128)(2,1)}), bf16[2048,1152]{1,0:T(8,128)(2,1)}) %all-gather.17.cloned.1.call-update) | async-done | bytes 4718608 | tf_op jit(solution)/shard_map/all_gather | solution.py:176
  223.7 34.7 %while.52 = (s32[]{:T(128)}, bf16[8,1024,72]{1,2,0:T(8,128)(2,1)S(1)}, f32[8,1024]{1,0:T(8,128)S(1)}, s32[8,1024]{1,0:T(8,128)S(1)}, bf16[8,1024,72]{2,1,0:T(8,1...) while((s32[]{:T(128)}, ...), condition=%wide.region_5.6_spmd, body=%wide.region_2.5_spmd.sunk | while | flops 317791232 | bytes 13588589 | solution.py:179
  266.3 47.3 %reduce-scatter.22.cloned.1.call-done = bf16[512,1152]{1,0:T(8,128)(2,1)} async-done(((bf16[2048,1152]{1,0:T(8,128)(2,1)}), bf16[512,1152]{1,0:T(8,128)(2,1)}) %reduce-scatter.22.cloned.1.call-update) | async-done | bytes 1179664 | tf_op jit(solution)/shard_map/reduce_scatter | solution.py:189
  326.3 44.5 %all-gather.23.cloned.1.call-done = bf16[1152,1152]{1,0:T(8,128)(2,1)} async-done(((bf16[144,1152]{1,0:T(8,128)(2,1)}), bf16[1152,1152]{1,0:T(8,128)(2,1)}) %all-gather.23.cloned.1.call-update) | async-done | bytes 2654224 | tf_op jit(solution)/shard_map/all_gather | solution.py:156
  370.8 38.1 %all-gather.21.cloned.1.call-done = bf16[2048,1152]{1,0:T(8,128)(2,1)} async-done(((bf16[512,1152]{1,0:T(8,128)(2,1)}), bf16[2048,1152]{1,0:T(8,128)(2,1)}) %all-gather.21.cloned.1.call-update) | async-done | bytes 4718608 | tf_op jit(solution)/shard_map/all_gather | solution.py:198
  420.8 45.7 %all-gather.25.cloned.1.call-done = bf16[1152,1152]{0,1:T(8,128)(2,1)} async-done(((bf16[1152,144]{0,1:T(8,128)(2,1)}), bf16[1152,1152]{0,1:T(8,128)(2,1)}) %all-gather.25.cloned.1.call-update) | async-done | bytes 2654224 | tf_op jit(solution)/shard_map/all_gather | solution.py:157
  479.5 24.6 %all-gather.31.cloned.1.call-done = bf16[2048,1152]{1,0:T(8,128)(2,1)} async-done(((bf16[512,1152]{1,0:T(8,128)(2,1)}), bf16[2048,1152]{1,0:T(8,128)(2,1)}) %all-gather.31.cloned.1.call-update) | async-done | bytes 4718608 | tf_op jit(solution)/shard_map/all_gather | solution.py:212
  504.2 17.7 convert_reduce_fusion.1
  533.4 21.3 %reduce-scatter.24.cloned.1.call-done = bf16[512,1152]{1,0:T(8,128)(2,1)} async-done(((bf16[2048,1152]{1,0:T(8,128)(2,1)}), bf16[512,1152]{1,0:T(8,128)(2,1)}) %reduce-scatter.24.cloned.1.call-update) | async-done | bytes 1179664 | tf_op jit(solution)/shard_map/reduce_scatter | solution.py:201
  554.7 50.2 %reduce-scatter.30.cloned.1.call-done = bf16[512,1152]{1,0:T(8,128)(2,1)} async-done(((bf16[2048,1152]{1,0:T(8,128)(2,1)}), bf16[512,1152]{1,0:T(8,128)(2,1)}) %reduce-scatter.30.cloned.1.call-update) | async-done | bytes 1179664 | tf_op jit(solution)/shard_map/reduce_scatter | solution.py:234
  617.3 37.6 %all-gather.33.cloned.1.call-done = bf16[2048,1152]{1,0:T(8,128)(2,1)} async-done(((bf16[512,1152]{1,0:T(8,128)(2,1)}), bf16[2048,1152]{1,0:T(8,128)(2,1)}) %all-gather.33.cloned.1.call-update) | async-done | bytes 4718608 | tf_op jit(solution)/shard_map/all_gather | solution.py:247
  664.9 87.5 %while.54 = (s32[]{:T(128)}, bf16[8,1024,72]{1,2,0:T(8,128)(2,1)}, bf16[8,1024,72]{1,2,0:T(8,128)(2,1)}, bf16[8,1024,72]{1,2,0:T(8,128)(2,1)S(1)}, s32[8,1024]{1...) while((s32[]{:T(128)}, bf16[8,1024,72]{1,2,0:T(8,128)(2,1)}, ...), condition=%wide.region_25.26_spmd, body=%wide.region_23.25_spmd.sunk | while | flops 766876672 | bytes 33776764 | solution.py:254
  799.0 29.6 %reduce-scatter.32.cloned.1.call-done = bf16[512,1152]{1,0:T(8,128)(2,1)} async-done(((bf16[2048,1152]{1,0:T(8,128)(2,1)}), bf16[512,1152]{1,0:T(8,128)(2,1)}) %reduce-scatter.32.cloned.1.call-update) | async-done | bytes 1179664 | tf_op jit(solution)/shard_map/reduce_scatter | solution.py:281
  839.2 37.3 %all-gather.27.cloned.1.call-done = bf16[2048,1152]{1,0:T(8,128)(2,1)} async-done(((bf16[512,1152]{1,0:T(8,128)(2,1)}), bf16[2048,1152]{1,0:T(8,128)(2,1)}) %all-gather.27.cloned.1.call-update) | async-done | bytes 4718608 | tf_op jit(solution)/shard_map/all_gather | solution.py:176
  907.5 34.7 %while.53 = (s32[]{:T(128)}, bf16[8,1024,72]{1,2,0:T(8,128)(2,1)S(1)}, f32[8,1024]{1,0:T(8,128)S(1)}, s32[8,1024]{1,0:T(8,128)S(1)}, bf16[8,1024,72]{2,1,0:T(8,1...) while((s32[]{:T(128)}, ...), condition=%wide.region_15.16_spmd, body=%wide.region_12.15_spmd.sunk | while | flops 317791232 | bytes 13588589 | solution.py:179
  949.4 48.0 %reduce-scatter.26.cloned.1.call-done = bf16[512,1152]{1,0:T(8,128)(2,1)} async-done(((bf16[2048,1152]{1,0:T(8,128)(2,1)}), bf16[512,1152]{1,0:T(8,128)(2,1)}) %reduce-scatter.26.cloned.1.call-update) | async-done | bytes 1179664 | tf_op jit(solution)/shard_map/reduce_scatter | solution.py:189
  1007.6 37.0 %all-gather.29.cloned.1.call-done = bf16[2048,1152]{1,0:T(8,128)(2,1)} async-done(((bf16[512,1152]{1,0:T(8,128)(2,1)}), bf16[2048,1152]{1,0:T(8,128)(2,1)}) %all-gather.29.cloned.1.call-update) | async-done | bytes 4718608 | tf_op jit(solution)/shard_map/all_gather | solution.py:198
  1056.7 27.5 %all-gather.35.cloned.1.call-done = bf16[2048,1152]{1,0:T(8,128)(2,1)} async-done(((bf16[512,1152]{1,0:T(8,128)(2,1)}), bf16[2048,1152]{1,0:T(8,128)(2,1)}) %all-gather.35.cloned.1.call-update) | async-done | bytes 4718608 | tf_op jit(solution)/shard_map/all_gather | solution.py:212
  1084.1 17.3 convert_reduce_fusion
  1125.7 34.5 %reduce-scatter.34.cloned.1.call-done = bf16[512,1152]{1,0:T(8,128)(2,1)} async-done(((bf16[2048,1152]{1,0:T(8,128)(2,1)}), bf16[512,1152]{1,0:T(8,128)(2,1)}) %reduce-scatter.34.cloned.1.call-update) | async-done | bytes 1179664 | tf_op jit(solution)/shard_map/reduce_scatter | solution.py:234
  1164.1 46.4 %reduce-scatter.28.cloned.1.call-done = bf16[512,1152]{1,0:T(8,128)(2,1)} async-done(((bf16[2048,1152]{1,0:T(8,128)(2,1)}), bf16[512,1152]{1,0:T(8,128)(2,1)}) %reduce-scatter.28.cloned.1.call-update) | async-done | bytes 1179664 | tf_op jit(solution)/shard_map/reduce_scatter | solution.py:201
  1219.5 37.5 %all-gather.37.cloned.1.call-done = bf16[2048,1152]{1,0:T(8,128)(2,1)} async-done(((bf16[512,1152]{1,0:T(8,128)(2,1)}), bf16[2048,1152]{1,0:T(8,128)(2,1)}) %all-gather.37.cloned.1.call-update) | async-done | bytes 4718608 | tf_op jit(solution)/shard_map/all_gather | solution.py:247
  1275.1 112.9 %while.55 = (s32[]{:T(128)}, bf16[8,1024,72]{1,2,0:T(8,128)(2,1)}, bf16[8,1024,72]{1,2,0:T(8,128)(2,1)}, bf16[8,1024,72]{1,2,0:T(8,128)(2,1)}, s32[8,1024]{1,0:T...) while((s32[]{:T(128)}, bf16[8,1024,72]{1,2,0:T(8,128)(2,1)}, ...), condition=%wide.region_34.35_spmd, body=%wide.region_32.34_spmd.sunk | while | flops 766876672 | bytes 33776764 | solution.py:254
  1438.3 33.2 %reduce-scatter.36.cloned.1.call-done = bf16[512,1152]{1,0:T(8,128)(2,1)} async-done(((bf16[2048,1152]{1,0:T(8,128)(2,1)}), bf16[512,1152]{1,0:T(8,128)(2,1)}) %reduce-scatter.36.cloned.1.call-update) | async-done | bytes 1179664 | tf_op jit(solution)/shard_map/reduce_scatter | solution.py:281
  1620.6 28.1 %reduce-scatter.40.cloned.1.call-done = bf16[144,1152]{1,0:T(8,128)(2,1)} async-done(((bf16[1152,1152]{1,0:T(8,128)(2,1)}), bf16[144,1152]{1,0:T(8,128)(2,1)}) %reduce-scatter.40.cloned.1.call-update) | async-done | bytes 331792 | tf_op jit(solution)/shard_map/reduce_scatter | solution.py:321
  1650.6 71.6 %reduce-scatter.42.cloned.1.call-done = bf16[1152,144]{0,1:T(8,128)(2,1)} async-done(((bf16[1152,1152]{0,1:T(8,128)(2,1)}), bf16[1152,144]{0,1:T(8,128)(2,1)}) %reduce-scatter.42.cloned.1.call-update) | async-done | bytes 331792 | tf_op jit(solution)/shard_map/reduce_scatter | solution.py:324
  1733.0 53.3 %reduce-scatter.38.cloned.1.call-done = bf16[288,144]{0,1:T(8,128)(2,1)} async-done(((bf16[288,1152]{0,1:T(8,128)(2,1)}), bf16[288,144]{0,1:T(8,128)(2,1)}) %reduce-scatter.38.cloned.1.call-update) | async-done | bytes 82960 | tf_op jit(solution)/shard_map/reduce_scatter | solution.py:318
  1787.9 68.0 %reduce-scatter.46.cloned.1.call-done = bf16[144,864]{1,0:T(8,128)(2,1)} async-done(((bf16[1152,864]{1,0:T(8,128)(2,1)}), bf16[144,864]{1,0:T(8,128)(2,1)}) %reduce-scatter.46.cloned.1.call-update) | async-done | bytes 248848
  1861.1 44.0 %all-reduce = (f32[2,1152]{1,0:T(2,128)}, f32[1152]{0:T(1024)}, f32[4608]{0:T(1024)}, f32[1152]{0:T(1024)}, f32[6912]{0:T(1024)}) all-reduce(f32[2,1152]{1,0:T(2,128)S(1)} %dynamic_update_slice.41, f32[1152]{0:T(1024)S(1)} %add.440, f32[4608]{0:T(1024)} %add_dynamic-update-slice_fusion.1, ...), channel_id=1, replica_groups=mesh['dp'=8,'tp'=4] {'dp','tp'}, use_global_device_ids=true, to_apply=%region_43.44 | all-reduce | flops 16128 | bytes 129024 | tf_op jit(solution)/shard_map/psum | solution.py:340
  1905.2 42.1 %reduce-scatter.44.cloned.1.call-done = bf16[144,1728]{1,0:T(8,128)(2,1)} async-done(((bf16[1152,1728]{1,0:T(8,128)(2,1)}), bf16[144,1728]{1,0:T(8,128)(2,1)}) %reduce-scatter.44.cloned.1.call-update) | async-done | bytes 497680 | tf_op jit(solution)/shard_map/reduce_scatter | solution.py:327
  (688 shorter events, 800.8 us)
Async XLA Ops:
  7.2 78.3 %all-gather.15.cloned.1.call-start = ((), (), s32[]{:S(2)}) async-start(), calls=%async_computation.15 | async-start | bytes 4644864 | tf_op jit(solution)/shard_map/all_gather | solution.py:158
  7.9 147.3 %all-gather.19.cloned.1.call-start = ((), (), s32[]{:S(2)}) async-start(), calls=%async_computation.17 | async-start | bytes 2985984 | tf_op jit(solution)/shard_map/all_gather | solution.py:154
  8.7 184.1 %all-gather.17.cloned.1.call-start = ((), (), s32[]{:S(2)}) async-start(), calls=%async_computation.16 | async-start | bytes 5898240 | tf_op jit(solution)/shard_map/all_gather | solution.py:176
  106.7 206.9 %reduce-scatter.22.cloned.1.call-start = ((), (), s32[]{:S(2)}) async-start(), calls=%async_computation.18 | async-start | bytes 5898240 | tf_op jit(solution)/shard_map/reduce_scatter | solution.py:189
  265.6 105.2 %all-gather.23.cloned.1.call-start = ((), (), s32[]{:S(2)}) async-start(), calls=%async_computation.20 | async-start | bytes 2985984 | tf_op jit(solution)/shard_map/all_gather | solution.py:156
  266.2 142.8 %all-gather.21.cloned.1.call-start = ((), (), s32[]{:S(2)}) async-start(), calls=%async_computation.19 | async-start | bytes 5898240 | tf_op jit(solution)/shard_map/all_gather | solution.py:198
  316.4 293.5 %copy-start.1 = (f32[512,1152]{1,0:T(8,128)}, f32[512,1152]{1,0:T(8,128)S(1)}, u32[]{:S(2)}) copy-start(f32[512,1152]{1,0:T(8,128)S(1)} %get-tuple-element.341) | copy-start | bytes 7077892
  316.5 293.5 %copy-start.69 = (f32[512]{0:T(512)}, f32[512]{0:T(512)S(1)}, u32[]{:S(2)}) copy-start(f32[512]{0:T(512)S(1)} %broadcast_multiply_fusion.2) | copy-start | bytes 6148
  319.0 291.0 %copy-start.76 = (f32[512]{0:T(512)}, f32[512]{0:T(512)S(1)}, u32[]{:S(2)}) copy-start(f32[512]{0:T(512)S(1)} %fusion.212) | copy-start | bytes 6148
  324.0 142.4 %all-gather.25.cloned.1.call-start = ((), (), s32[]{:S(2)}) async-start(), calls=%async_computation.21 | async-start | bytes 2985984 | tf_op jit(solution)/shard_map/all_gather | solution.py:157
  324.8 179.4 %all-gather.31.cloned.1.call-start = ((), (), s32[]{:S(2)}) async-start(), calls=%async_computation.27 | async-start | bytes 5898240 | tf_op jit(solution)/shard_map/all_gather | solution.py:212
  325.5 229.2 %reduce-scatter.24.cloned.1.call-start = ((), (), s32[]{:S(2)}) async-start(), calls=%async_computation.22 | async-start | bytes 5898240 | tf_op jit(solution)/shard_map/reduce_scatter | solution.py:201
  479.5 125.5 %reduce-scatter.30.cloned.1.call-start = ((), (), s32[]{:S(2)}) async-start(), calls=%async_computation.28 | async-start | bytes 5898240 | tf_op jit(solution)/shard_map/reduce_scatter | solution.py:234
  532.8 122.2 %all-gather.33.cloned.1.call-start = ((), (), s32[]{:S(2)}) async-start(), calls=%async_computation.29 | async-start | bytes 5898240 | tf_op jit(solution)/shard_map/all_gather | solution.py:247
  612.7 215.8 %copy-start.85 = (f32[512]{0:T(512)}, f32[512]{0:T(512)S(1)}, u32[]{:S(2)}) copy-start(f32[512]{0:T(512)S(1)} %negate_multiply_fusion.3) | copy-start | bytes 6148
  617.3 211.2 %reduce-scatter.32.cloned.1.call-start = ((), (), s32[]{:S(2)}) async-start(), calls=%async_computation.30 | async-start | bytes 5898240 | tf_op jit(solution)/shard_map/reduce_scatter | solution.py:281
  780.5 96.1 %all-gather.27.cloned.1.call-start = ((), (), s32[]{:S(2)}) async-start(), calls=%async_computation.23 | async-start | bytes 5898240 | tf_op jit(solution)/shard_map/all_gather | solution.py:176
  839.0 158.4 %reduce-scatter.26.cloned.1.call-start = ((), (), s32[]{:S(2)}) async-start(), calls=%async_computation.24 | async-start | bytes 5898240 | tf_op jit(solution)/shard_map/reduce_scatter | solution.py:189
  949.4 95.2 %all-gather.29.cloned.1.call-start = ((), (), s32[]{:S(2)}) async-start(), calls=%async_computation.25 | async-start | bytes 5898240 | tf_op jit(solution)/shard_map/all_gather | solution.py:198
  1001.9 208.6 %copy-start.78 = (f32[512]{0:T(512)}, f32[512]{0:T(512)S(1)}, u32[]{:S(2)}) copy-start(f32[512]{0:T(512)S(1)} %fusion.214) | copy-start | bytes 6148
  1006.9 77.2 %all-gather.35.cloned.1.call-start = ((), (), s32[]{:S(2)}) async-start(), calls=%async_computation.31 | async-start | bytes 5898240 | tf_op jit(solution)/shard_map/all_gather | solution.py:212
  1007.5 152.7 %reduce-scatter.34.cloned.1.call-start = ((), (), s32[]{:S(2)}) async-start(), calls=%async_computation.32 | async-start | bytes 5898240 | tf_op jit(solution)/shard_map/reduce_scatter | solution.py:234
  1112.2 98.3 %reduce-scatter.28.cloned.1.call-start = ((), (), s32[]{:S(2)}) async-start(), calls=%async_computation.26 | async-start | bytes 5898240 | tf_op jit(solution)/shard_map/reduce_scatter | solution.py:201
  1125.7 131.4 %all-gather.37.cloned.1.call-start = ((), (), s32[]{:S(2)}) async-start(), calls=%async_computation.33 | async-start | bytes 5898240 | tf_op jit(solution)/shard_map/all_gather | solution.py:247
  1219.4 252.1 %reduce-scatter.36.cloned.1.call-start = ((), (), s32[]{:S(2)}) async-start(), calls=%async_computation.34 | async-start | bytes 5898240 | tf_op jit(solution)/shard_map/reduce_scatter | solution.py:281
  1423.5 177.1 %reduce-scatter.48.cloned.1.call-start = ((), (), s32[]{:S(2)}) async-start(), calls=%async_computation.40 | async-start | bytes 2211840
  1512.5 93.7 %reduce-scatter.50.cloned.1.call-start = ((), (), s32[]{:S(2)}) async-start(), calls=%async_computation.41 | async-start | bytes 2211840
  1522.1 126.7 %reduce-scatter.40.cloned.1.call-start = ((), (), s32[]{:S(2)}) async-start(), calls=%async_computation.36 | async-start | bytes 2985984 | tf_op jit(solution)/shard_map/reduce_scatter | solution.py:321
  1535.5 186.8 %reduce-scatter.42.cloned.1.call-start = ((), (), s32[]{:S(2)}) async-start(), calls=%async_computation.37 | async-start | bytes 2985984 | tf_op jit(solution)/shard_map/reduce_scatter | solution.py:324
  1561.1 225.2 %reduce-scatter.38.cloned.1.call-start = ((), (), s32[]{:S(2)}) async-start(), calls=%async_computation.35 | async-start | bytes 995328 | tf_op jit(solution)/shard_map/reduce_scatter | solution.py:318
  1573.6 282.3 %reduce-scatter.46.cloned.1.call-start = ((), (), s32[]{:S(2)}) async-start(), calls=%async_computation.39 | async-start | bytes 2322432
  1600.4 346.9 %reduce-scatter.44.cloned.1.call-start = ((), (), s32[]{:S(2)}) async-start(), calls=%async_computation.38 | async-start | bytes 4644864 | tf_op jit(solution)/shard_map/reduce_scatter | solution.py:327
  (108 other events, 2566.6 us)
Sparse Core Ops, SparseCore 0:
  10.2 75.2 all-gather.14
  87.7 66.9 all-gather.18
  156.9 35.8 all-gather.16
  265.7 47.7 reduce-scatter.21
  315.8 54.9 all-gather.22
  372.9 36.0 all-gather.20
  411.4 55.0 all-gather.24
  468.1 36.0 all-gather.30
  506.9 47.8 reduce-scatter.23
  557.1 47.8 reduce-scatter.29
  617.4 37.4 all-gather.32
  780.6 47.8 reduce-scatter.31
  839.1 37.4 all-gather.26
  949.5 47.8 reduce-scatter.25
  1007.1 37.4 all-gather.28
  1046.6 37.4 all-gather.34
  1112.3 47.8 reduce-scatter.33
  1162.6 47.8 reduce-scatter.27
  1219.6 37.4 all-gather.36
  1423.6 47.8 reduce-scatter.35
  1512.6 29.3 reduce-scatter.47
  1544.8 29.3 reduce-scatter.49
  1577.8 70.9 reduce-scatter.39
  1652.7 69.4 reduce-scatter.41
  1726.2 60.0 reduce-scatter.37
  1790.3 65.5 reduce-scatter.45
  1859.3 87.9 reduce-scatter.43
where the time goes:
time: 1970 us; the launch traced here: 1960 us
  waiting for transfers between devices  1020 us (52%)
  matrix products  502 us (25%)
  local copies, waits for them, and re-layouts  183 us (9%)
  other arithmetic  134 us (7%)
  blocking collectives  103 us (5%)
    reduce_scatter x2, waiting for transfers between devices, body(): lax.psum_scatter(jnp.dot(attended, full_out, preferred_element_type=jnp.f...  95.2 us
    reduce_scatter x2, waiting for transfers between devices, body(): lax.psum_scatter(lax.dot_general(grad_pre, full_fc1, (((1,), (1,)), ((),...  84.7 us
    all_gather x2, waiting for transfers between devices, body(): mlp_full = lax.all_gather(mlp_in, 'tp', axis=0, tiled=True)  75.1 us
    all_gather x2, waiting for transfers between devices, body(): grad_one_full = lax.all_gather(grad_branch_one, 'tp', axis=0, tiled=True)  75.1 us
    all_gather x2, waiting for transfers between devices, body(): attn_full = lax.all_gather(attn_in, 'tp', axis=0, tiled=True)  74.9 us
    dot_general x32, matrix products, masked_scores(): lax.dot_general(query_rows, key_rows, (((1,), (1,)), ((), ())), preferred...  72.8 us
    unnamed x30, waiting for transfers between devices  72.2 us
    reduce_scatter x1, waiting for transfers between devices, body(): lax.psum_scatter(grad_fc2.astype(jnp.bfloat16), 'dp', scatter_dimension=1...  71.6 us
  transfers between devices with their start and end apart: 27, of which 24 were waited for; matrix products, arithmetic and copies ran while one was open for 13% of the time, Pallas kernels for 0%

commit v1 on v0

--- a/solution.py
+++ b/solution.py
@@ -3,6 +3,8 @@
 import jax
 import jax.numpy as jnp
 from jax import lax
+from jax.experimental import pallas as pl
+from jax.experimental.pallas import tpu as pltpu
 from jax.sharding import PartitionSpec as P
 
 HD = 72
@@ -100,7 +102,7 @@
     )
 
 
-def body(
+def general_body(
     block_input,
     segment_ids,
     conditioning,
@@ -356,6 +358,767 @@
     )
 
 
+f32, bf16 = jnp.float32, jnp.bfloat16
+AXES = ("dp", "tp")
+CORE, CHIP = 1, 2
+ROWS = 144
+QT = 256
+ET = 128
+LOG2E = 1.4426950408889634
+GELU_A = 0.7978845608028654
+GELU_B = 0.7978845608028654 * 0.044715
+VMEM_BYTES = 56 * 2**20
+NN = (((1,), (0,)), ((), ()))
+NT = (((1,), (1,)), ((), ()))
+SMEM_SPEC = pl.BlockSpec(memory_space=pltpu.SMEM)
+VMEM_SPEC = pl.BlockSpec(memory_space=pltpu.VMEM)
+ANY_SPEC = pl.BlockSpec(memory_space=pl.ANY)
+
+
+def dot(left, right, dims=NN):
+    return lax.dot_general(left, right, dims, preferred_element_type=f32)
+
+
+def compiler_params():
+    return pltpu.CompilerParams(vmem_limit_bytes=VMEM_BYTES)
+
+
+def swap(values, dp_mask, tp_mask):
+    pairs = [(d * 4 + t, (d ^ dp_mask) * 4 + (t ^ tp_mask)) for d in range(8) for t in range(4)]
+    return lax.ppermute(values, AXES, pairs)
+
+
+def across(values, tp_mask):
+    return swap(values, 0, tp_mask)
+
+
+def tie(values, after):
+    count = len(values)
+    return pl.pallas_call(
+        lambda *refs: None,
+        in_specs=[ANY_SPEC] * (count + len(after)),
+        out_specs=[ANY_SPEC] * count,
+        out_shape=[jax.ShapeDtypeStruct(v.shape, v.dtype) for v in values],
+        input_output_aliases={i: i for i in range(count)},
+    )(*values, *after)
+
+
+def fetch(whole_ref, block, column, out_ref, sem):
+    width = out_ref.shape[1]
+    return [
+        pltpu.make_async_copy(
+            whole_ref.at[d * 4 + block, :, pl.ds(column, width)],
+            out_ref.at[pl.ds(d * ROWS, ROWS), :],
+            sem.at[d],
+        )
+        for d in range(8)
+    ]
+
+
+def send_pieces(stage, place_ref, first, count, outs, sem):
+    for q in range(count):
+        source = stage.at[pl.ds(q * ROWS, ROWS), :]
+        spot = place_ref[first + q]
+
+        @pl.when(spot < 4)
+        def _():
+            pltpu.make_async_copy(source, outs[0].at[spot], sem.at[q]).start()
+
+        @pl.when(spot >= 4)
+        def _():
+            pltpu.make_async_copy(source, outs[1].at[spot - 4], sem.at[q]).start()
+
+
+def wait_pieces(stage, count, outs, sem):
+    for q in range(count):
+        pltpu.make_async_copy(stage.at[pl.ds(q * ROWS, ROWS), :], outs[0].at[0], sem.at[q]).wait()
+
+
+def mlp_body(added, waits, tok_steps, *refs):
+    block_ref, x_ref, g_ref, xt_ref, gt_ref, whole_ref, b_ref = refs[:7]
+    init_ref = refs[7] if added else None
+    b2_ref, dm_ref, db_ref, dw_ref, w1_ref, w2_ref, act_s, slope_s, sem = refs[7 + added + waits :]
+    step = pl.program_id(0)
+    rows = x_ref.shape[0]
+    ff = w1_ref.shape[1]
+
+    @pl.when(step == 0)
+    def _():
+        copies = fetch(whole_ref, block_ref[0], 0, w1_ref, sem.at[0])
+        copies += fetch(whole_ref, block_ref[0], ff, w2_ref, sem.at[1])
+        for copy in copies:
+            copy.start()
+        for copy in copies:
+            copy.wait()
+
+    @pl.when(step < tok_steps)
+    def _():
+        pre = dot(x_ref[...], w1_ref[...]) + b_ref[...]
+        act_grad = dot(g_ref[...], w2_ref[...])
+        square = pre * pre
+        bend = jnp.tanh(pre * (GELU_A + GELU_B * square))
+        half = 0.5 + 0.5 * bend
+        act = (pre * half).astype(bf16)
+        slope = half + pre * (half * (1.0 - bend)) * (GELU_A + (3 * GELU_B) * square)
+        pre_grad = (act_grad * slope).astype(bf16)
+        b2_ref[...] = dot(act, w2_ref[...], NT).astype(bf16)
+        dm_ref[...] = dot(pre_grad, w1_ref[...], NT).astype(bf16)
+        here = pl.ds(pl.multiple_of(step * rows, rows), rows)
+        act_s[here, :] = act
+        slope_s[here, :] = pre_grad
+        sums = jnp.sum(pre_grad.astype(f32), axis=0, keepdims=True)
+
+        @pl.when(step == 0)
+        def _():
+            db_ref[...] = sums
+
+        @pl.when(step > 0)
+        def _():
+            db_ref[...] += sums
+
+    @pl.when(step >= tok_steps)
+    def _():
+        grad1 = dot(xt_ref[...], slope_s[...])
+        grad2 = dot(gt_ref[...], act_s[...])
+        if added:
+            grad1 += init_ref[:, :ff].astype(f32)
+            grad2 += init_ref[:, ff:].astype(f32)
+        dw_ref[:, :ff] = grad1.astype(bf16)
+        dw_ref[:, ff:] = grad2.astype(bf16)
+
+
+def mlp_block(x, g, xt, gt, whole, block, bias, init=None, waits=(), tok_steps=4, row_steps=4):
+    n, d = x.shape
+    ff = whole.shape[2] // 2
+    added = init is not None
+    tok_rows, dim_rows = n // tok_steps, d // row_steps
+
+    def tok(s):
+        return (jnp.minimum(s, tok_steps - 1), 0)
+
+    def row(s):
+        return (jnp.maximum(s - tok_steps, 0), 0)
+
+    in_specs = [
+        SMEM_SPEC,
+        pl.BlockSpec((tok_rows, d), tok),
+        pl.BlockSpec((tok_rows, d), tok),
+        pl.BlockSpec((dim_rows, n), row),
+        pl.BlockSpec((dim_rows, n), row),
+        ANY_SPEC,
+        pl.BlockSpec((1, ff), lambda s: (0, 0)),
+    ]
+    operands = [block, x, g, xt, gt, whole, bias]
+    if added:
+        in_specs.append(pl.BlockSpec((dim_rows, 2 * ff), row))
+        operands.append(init)
+    return pl.pallas_call(
+        lambda *refs: mlp_body(added, len(waits), tok_steps, *refs),
+        grid=(tok_steps + row_steps,),
+        in_specs=in_specs + [ANY_SPEC] * len(waits),
+        out_specs=[
+            pl.BlockSpec((tok_rows, d), tok),
+            pl.BlockSpec((tok_rows, d), tok),
+            pl.BlockSpec((1, ff), lambda s: (0, 0)),
+            pl.BlockSpec((dim_rows, 2 * ff), row),
+        ],
+        out_shape=[
+            jax.ShapeDtypeStruct((n, d), bf16),
+            jax.ShapeDtypeStruct((n, d), bf16),
+            jax.ShapeDtypeStruct((1, ff), f32),
+            jax.ShapeDtypeStruct((d, 2 * ff), bf16),
+        ],
+        scratch_shapes=[
+            pltpu.VMEM((d, ff), bf16),
+            pltpu.VMEM((d, ff), bf16),
+            pltpu.VMEM((n, ff), bf16),
+            pltpu.VMEM((n, ff), bf16),
+            pltpu.SemaphoreType.DMA((2, 8)),
+        ],
+        compiler_params=compiler_params(),
+        cost_estimate=pl.CostEstimate(
+            flops=12 * n * d * ff, bytes_accessed=30 << 20, transcendentals=n * ff
+        ),
+    )(*operands, *waits)
+
+
+def attend_fwd_body(
+    heads, lo_ref, hi_ref, block_ref, x_ref, whole_ref, b_ref, sc_ref, sr_ref, *refs
+):
+    qkv_ref, att_ref, lse_ref, part_ref, w_ref, qt_s, k_s, vt_s, ot_s, m_s, l_s, acc_s, sem = refs[-13:]
+    copies = fetch(whole_ref, block_ref[0], 0, w_ref, sem)
+    for copy in copies:
+        copy.start()
+    for copy in copies:
+        copy.wait()
+    n = x_ref.shape[0]
+    e = heads * HD
+    c = LOG2E / math.sqrt(HD)
+    qkv = dot(x_ref[...], w_ref[:, : 3 * e]) + b_ref[...]
+    qkv_ref[...] = qkv.astype(bf16)
+    qt = qkv[:, :e].T
+    vt = qkv[:, 2 * e :].T
+    for h in range(heads):
+        qt_s[h] = qt[h * HD : (h + 1) * HD].astype(bf16)
+        vt_s[h] = vt[h * HD : (h + 1) * HD].astype(bf16)
+        k_s[h] = qkv[:, e + h * HD : e + (h + 1) * HD].astype(bf16)
+
+    @pl.loop(0, n // QT)
+    def _(i):
+        qi = pl.ds(pl.multiple_of(i * QT, QT), QT)
+        m_s[...] = jnp.full(m_s.shape, masked_score, f32)
+        l_s[...] = jnp.zeros(l_s.shape, f32)
+        acc_s[...] = jnp.zeros(acc_s.shape, f32)
+        seg_row = sr_ref[:1, qi]
+
+        @pl.loop(lo_ref[i], hi_ref[i])
+        def _(j):
+            kj = pl.ds(pl.multiple_of(j * QT, QT), QT)
+            same = sc_ref[kj, :1] == seg_row
+            for h in range(heads):
+                scores = jnp.where(same, dot(k_s[h, kj, :], qt_s[h, :, qi]), masked_score)
+                old = m_s[h]
+                top = jnp.maximum(old, jnp.max(scores, axis=0, keepdims=True))
+                fade = jnp.exp2((old - top) * c)
+                p = jnp.exp2((scores - top) * c)
+                l_s[h] = l_s[h] * fade + jnp.sum(p, axis=0, keepdims=True)
+                acc_s[h] = acc_s[h] * fade + dot(vt_s[h, :, kj], p.astype(bf16))
+                m_s[h] = top
+
+        for h in range(heads):
+            total = l_s[h]
+            ot_s[h * HD : (h + 1) * HD, qi] = acc_s[h] / total
+            lse_ref[h : h + 1, qi] = m_s[h] * c + jnp.log(total) * LOG2E
+
+    att = ot_s[...].T.astype(bf16)
+    att_ref[...] = att
+    part_ref[...] = dot(att, w_ref[:, 3 * e :], NT).astype(bf16)
+
+
+def attend_fwd(x, whole, block, bias, lo, hi, seg_col, seg_row, waits=()):
+    n, d = x.shape
+    e = whole.shape[2] // 4
+    heads = e // HD
+    return pl.pallas_call(
+        lambda *refs: attend_fwd_body(heads, *refs),
+        in_specs=[SMEM_SPEC] * 3
+        + [VMEM_SPEC, ANY_SPEC]
+        + [VMEM_SPEC] * 3
+        + [ANY_SPEC] * len(waits),
+        out_specs=[VMEM_SPEC] * 4,
+        out_shape=[
+            jax.ShapeDtypeStruct((n, 3 * e), bf16),
+            jax.ShapeDtypeStruct((n, e), bf16),
+            jax.ShapeDtypeStruct((8, n), f32),
+            jax.ShapeDtypeStruct((n, d), bf16),
+        ],
+        scratch_shapes=[
+            pltpu.VMEM((d, 4 * e), bf16),
+            pltpu.VMEM((heads, HD, n), bf16),
+            pltpu.VMEM((heads, n, HD), bf16),
+            pltpu.VMEM((heads, HD, n), bf16),
+            pltpu.VMEM((e, n), f32),
+            pltpu.VMEM((heads, 1, QT), f32),
+            pltpu.VMEM((heads, 1, QT), f32),
+            pltpu.VMEM((heads, HD, QT), f32),
+            pltpu.SemaphoreType.DMA((8,)),
+        ],
+        compiler_params=compiler_params(),
+        cost_estimate=pl.CostEstimate(
+            flops=8 * n * d * e * 3, bytes_accessed=12 << 20, transcendentals=heads * n * n
+        ),
+    )(lo, hi, block, x, whole, bias, seg_col, seg_row, *waits)
+
+
+def attend_bwd_body(final, waits, heads, *refs):
+    (lo_ref, hi_ref, block_ref, place_ref, qkv_ref, att_ref, g_ref, gt_ref, xt_ref, whole_ref, lse_ref, sc_ref, sr_ref) = refs[:13]
+    init_ref = refs[13] if final else None
+    refs = refs[13 + final + waits :]
+    if final:
+        dx_ref, db_ref = refs[:2]
+        outs, (stage, sem) = refs[2:4], refs[-2:]
+        refs = refs[4:-2]
+    else:
+        dx_ref, db_ref, stage = refs[:3]
+        refs = refs[3:]
+    qt_s, q_s, k_s, kt_s, v_s, do_s, dot_s, delta_s, dqt_s, dk_s, dv_s, w_ref, w_sem = refs
+    copies = fetch(whole_ref, block_ref[0], 0, w_ref, w_sem)
+    for copy in copies:
+        copy.start()
+    for copy in copies:
+        copy.wait()
+    n = g_ref.shape[0]
+    e = heads * HD
+    c = LOG2E / math.sqrt(HD)
+    scale = 1.0 / math.sqrt(HD)
+    out_grad = dot(g_ref[...], w_ref[:, 3 * e :]).astype(bf16).astype(f32)
+    out_grad_t = out_grad.T
+    qkv = qkv_ref[...].astype(f32)
+    qt = qkv[:, :e].T
+    kt = qkv[:, e : 2 * e].T
+    att = att_ref[...]
+    products = out_grad_t * att.astype(f32).T
+    for h in range(heads):
+        s = slice(h * HD, (h + 1) * HD)
+        qt_s[h] = qt[s].astype(bf16)
+        kt_s[h] = kt[s].astype(bf16)
+        dot_s[h] = out_grad_t[s].astype(bf16)
+        delta_s[h] = jnp.sum(products[s], axis=0, keepdims=True)
+        q_s[h] = qkv[:, h * HD : (h + 1) * HD].astype(bf16)
+        k_s[h] = qkv[:, e + h * HD : e + (h + 1) * HD].astype(bf16)
+        v_s[h] = qkv[:, 2 * e + h * HD : 2 * e + (h + 1) * HD].astype(bf16)
+        do_s[h] = out_grad[:, s].astype(bf16)
+    dqt_s[...] = jnp.zeros(dqt_s.shape, f32)
+    dk_s[...] = jnp.zeros(dk_s.shape, f32)
+    dv_s[...] = jnp.zeros(dv_s.shape, f32)
+
+    @pl.loop(0, n // QT)
+    def _(j):
+        kj = pl.ds(pl.multiple_of(j * QT, QT), QT)
+        seg_col = sc_ref[kj, :1]
+
+        @pl.loop(lo_ref[j], hi_ref[j])
+        def _(i):
+            qi = pl.ds(pl.multiple_of(i * QT, QT), QT)
+            same = seg_col == sr_ref[:1, qi]
+            for h in range(heads):
+                scores = dot(k_s[h, kj, :], qt_s[h, :, qi])
+                p = jnp.where(same, jnp.exp2(scores * c - lse_ref[h : h + 1, qi]), 0.0)
+                p_grad = dot(v_s[h, kj, :], dot_s[h, :, qi])
+                s_grad = (p * (p_grad - delta_s[h, :, qi])).astype(bf16)
+                dv_s[h, kj, :] += dot(p.astype(bf16), do_s[h, qi, :])
+                dk_s[h, kj, :] += dot(s_grad, q_s[h, qi, :])
+                dqt_s[h, :, qi] += dot(kt_s[h, :, kj], s_grad)
+
+    dq = jnp.concatenate([dqt_s[h] for h in range(heads)], axis=0).T * scale
+    dk = [dk_s[h] * scale for h in range(heads)]
+    dv = [dv_s[h] for h in range(heads)]
+    grads = jnp.concatenate([dq] + dk + dv, axis=1).astype(bf16)
+    db_ref[...] = jnp.sum(grads.astype(f32), axis=0, keepdims=True)
+    dx_ref[...] = dot(grads, w_ref[:, : 3 * e], NT).astype(bf16)
+    dw = jnp.concatenate([dot(xt_ref[...], grads), dot(gt_ref[...], att)], axis=1)
+    if not final:
+        stage[...] = dw.astype(bf16)
+    else:
+        stage[...] = (dw + init_ref[...].astype(f32)).astype(bf16)
+        send_pieces(stage, place_ref, 0, 8, outs, sem)
+        wait_pieces(stage, 8, outs, sem)
+
+
+def attend_bwd(
+    qkv, att, g, gt, xt, whole, block, lse, lo, hi, seg_col, seg_row, place, init=None, waits=()
+):
+    n, d = g.shape
+    e = whole.shape[2] // 4
+    heads = e // HD
+    final = init is not None
+    operands = [lo, hi, block, place, qkv, att, g, gt, xt, whole, lse, seg_col, seg_row]
+    in_specs = [SMEM_SPEC] * 4 + [VMEM_SPEC] * 5 + [ANY_SPEC] + [VMEM_SPEC] * 3
+    out_shape = [jax.ShapeDtypeStruct((n, d), bf16), jax.ShapeDtypeStruct((1, 3 * e), f32)]
+    out_specs = [VMEM_SPEC, VMEM_SPEC]
+    tall, wide = (heads, n, HD), (heads, HD, n)
+    scratch = [pltpu.VMEM(s, bf16) for s in (wide, tall, tall, wide, tall, tall, wide)]
+    scratch += [pltpu.VMEM((heads, 1, n), f32)] + [pltpu.VMEM(s, f32) for s in (wide, tall, tall)]
+    scratch += [pltpu.VMEM((d, 4 * e), bf16), pltpu.SemaphoreType.DMA((8,))]
+    if final:
+        operands.append(init)
+        in_specs.append(VMEM_SPEC)
+        out_shape += [jax.ShapeDtypeStruct((4, ROWS, 4 * e), bf16)] * 2
+        out_specs += [ANY_SPEC] * 2
+        scratch += [pltpu.VMEM((d, 4 * e), bf16), pltpu.SemaphoreType.DMA((8,))]
+    else:
+        out_shape.append(jax.ShapeDtypeStruct((d, 4 * e), bf16))
+        out_specs.append(VMEM_SPEC)
+    in_specs += [ANY_SPEC] * len(waits)
+    operands += waits
+    return pl.pallas_call(
+        lambda *refs: attend_bwd_body(final, len(waits), heads, *refs),
+        in_specs=in_specs,
+        out_specs=out_specs,
+        out_shape=out_shape,
+        scratch_shapes=scratch,
+        compiler_params=compiler_params(),
+        cost_estimate=pl.CostEstimate(
+            flops=16 * n * d * e * 3, bytes_accessed=20 << 20, transcendentals=heads * n * n
+        ),
+    )(*operands)
+
+
+def token_rows(mod_ref, block, sc_ref):
+    d = mod_ref.shape[1] // 6
+    seg = sc_ref[:, :1]
+    rows = mod_ref[:, block * d : (block + 1) * d]
+    value = jnp.where(seg == 0, rows[0:1], rows[1:2])
+    value = jnp.where(seg == 2, rows[2:3], value)
+    return jnp.where(seg == 3, rows[3:4], value)
+
+
+def normalize(values):
+    centred = values - jnp.mean(values, axis=-1, keepdims=True)
+    inverse = lax.rsqrt(jnp.mean(centred * centred, axis=-1, keepdims=True) + epsilon)
+    return centred * inverse, inverse
+
+
+def norm_back(normed, inverse, grad):
+    mean = jnp.mean(grad, axis=-1, keepdims=True)
+    along = jnp.mean(grad * normed, axis=-1, keepdims=True)
+    return inverse * (grad - mean - normed * along)
+
+
+def add_images(acc_ref, first_ref, last_ref, sc_ref, columns):
+    step = pl.program_id(0)
+    seg = sc_ref[:, :1]
+
+    @pl.when(step == 0)
+    def _():
+        acc_ref[...] = jnp.zeros(acc_ref.shape, f32)
+
+    @pl.loop(first_ref[step], last_ref[step] + 1)
+    def _(image):
+        mine = seg == image
+        for i, values in enumerate(columns):
+            d = values.shape[1]
+            part = jnp.sum(jnp.where(mine, values, 0.0), axis=0, keepdims=True)
+            acc_ref[pl.ds(image, 1), i * d : (i + 1) * d] += part
+
+
+def add_rows(acc_ref, values):
+    part = jnp.sum(values, axis=0, keepdims=True)
+
+    @pl.when(pl.program_id(0) == 0)
+    def _():
+        acc_ref[...] = part
+
+    @pl.when(pl.program_id(0) > 0)
+    def _():
+        acc_ref[...] += part
+
+
+def enter_body(x_ref, g_ref, mod_ref, sc_ref, a_ref, at_ref, bg_ref, bgt_ref, sum_ref):
+    normed, _ = normalize(x_ref[...].astype(f32))
+    a = normed * (1.0 + token_rows(mod_ref, 1, sc_ref)) + token_rows(mod_ref, 0, sc_ref)
+    a_ref[...] = a.astype(bf16)
+    at_ref[...] = a.T.astype(bf16)
+    bg = token_rows(mod_ref, 5, sc_ref) * g_ref[...].astype(f32)
+    bg_ref[...] = bg.astype(bf16)
+    bgt_ref[...] = bg.T.astype(bf16)
+    add_rows(sum_ref, bg)
+
+
+def middle_body(x_ref, p0, p1, p2, p3, mod_ref, sc_ref, ob_ref, hid_ref, br_ref, m_ref, mt_ref):
+    branch = p0[...].astype(f32) + p1[...].astype(f32) + p2[...].astype(f32) + p3[...].astype(f32)
+    branch = branch + ob_ref[...]
+    br_ref[...] = branch
+    hidden = x_ref[...].astype(f32) + token_rows(mod_ref, 2, sc_ref) * branch
+    hid_ref[...] = hidden
+    normed, _ = normalize(hidden)
+    m = normed * (1.0 + token_rows(mod_ref, 4, sc_ref)) + token_rows(mod_ref, 3, sc_ref)
+    m_ref[...] = m.astype(bf16)
+    mt_ref[...] = m.T.astype(bf16)
+
+
+def turn_body(
+    first_ref, last_ref, hid_ref, br_ref, g_ref, b0, b1, b2, b3, d0, d1, d2, d3, mod_ref, sc_ref, fb_ref,
+    out_ref, hg_ref, bg_ref, bgt_ref, sum_ref, img_ref,
+):
+    hidden, g = hid_ref[...], g_ref[...].astype(f32)
+    branch = b0[...].astype(f32) + b1[...].astype(f32) + b2[...].astype(f32) + b3[...].astype(f32)
+    branch = branch + fb_ref[...]
+    out_ref[...] = (hidden + token_rows(mod_ref, 5, sc_ref) * branch).astype(bf16)
+    m_grad = d0[...].astype(f32) + d1[...].astype(f32) + d2[...].astype(f32) + d3[...].astype(f32)
+    normed, inverse = normalize(hidden)
+    hidden_grad = g + norm_back(normed, inverse, m_grad * (1.0 + token_rows(mod_ref, 4, sc_ref)))
+    hg_ref[...] = hidden_grad
+    bg = token_rows(mod_ref, 2, sc_ref) * hidden_grad
+    bg_ref[...] = bg.astype(bf16)
+    bgt_ref[...] = bg.T.astype(bf16)
+    add_rows(sum_ref, bg)
+    add_images(
+        img_ref, first_ref, last_ref, sc_ref,
+        (hidden_grad * br_ref[...], m_grad, m_grad * normed, g * branch),
+    )
+
+
+def leave_body(first_ref, last_ref, x_ref, hg_ref, d0, d1, d2, d3, mod_ref, sc_ref, out_ref, img_ref):
+    a_grad = d0[...].astype(f32) + d1[...].astype(f32) + d2[...].astype(f32) + d3[...].astype(f32)
+    normed, inverse = normalize(x_ref[...].astype(f32))
+    back = norm_back(normed, inverse, a_grad * (1.0 + token_rows(mod_ref, 1, sc_ref)))
+    out_ref[...] = (hg_ref[...] + back).astype(bf16)
+    add_images(img_ref, first_ref, last_ref, sc_ref, (a_grad, a_grad * normed))
+
+
+def by_rows(body_fn, scalars, operands, outs, waits=(), carried=()):
+    def spec(kind, shape):
+        if kind == "t":
+            return pl.BlockSpec((ET, shape[1]), lambda s: (s, 0))
+        if kind == "T":
+            return pl.BlockSpec((shape[0], ET), lambda s: (0, s))
+        return pl.BlockSpec(shape, lambda s: (0, 0))
+
+    n = operands[0][1].shape[0]
+    own_in, own_out = len(scalars) + len(operands), len(outs)
+    idle = len(waits) + len(carried)
+
+    def body(*refs):
+        body_fn(*refs[:own_in], *refs[own_in + idle : own_in + idle + own_out])
+
+    return pl.pallas_call(
+        body,
+        grid=(n // ET,),
+        in_specs=[SMEM_SPEC] * len(scalars)
+        + [spec(k, v.shape) for k, v in operands]
+        + [ANY_SPEC] * idle,
+        out_specs=[spec(k, s) for k, s, _ in outs] + [ANY_SPEC] * len(carried),
+        out_shape=[jax.ShapeDtypeStruct(s, t) for _, s, t in outs]
+        + [jax.ShapeDtypeStruct(v.shape, v.dtype) for v in carried],
+        input_output_aliases={
+            own_in + len(waits) + i: own_out + i for i in range(len(carried))
+        },
+        compiler_params=compiler_params(),
+        cost_estimate=pl.CostEstimate(
+            flops=100 * n * 1152, bytes_accessed=24 << 20, transcendentals=n
+        ),
+    )(*scalars, *[v for _, v in operands], *waits, *carried)
+
+
+def trade_rows(values, core):
+    own = lax.dynamic_index_in_dim(values, core, 0, keepdims=False)
+    got = across(lax.dynamic_index_in_dim(values, 1 - core, 0, keepdims=False), CORE)
+    first = core == 0
+    return jnp.concatenate([jnp.where(first, own, got), jnp.where(first, got, own)])
+
+
+def trade_back(row, core):
+    half = row.shape[0] // 2
+    own = lax.dynamic_slice_in_dim(row, core * half, half, 0)
+    got = across(lax.dynamic_slice_in_dim(row, (1 - core) * half, half, 0), CORE)
+    first = core == 0
+    return jnp.stack([jnp.where(first, own, got), jnp.where(first, got, own)])
+
+
+def add_pieces(*terms):
+    return sum(t.astype(f32) for t in terms)
+
+
+class Scatter:
+    def __init__(self, low, high):
+        self.low, self.got = low, swap(high, 1, 0)
+
+    def turn(self):
+        sums = [add_pieces(self.low[i], self.got[i]) for i in range(4)]
+        self.low = sums[0]
+        self.got = [swap(sums[i].astype(bf16), 2 * i, 0) for i in range(1, 4)]
+
+    def total(self):
+        return add_pieces(self.low, *self.got)
+
+
+def gather_all(values, dp_rank, tp_rank):
+    order = dp_rank * 4 + tp_rank + jnp.zeros((1,), jnp.int32)
+    for dp_mask, tp_mask in ((1, 0), (2, 0), (6, 0), (0, CHIP), (0, CORE)):
+        values = jnp.concatenate([values, swap(values, dp_mask, tp_mask)])
+        order = jnp.concatenate([order, order ^ (dp_mask * 4 + tp_mask)])
+    return values, order
+
+
+def row_body(
+    block_input,
+    segment_ids,
+    conditioning,
+    w_qkv,
+    qv_bias,
+    w_out,
+    out_bias,
+    w_fc1,
+    fc1_bias,
+    w_fc2,
+    fc2_bias,
+    w_ada,
+    ada_bias,
+    cotangent,
+):
+    dp_rank, tp_rank = lax.axis_index("dp"), lax.axis_index("tp")
+    core, chip = tp_rank & 1, tp_rank >> 1
+    d = block_input.shape[2]
+    e, ff, mod_dev = w_qkv.shape[2], w_fc1.shape[1], w_ada.shape[1]
+    flips = jnp.arange(8, dtype=jnp.int32) ^ dp_rank
+    place = (flips & 1) * 4 + (flips >> 1)
+    blocks = [(tp_rank ^ k).reshape(1) for k in range(4)]
+    att_shard = jnp.concatenate([w_qkv[0], w_qkv[1], w_qkv[2], w_out.T], axis=1)
+    mlp_shard = jnp.concatenate([w_fc1, w_fc2.T], axis=1)
+    att_w = lax.all_gather(att_shard, AXES)
+    mlp_w = lax.all_gather(mlp_shard, AXES)
+    x = trade_rows(block_input, core)
+    g = trade_rows(cotangent, core)
+    seg = lax.dynamic_slice(segment_ids, (core, chip * PACK), (1, PACK))[0]
+    seg_col = jnp.broadcast_to(seg[:, None], (PACK, 128))
+    seg_row = jnp.broadcast_to(seg[None, :], (8, PACK))
+    tiles = seg.reshape(-1, QT)
+    lo = jnp.sum((tiles[None, :, -1] < tiles[:, None, 0]).astype(jnp.int32), axis=1)
+    hi = jnp.sum((tiles[None, :, 0] <= tiles[:, None, -1]).astype(jnp.int32), axis=1)
+    small = seg.reshape(-1, ET)
+    first, last = small[:, 0], small[:, -1]
+    lifted = smooth_gate(conditioning.astype(f32)).astype(bf16).reshape(-1, 8, w_ada.shape[0])
+    lifted = lax.all_to_all(lifted.transpose(1, 0, 2), "dp", 0, 0)
+    lifted = lifted.reshape(8, 2, 2, IMG_ROW, -1).transpose(0, 2, 1, 3, 4).reshape(32 * IMG_ROW, -1)
+    mod_part = dot(lifted, w_ada).reshape(32, IMG_ROW, mod_dev)
+    mod_part = lax.all_to_all(mod_part, AXES, 0, 0).reshape(8, 4, IMG_ROW, mod_dev)
+    modulation = jnp.sum(mod_part, axis=0).transpose(1, 0, 2).reshape(IMG_ROW, -1)
+    modulation = modulation + ada_bias.astype(f32)
+    row_f, row_b = ((PACK, d), f32), ((PACK, d), bf16)
+    turned = ((d, PACK), bf16)
+    a, a_t, bg2, bg2_t, fc2_sum = by_rows(
+        enter_body,
+        (),
+        [("t", x), ("t", g), ("w", modulation), ("t", seg_col)],
+        [("t", *row_b), ("T", *turned), ("t", *row_b), ("T", *turned), ("w", (1, d), f32)],
+    )
+    qkv_bias = jnp.stack([qv_bias[0], jnp.zeros_like(qv_bias[0]), qv_bias[1]]).astype(f32)
+    kept = {}
+
+    def forward(k, waits):
+        bias = lax.dynamic_slice_in_dim(qkv_bias, (tp_rank ^ k) * e, e, 1).reshape(1, 3 * e)
+        kept[k] = attend_fwd(a, att_w, blocks[k], bias, lo, hi, seg_col, seg_row, waits)
+        return (kept[k][2],)
+
+    after = ()
+    for k in range(4):
+        after = forward(k, after)
+    hidden, branch1, m, m_t = by_rows(
+        middle_body,
+        (),
+        [("t", x)]
+        + [("t", kept[k][3]) for k in range(4)]
+        + [("w", modulation), ("t", seg_col), ("w", out_bias.astype(f32)[None])],
+        [("t", *row_f), ("t", *row_f), ("t", *row_b), ("T", *turned)],
+    )
+    done = {}
+    fc1_f = fc1_bias.astype(f32)[None]
+
+    def feed_forward(k, init, waits):
+        bias = lax.dynamic_slice_in_dim(fc1_f, (tp_rank ^ k) * ff, ff, 1)
+        done[k] = mlp_block(m, bg2, m_t, bg2_t, mlp_w, blocks[k], bias, init, waits)
+        return (done[k][2],)
+
+    after = feed_forward(1, None, ())
+    init = across(done[1][3], CORE)
+    after = feed_forward(3, None, after)
+    after = feed_forward(0, init, after)
+    init = across(done[3][3], CORE)
+    mlp_sum = {0: lax.psum_scatter(done[0][3], "dp", scatter_dimension=0, tiled=True)}
+    after = feed_forward(2, init, after)
+    mlp_sum[2] = lax.psum_scatter(done[2][3], "dp", scatter_dimension=0, tiled=True)
+    block_output, hidden_grad, bg1, bg1_t, out_sum, img_late = by_rows(
+        turn_body,
+        (first, last),
+        [("t", hidden), ("t", branch1), ("t", g)]
+        + [("t", done[k][0]) for k in range(4)]
+        + [("t", done[k][1]) for k in range(4)]
+        + [("w", modulation), ("t", seg_col), ("w", fc2_bias.astype(f32)[None])],
+        [("t", *row_b), ("t", *row_f), ("t", *row_b), ("T", *turned), ("w", (1, d), f32), ("w", (IMG_ROW, 4 * d), f32)],
+        waits=after,
+    )
+    fc1_sum = jnp.zeros((1, 4 * ff), f32)
+    for k in range(4):
+        fc1_sum = lax.dynamic_update_slice_in_dim(fc1_sum, done[k][2], (tp_rank ^ k) * ff, 1)
+    late = jnp.concatenate([jnp.zeros((IMG_ROW, 2 * d), f32), img_late], axis=1)
+    late = late.reshape(IMG_ROW, 4, mod_dev).transpose(1, 0, 2).reshape(4, IMG_ROW * mod_dev)
+    sums = jnp.concatenate([jnp.sum(img_late, axis=0, keepdims=True), fc1_sum, fc2_sum, out_sum], axis=1)
+    late = jnp.concatenate([late, jnp.broadcast_to(sums, (4, sums.shape[1]))], axis=1)
+    late = lax.all_to_all(jnp.concatenate([late] * 8), AXES, 0, 0, tiled=True)
+    back = {}
+
+    def backward(k, init, waits):
+        qkv, att, lse, _ = kept[k]
+        back[k] = attend_bwd(
+            qkv, att, bg1, bg1_t, a_t, att_w, blocks[k], lse, lo, hi, seg_col, seg_row, place, init, waits
+        )
+        return (back[k][1],)
+
+    block_output = trade_back(block_output, core)
+    after = backward(1, None, ())
+    init = across(back[1][2], CORE)
+    (block_output,) = tie([block_output], after)
+    after = backward(3, None, after + (block_output,))
+    (late,) = tie([late], after)
+    after = backward(0, init, after + (late,))
+    init = across(back[3][2], CORE)
+    near = Scatter(*back[0][2:])
+    after = backward(2, init, after + (mlp_sum[0],))
+    (near.got,) = tie([near.got], after)
+    near.turn()
+    far = Scatter(*back[2][2:])
+    input_grad, img_early = by_rows(
+        leave_body,
+        (first, last),
+        [("t", x), ("t", hidden_grad)]
+        + [("t", back[k][0]) for k in range(4)]
+        + [("w", modulation), ("t", seg_col)],
+        [("t", *row_b), ("w", (IMG_ROW, 2 * d), f32)],
+        waits=(near.low,),
+    )
+    mlp_total = mlp_sum[0].astype(f32) + across(mlp_sum[2], CHIP).astype(f32)
+    far.got, *near.got = tie([far.got] + near.got, (img_early,))
+    far.turn()
+    att_total = near.total() + across(far.total().astype(bf16), CHIP).astype(f32)
+    qv_sum = jnp.zeros((2, 4 * e), f32)
+    for k in range(4):
+        grads = back[k][1].reshape(3, e)
+        qv_sum = lax.dynamic_update_slice_in_dim(
+            qv_sum, jnp.stack([grads[0], grads[2]]), (tp_rank ^ k) * e, 1
+        )
+    all_b = jnp.concatenate([img_early.reshape(1, -1), qv_sum.reshape(1, -1)], axis=1)
+    all_b, order = gather_all(all_b, dp_rank, tp_rank)
+    early = 2 * d * IMG_ROW
+    own = IMG_ROW * mod_dev
+    late_bias, fc1_total, fc2_total, out_total = jnp.split(
+        jnp.sum(late[:, own:], axis=0), [4 * d, 4 * d + 4 * ff, 5 * d + 4 * ff]
+    )
+    qv_total = jnp.sum(all_b[:, early:], axis=0).reshape(2, -1)
+    all_b = all_b[:, :early].reshape(32 * IMG_ROW, 2 * d)
+    ada_total = jnp.concatenate([jnp.sum(all_b, axis=0), late_bias])
+    grad_b = lax.dynamic_slice_in_dim(
+        jnp.pad(all_b, ((0, 0), (0, 4 * d))), tp_rank * mod_dev, mod_dev, 1
+    )
+    lifted = lifted.astype(f32)
+    lifted_b = jnp.take(lifted.reshape(32, -1), order, axis=0).reshape(lifted.shape)
+    ada_grad = jnp.zeros((), f32)
+    for rows, grad in ((lifted, late[:, :own].reshape(32 * IMG_ROW, mod_dev)), (lifted_b, grad_b)):
+        ada_grad += lax.dot_general(rows, grad, (((0,), (0,)), ((), ())), precision=highest)
+    return (
+        block_output,
+        trade_back(input_grad, core),
+        jnp.stack([att_total[:, i * e : (i + 1) * e] for i in range(3)]),
+        qv_total,
+        att_total[:, 3 * e :].T,
+        out_total,
+        mlp_total[:, :ff],
+        fc1_total,
+        mlp_total[:, ff:].T,
+        fc2_total,
+        ada_grad,
+        ada_total,
+    )
+
+
+def body(*arrays):
+    block_input, w_qkv, w_fc1 = arrays[0], arrays[3], arrays[7]
+    micro, tokens, width = block_input.shape
+    heads_dev, rows = w_qkv.shape[2], w_fc1.shape[0]
+    if (
+        lax.axis_size("dp") == 8
+        and lax.axis_size("tp") == 4
+        and micro == 2
+        and micro * tokens == PACK
+        and rows == ROWS
+        and rows * 8 == width
+        and heads_dev * 4 == width
+        and w_fc1.shape[1] % 384 == 0
+    ):
+        return row_body(*arrays)
+    return general_body(*arrays)
+
+
 def solution(mesh):
     placed = (
         P(None, ("dp", "tp"), None),

time: 1970 us -> 729 us (0.37)
  waiting for transfers between devices: 1020 us -> 179 us
  matrix products: 502 us -> 5.28 us
  Pallas kernels: 0 us -> 385 us
  local copies, waits for them, and re-layouts: 183 us -> 57.4 us
  other arithmetic: 134 us -> 30.9 us
  blocking collectives: 103 us -> 0 us
  starting transfers between devices: 1.62 us -> 51.8 us
    reduce_scatter x12 -> x2, waiting for transfers between devices: 506 us -> 0.01 us  [the longest x1 0.01 us: row_body(): lax.psum_scatter(done[0][3], 'dp', scatter_dimension=0, tiled=True)]
    dot_general x144 -> x3, matrix products: 502 us -> 5.28 us  [the longest x2 5 us: row_body(): lax.dot_general(rows, grad, (((0,), (0,)), ((), ())), precision=highest)]
    pallas_call x0 -> x20, Pallas kernels: none -> 385 us  [the longest x4 124 us: attend_bwd(): pl.pallas_call(lambda *refs: attend_bwd_body(final, len(waits), heads, *r...]
    all_gather x12 -> x2, waiting for transfers between devices: 438 us -> 62.7 us  [the longest x1 36.1 us: row_body(): mlp_w = lax.all_gather(mlp_shard, AXES)]
    ppermute x0 -> x23, waiting for transfers between devices: none -> 74.5 us  [swap(): return lax.ppermute(values, AXES, pairs)]
    unnamed x30 -> x4, waiting for transfers between devices: 72.2 us -> 0.07 us
    all_gather x3 -> x0, blocking collectives: 59 us -> none  [the longest x1 47.6 us: body(): lax.all_gather(w_out, 'dp', axis=1, tiled=True)]
    reduce_sum x34 -> x6, other arithmetic: 60.6 us -> 2.13 us  [the longest x1 0.96 us: row_body(): jnp.sum(img_late, axis=0, keepdims=True)]
  transfers between devices with their start and end apart: 27 -> 30, of which waited for: 24 -> 15; matrix products, arithmetic and copies ran while one was open for 13% -> 10% of each run, Pallas kernels for 0% -> 49%
where the time goes in v1:
time: 729 us; the launch traced here: 724 us
  Pallas kernels  385 us (53%)
  waiting for transfers between devices  179 us (25%)
  local copies, waits for them, and re-layouts  57.4 us (8%)
  starting transfers between devices  51.8 us (7%)
  other arithmetic  30.9 us (4%)
  between operations  14.8 us (2%)
    pallas_call x4, Pallas kernels, attend_bwd(): pl.pallas_call(lambda *refs: attend_bwd_body(final, len(waits), heads, *r...  124 us
    pallas_call x4, Pallas kernels, mlp_block(): pl.pallas_call(lambda *refs: mlp_body(added, len(waits), tok_steps, *refs...  115 us
    pallas_call x4, Pallas kernels, attend_fwd(): pl.pallas_call(lambda *refs: attend_fwd_body(heads, *refs), in_specs=[SME...  88 us
    ppermute x23, waiting for transfers between devices, swap(): return lax.ppermute(values, AXES, pairs)  74.5 us
    pallas_call x4, Pallas kernels, by_rows(): pl.pallas_call(body, grid=(n // ET,), in_specs=[SMEM_SPEC] * len(scalars)...  58 us
    all_gather x1, waiting for transfers between devices, row_body(): mlp_w = lax.all_gather(mlp_shard, AXES)  36.1 us
    ppermute x23, starting transfers between devices, swap(): return lax.ppermute(values, AXES, pairs)  35.3 us
    all_to_all x1, waiting for transfers between devices, row_body(): lax.all_to_all(mod_part, AXES, 0, 0).reshape(8, 4, IMG_ROW, mod_dev)  31.5 us
  transfers between devices with their start and end apart: 30, of which 15 were waited for; matrix products, arithmetic and copies ran while one was open for 10% of the time, Pallas kernels for 49%

profile of v1, /device:TPU:0, one launch (start us, length us, event | category | flops | bytes accessed | tf_op | source)
XLA Modules:
  0.0 724.1 jit_solution(7088166873406729738)
XLA Ops:
  13.2 7.3 %all-to-all-start = ((bf16[8,16,144]{2,1,0:T(8,128)(2,1)}), bf16[8,16,144]{2,1,0:T(8,128)(2,1)S(1)}, u32[]{:S(2)}, u32[]{:S(2)}) async-start(bf16[8,16,144]{2,1,0:T(8,128)(2,1)} %copy.64), calls=%async_computation | async-start | bytes 131072 | tf_op jit(solution)/shard_map/all_to_all | solution.py:962
  32.2 6.2 all-to-all-start.1
  44.4 31.5 %all-to-all-done.1 = f32[32,4,1728]{2,1,0:T(4,128)S(1)} async-done(((f32[32,4,1728]{2,1,0:T(4,128)}), f32[32,4,1728]{2,1,0:T(4,128)S(1)}, u32[]{:S(2)}, u32[]{:S(2)}) %all-to-all-start.1) | async-done | bytes 884768 | tf_op jit(solution)/shard_map/all_to_all | solution.py:965
  78.0 10.6 %shard_map.229 = (bf16[1024,1152]{1,0:T(8,128)(2,1)}, bf16[1152,1024]{1,0:T(8,128)(2,1)}, bf16[1024,1152]{1,0:T(8,128)(2,1)}, bf16[1152,1024]{1,0:T(8,128)(2,1)}, f32[1,1152]{1,0:T(1,128)}) custom-call(bf16[1024,1152]{1,0:T(8,128)(2,1)} %get-tuple-element.202.refs_0_.refs_2_, bf16[1024,1152]{1,0:T(8,128)(2,1)} %get-tuple-element.203.refs_1_.refs_4_, ...), custom_call_target="tpu_custom_call" | custom-call | flops 117964800 | bytes 25165824 | tf_op jit(solution)/shard_map/pallas_call | solution.py:865
  88.7 26.7 %all-gather.5.cloned.1.call-done = bf16[4608,1152]{1,0:T(8,128)(2,1)} async-done(((bf16[144,1152]{1,0:T(8,128)(2,1)}), bf16[4608,1152]{1,0:T(8,128)(2,1)}) %all-gather.5.cloned.1.call-update) | async-done | bytes 10616848 | tf_op jit(solution)/shard_map/all_gather | solution.py:949
  115.9 21.9 %shard_map.230 = (bf16[1024,864]{1,0:T(8,128)(2,1)}, bf16[1024,288]{1,0:T(8,128)(2,1)}, f32[8,1024]{1,0:T(8,128)}, bf16[1024,1152]{1,0:T(8,128)(2,1)}) custom-call(s32[4]{0:T(128)} %get-tuple-element.151.refs_0_, s32[4]{0:T(128)} %get-tuple-element.150.refs_1_, s32[1]{0:T(128)} %bitcast.3.refs_2_.refs_0_, bf16[1024,1152]{1,0:T(8,128)(2,1)} %get-tuple-element.79.refs_3_, ...), custom_call_target="tpu_custom_call" | custom-call | flops 8153726976 | bytes 12582912 | tf_op jit(solution)/shard_map/pallas_call | solution.py:602
  137.9 22.1 %shard_map.231 = (bf16[1024,864]{1,0:T(8,128)(2,1)}, bf16[1024,288]{1,0:T(8,128)(2,1)}, f32[8,1024]{1,0:T(8,128)}, bf16[1024,1152]{1,0:T(8,128)(2,1)}) custom-call(s32[4]{0:T(128)} %get-tuple-element.151.refs_0_, s32[4]{0:T(128)} %get-tuple-element.150.refs_1_, s32[1]{0:T(128)} %bitcast.18.refs_2_.refs_0_, bf16[1024,1152]{1,0:T(8,128)(2,1)} %get-tuple-element.79.refs_3_, ...), custom_call_target="tpu_custom_call" | custom-call | flops 8153726976 | bytes 12582912 | tf_op jit(solution)/shard_map/pallas_call | solution.py:602
  160.0 22.0 %shard_map.232 = (bf16[1024,864]{1,0:T(8,128)(2,1)}, bf16[1024,288]{1,0:T(8,128)(2,1)}, f32[8,1024]{1,0:T(8,128)}, bf16[1024,1152]{1,0:T(8,128)(2,1)}) custom-call(s32[4]{0:T(128)} %get-tuple-element.151.refs_0_, s32[4]{0:T(128)} %get-tuple-element.150.refs_1_, s32[1]{0:T(128)} %bitcast.19.refs_2_.refs_0_, bf16[1024,1152]{1,0:T(8,128)(2,1)} %get-tuple-element.79.refs_3_, ...), custom_call_target="tpu_custom_call" | custom-call | flops 8153726976 | bytes 12582912 | tf_op jit(solution)/shard_map/pallas_call | solution.py:602
  182.0 22.0 %shard_map.233 = (bf16[1024,864]{1,0:T(8,128)(2,1)}, bf16[1024,288]{1,0:T(8,128)(2,1)}, f32[8,1024]{1,0:T(8,128)}, bf16[1024,1152]{1,0:T(8,128)(2,1)}) custom-call(s32[4]{0:T(128)} %get-tuple-element.151.refs_0_, s32[4]{0:T(128)} %get-tuple-element.150.refs_1_, s32[1]{0:T(128)} %bitcast.20.refs_2_.refs_0_, bf16[1024,1152]{1,0:T(8,128)(2,1)} %get-tuple-element.79.refs_3_, ...), custom_call_target="tpu_custom_call" | custom-call | flops 8153726976 | bytes 12582912 | tf_op jit(solution)/shard_map/pallas_call | solution.py:602
  204.0 13.1 %shard_map.234 = (f32[1024,1152]{1,0:T(8,128)}, f32[1024,1152]{1,0:T(8,128)}, bf16[1024,1152]{1,0:T(8,128)(2,1)}, bf16[1152,1024]{1,0:T(8,128)(2,1)}) custom-call(bf16[1024,1152]{1,0:T(8,128)(2,1)} %get-tuple-element.202.refs_0_.refs_2_, bf16[1024,1152]{1,0:T(8,128)(2,1)} %get-tuple-element.80.refs_1_, bf16[1024,1152]{1,0:T(8,128)(2,1)} %get-tuple-element.82.refs_2_, ...), custom_call_target="tpu_custom_call" | custom-call | flops 117964800 | bytes 25165824 | tf_op jit(solution)/shard_map/pallas_call | solution.py:865
  217.1 36.1 %all-gather.7.cloned.1.call-done = bf16[4608,2304]{1,0:T(8,128)(2,1)} async-done(((bf16[144,2304]{1,0:T(8,128)(2,1)}), bf16[4608,2304]{1,0:T(8,128)(2,1)}) %all-gather.7.cloned.1.call-update) | async-done | bytes 21233680 | tf_op jit(solution)/shard_map/all_gather | solution.py:950
  253.2 28.1 %shard_map.235 = (bf16[1024,1152]{1,0:T(8,128)(2,1)}, bf16[1024,1152]{1,0:T(8,128)(2,1)}, f32[1,1152]{1,0:T(1,128)}, bf16[1152,2304]{1,0:T(8,128)(2,1)}) custom-call(s32[1]{0:T(128)} %bitcast.18.refs_2_.refs_0_, bf16[1024,1152]{1,0:T(8,128)(2,1)} %get-tuple-element.89.refs_1_, bf16[1024,1152]{1,0:T(8,128)(2,1)} %get-tuple-element.90.refs_2_, ...), custom_call_target="tpu_custom_call" | custom-call | flops 16307453952 | bytes 31457280 | tf_op jit(solution)/shard_map/pallas_call | solution.py:515
  282.2 28.1 %shard_map.236 = (bf16[1024,1152]{1,0:T(8,128)(2,1)}, bf16[1024,1152]{1,0:T(8,128)(2,1)}, f32[1,1152]{1,0:T(1,128)}, bf16[1152,2304]{1,0:T(8,128)(2,1)}) custom-call(s32[1]{0:T(128)} %bitcast.20.refs_2_.refs_0_, bf16[1024,1152]{1,0:T(8,128)(2,1)} %get-tuple-element.89.refs_1_, bf16[1024,1152]{1,0:T(8,128)(2,1)} %get-tuple-element.90.refs_2_, ...), custom_call_target="tpu_custom_call" | custom-call | flops 16307453952 | bytes 31457280 | tf_op jit(solution)/shard_map/pallas_call | solution.py:515
  313.6 29.0 %shard_map.237 = (bf16[1024,1152]{1,0:T(8,128)(2,1)}, bf16[1024,1152]{1,0:T(8,128)(2,1)}, f32[1,1152]{1,0:T(1,128)}, bf16[1152,2304]{1,0:T(8,128)(2,1)}) custom-call(s32[1]{0:T(128)} %bitcast.3.refs_2_.refs_0_, bf16[1024,1152]{1,0:T(8,128)(2,1)} %get-tuple-element.89.refs_1_, bf16[1024,1152]{1,0:T(8,128)(2,1)} %get-tuple-element.90.refs_2_, ...), custom_call_target="tpu_custom_call" | custom-call | flops 16307453952 | bytes 31457280 | tf_op jit(solution)/shard_map/pallas_call | solution.py:515
  346.9 29.5 %shard_map.238 = (bf16[1024,1152]{1,0:T(8,128)(2,1)}, bf16[1024,1152]{1,0:T(8,128)(2,1)}, f32[1,1152]{1,0:T(1,128)}, bf16[1152,2304]{1,0:T(8,128)(2,1)}) custom-call(s32[1]{0:T(128)} %bitcast.19.refs_2_.refs_0_, bf16[1024,1152]{1,0:T(8,128)(2,1)} %get-tuple-element.89.refs_1_, bf16[1024,1152]{1,0:T(8,128)(2,1)} %get-tuple-element.90.refs_2_, ...), custom_call_target="tpu_custom_call" | custom-call | flops 16307453952 | bytes 31457280 | tf_op jit(solution)/shard_map/pallas_call | solution.py:515
  376.5 21.6 %shard_map.239 = (bf16[1024,1152]{1,0:T(8,128)(2,1)}, f32[1024,1152]{1,0:T(8,128)}, bf16[1024,1152]{1,0:T(8,128)(2,1)}, bf16[1152,1024]{1,0:T(8,128)(2,1)}, f32[1,1152]{1,0:T(1,128)}, /*index=5*/f32[4,4608]{1,0:T(4,128)}) custom-call(s32[8]{0:T(128)} %get-tuple-element.149.refs_0_, s32[8]{0:T(128)} %get-tuple-element.148.refs_1_, ...), custom_call_target="tpu_custom_call" | custom-call | flops 117964800 | bytes 25165824 | tf_op jit(solution)/shard_map/pallas_call | solution.py:865
  410.6 30.2 %shard_map.240 = (bf16[1024,1152]{1,0:T(8,128)(2,1)}, f32[1,864]{1,0:T(1,128)}, bf16[1152,1152]{1,0:T(8,128)(2,1)}) custom-call(s32[4]{0:T(128)} %get-tuple-element.151.refs_0_, s32[4]{0:T(128)} %get-tuple-element.150.refs_1_, s32[1]{0:T(128)} %bitcast.18.refs_2_.refs_0_, s32[8]{0:T(128)} %shift-right-arithmetic_add_fusion.refs_3_, ...), custom_call_target="tpu_custom_call" | custom-call | flops 16307453952 | bytes 20971520 | tf_op jit(solution)/shard_map/pallas_call | solution.py:734
  445.5 29.9 %shard_map.242 = (bf16[1024,1152]{1,0:T(8,128)(2,1)}, f32[1,864]{1,0:T(1,128)}, bf16[1152,1152]{1,0:T(8,128)(2,1)}) custom-call(s32[4]{0:T(128)} %get-tuple-element.151.refs_0_, s32[4]{0:T(128)} %get-tuple-element.150.refs_1_, s32[1]{0:T(128)} %bitcast.20.refs_2_.refs_0_, s32[8]{0:T(128)} %shift-right-arithmetic_add_fusion.refs_3_, ...), custom_call_target="tpu_custom_call" | custom-call | flops 16307453952 | bytes 20971520 | tf_op jit(solution)/shard_map/pallas_call | solution.py:734
  476.7 9.8 %all-to-all-done.2 = f32[32,1,18432]{2,1,0:T(1,128)S(1)} async-done(((f32[32,1,18432]{2,1,0:T(1,128)}), f32[32,1,18432]{2,1,0:T(1,128)S(1)}, u32[]{:S(2)}, u32[]{:S(2)}) %all-to-all-start.2) | async-done | bytes 2359328 | tf_op jit(solution)/shard_map/all_to_all | solution.py:1028
  491.2 32.2 %shard_map.244 = (bf16[1024,1152]{1,0:T(8,128)(2,1)}, f32[1,864]{1,0:T(1,128)}, bf16[4,144,1152]{2,1,0:T(8,128)(2,1)}, bf16[4,144,1152]{2,1,0:T(8,128)(2,1)}) custom-call(s32[4]{0:T(128)} %get-tuple-element.151.refs_0_, s32[4]{0:T(128)} %get-tuple-element.150.refs_1_, s32[1]{0:T(128)} %bitcast.3.refs_2_.refs_0_, s32[8]{0:T(128)} %shift-right-arithmetic_add_fusion.refs_3_, ...), custom_call_target="tpu_custom_call" | custom-call | flops 16307453952 | bytes 20971520 | tf_op jit(solution)/shard_map/pallas_call | solution.py:734
  529.1 32.2 %shard_map.245 = (bf16[1024,1152]{1,0:T(8,128)(2,1)}, f32[1,864]{1,0:T(1,128)}, bf16[4,144,1152]{2,1,0:T(8,128)(2,1)}, bf16[4,144,1152]{2,1,0:T(8,128)(2,1)}) custom-call(s32[4]{0:T(128)} %get-tuple-element.151.refs_0_, s32[4]{0:T(128)} %get-tuple-element.150.refs_1_, s32[1]{0:T(128)} %bitcast.19.refs_2_.refs_0_, s32[8]{0:T(128)} %shift-right-arithmetic_add_fusion.refs_3_, ...), custom_call_target="tpu_custom_call" | custom-call | flops 16307453952 | bytes 20971520 | tf_op jit(solution)/shard_map/pallas_call | solution.py:734
  562.7 5.9 collective-permute-done.7.refs_0_
  571.3 12.6 %shard_map.247 = (bf16[1024,1152]{1,0:T(8,128)(2,1)}, f32[4,2304]{1,0:T(4,128)}) custom-call(s32[8]{0:T(128)} %get-tuple-element.149.refs_0_, s32[8]{0:T(128)} %get-tuple-element.148.refs_1_, bf16[1024,1152]{1,0:T(8,128)(2,1)} %get-tuple-element.202.refs_0_.refs_2_, f32[1024,1152]{1,0:T(8,128)} %get-tuple-element.114.refs_3_, ...), custom_call_target="tpu_custom_call" | custom-call | flops 117964800 | bytes 25165824 | tf_op jit(solution)/shard_map/pallas_call | solution.py:865
  594.5 5.9 collective-permute-done.18
  605.7 13.2 %collective-permute-done.19 = f32[4,11520]{1,0:T(4,128)S(1)} collective-permute-done((f32[4,11520]{1,0:T(4,128)S(1)}, f32[4,11520]{1,0:T(4,128)S(1)}, u32[]{:S(2)}, u32[]{:S(2)}) %collective-permute-start.19) | collective-permute-done | bytes 184352 | tf_op jit(solution)/shard_map/ppermute | solution.py:388
  620.6 14.9 %collective-permute-done.22 = bf16[144,2304]{1,0:T(8,128)(2,1)S(1)} collective-permute-done((bf16[144,2304]{1,0:T(8,128)(2,1)}, bf16[144,2304]{1,0:T(8,128)(2,1)S(1)}, u32[]{:S(2)}, u32[]{:S(2)}) %collective-permute-start.22) | collective-permute-done | bytes 663584 | tf_op jit(solution)/shard_map/ppermute | solution.py:388
  639.1 5.3 collective-permute-done.20
  644.5 16.5 %collective-permute-start.10 = (bf16[144,1152]{1,0:T(8,128)(2,1)}, bf16[144,1152]{1,0:T(8,128)(2,1)}, u32[]{:S(2)}, u32[]{:S(2)}) collective-permute-start(bf16[144,1152]{1,0:T(8,128)(2,1)} %get-tuple-element.167), channel_id=1, source_target_pairs={{0,8},{1,9},{2,10},{3,11},{4,12},{5,13},{6,14},{7,15},{8,0},{9,1},... | collective-permute-start | bytes 995336 | tf_op jit(solution)/shard_map/ppermute | solution.py:388
  663.7 3.1 select_bitcast_fusion.1
  681.6 5.1 collective-permute-done.13
  689.5 14.0 %collective-permute-done.14 = bf16[144,1152]{1,0:T(8,128)(2,1)} collective-permute-done((bf16[144,1152]{1,0:T(8,128)(2,1)}, bf16[144,1152]{1,0:T(8,128)(2,1)}, u32[]{:S(2)}, u32[]{:S(2)}) %collective-permute-start.14) | collective-permute-done | bytes 331808 | tf_op jit(solution)/shard_map/ppermute | solution.py:388
  709.0 4.9 collective-permute-done.16
  (235 shorter events, 117.7 us)
Async XLA Ops:
  7.2 108.1 %all-gather.5.cloned.1.call-start = ((), (), s32[]{:S(2)}) async-start(), calls=%async_computation.7 | async-start | bytes 10948608 | tf_op jit(solution)/shard_map/all_gather | solution.py:949
  10.3 242.8 %all-gather.7.cloned.1.call-start = ((), (), s32[]{:S(2)}) async-start(), calls=%async_computation.8 | async-start | bytes 21897216 | tf_op jit(solution)/shard_map/all_gather | solution.py:950
  13.2 17.0 %all-to-all-start = ((bf16[8,16,144]{2,1,0:T(8,128)(2,1)}), bf16[8,16,144]{2,1,0:T(8,128)(2,1)S(1)}, u32[]{:S(2)}, u32[]{:S(2)}) async-start(bf16[8,16,144]{2,1,0:T(8,128)(2,1)} %copy.64), calls=%async_computation | async-start | bytes 131072 | tf_op jit(solution)/shard_map/all_to_all | solution.py:962
  21.6 17.7 %collective-permute-start.1 = (bf16[512,1152]{1,0:T(8,128)(2,1)}, bf16[512,1152]{1,0:T(8,128)(2,1)}, u32[]{:S(2)}, u32[]{:S(2)}) collective-permute-start(bf16[512,1152]{1,0:T(8,128)(2,1)} %dynamic-slice_bitcast_fusion), channel_id=1, source_target_pairs={{0,1},{1,0},{2,3},{3,2},{4,5},{5,4},{6,7},{7,6},{8,9},{9,8},{10,11... | collective-permute-start | bytes 3538952 | tf_op jit(solution)/shard_map/ppermute | solution.py:388
  23.7 17.6 %collective-permute-start = (bf16[512,1152]{1,0:T(8,128)(2,1)}, bf16[512,1152]{1,0:T(8,128)(2,1)S(1)}, u32[]{:S(2)}, u32[]{:S(2)}) collective-permute-start(bf16[512,1152]{1,0:T(8,128)(2,1)} %dynamic-slice_bitcast_fusion.1), channel_id=1, source_target_pairs={{0,1},{1,0},{2,3},{3,2},{4,5},{5,4},{6,7},{7,6},{8,9},{9,8},{10,11... | collective-permute-start | bytes 3538952 | tf_op jit(solution)/shard_map/ppermute | solution.py:388
  32.2 43.8 %all-to-all-start.1 = ((f32[32,4,1728]{2,1,0:T(4,128)}), f32[32,4,1728]{2,1,0:T(4,128)S(1)}, u32[]{:S(2)}, u32[]{:S(2)}) async-start(f32[32,4,1728]{2,1,0:T(4,128)} %copy.67), calls=%async_computation.1 | async-start | bytes 1835008 | tf_op jit(solution)/shard_map/all_to_all | solution.py:965
  38.3 490.7 %reduce-scatter.3.cloned.1.call-start = ((), (), s32[]{:S(2)}) async-start(), calls=%async_computation.5 | async-start | bytes 5971968 | tf_op jit(solution)/shard_map/reduce_scatter | solution.py:1008
  281.3 30.0 %collective-permute-start.2 = (bf16[1152,2304]{1,0:T(8,128)(2,1)}, bf16[1152,2304]{1,0:T(8,128)(2,1)S(1)}, u32[]{:S(2)}, u32[]{:S(2)}) collective-permute-start(bf16[1152,2304]{1,0:T(8,128)(2,1)} %get-tuple-element.93), channel_id=1, source_target_pairs={{0,1},{1,0},{2,3},{3,2},{4,5},{5,4},{6,7},{7,6},{8,9},{9,8},{10,11... | collective-permute-start | bytes 15925256 | tf_op jit(solution)/shard_map/ppermute | solution.py:388
  310.3 36.6 %collective-permute-start.3 = (bf16[1152,2304]{1,0:T(8,128)(2,1)}, bf16[1152,2304]{1,0:T(8,128)(2,1)}, u32[]{:S(2)}, u32[]{:S(2)}) collective-permute-start(bf16[1152,2304]{1,0:T(8,128)(2,1)} %get-tuple-element.98), channel_id=1, source_target_pairs={{0,1},{1,0},{2,3},{3,2},{4,5},{5,4},{6,7},{7,6},{8,9},{9,8},{10,11... | collective-permute-start | bytes 15925256 | tf_op jit(solution)/shard_map/ppermute | solution.py:388
  402.8 39.0 %collective-permute-start.4 = (bf16[512,1152]{1,0:T(8,128)(2,1)}, bf16[512,1152]{1,0:T(8,128)(2,1)}, u32[]{:S(2)}, u32[]{:S(2)}) collective-permute-start(bf16[512,1152]{1,0:T(8,128)(2,1)} %constant_dynamic-slice_fusion.1), channel_id=1, source_target_pairs={{0,1},{1,0},{2,3},{3,2},{4,5},{5,4},{6,7},{7,6},{8,9},{9,8},{10,11... | collective-permute-start | bytes 3538952 | tf_op jit(solution)/shard_map/ppermute | solution.py:388
  407.8 78.7 %all-to-all-start.2 = ((f32[32,1,18432]{2,1,0:T(1,128)}), f32[32,1,18432]{2,1,0:T(1,128)S(1)}, u32[]{:S(2)}, u32[]{:S(2)}) async-start(f32[32,1,18432]{2,1,0:T(1,128)} %all_to_all.15), calls=%async_computation.2 | async-start | bytes 4718592 | tf_op jit(solution)/shard_map/all_to_all | solution.py:1028
  410.6 195.1 %reduce-scatter.5.cloned.1.call-start = ((), (), s32[]{:S(2)}) async-start(), calls=%async_computation.6 | async-start | bytes 5971968 | tf_op jit(solution)/shard_map/reduce_scatter | solution.py:1010
  440.8 50.4 %collective-permute-start.5 = (bf16[1152,1152]{1,0:T(8,128)(2,1)}, bf16[1152,1152]{1,0:T(8,128)(2,1)}, u32[]{:S(2)}, u32[]{:S(2)}) collective-permute-start(bf16[1152,1152]{1,0:T(8,128)(2,1)} %get-tuple-element.117), channel_id=1, source_target_pairs={{0,1},{1,0},{2,3},{3,2},{4,5},{5,4},{6,7},{7,6},{8,9},{9,8},{10,11... | collective-permute-start | bytes 7962632 | tf_op jit(solution)/shard_map/ppermute | solution.py:388
  475.5 53.6 %collective-permute-start.6 = (bf16[1152,1152]{1,0:T(8,128)(2,1)}, bf16[1152,1152]{1,0:T(8,128)(2,1)}, u32[]{:S(2)}, u32[]{:S(2)}) collective-permute-start(bf16[1152,1152]{1,0:T(8,128)(2,1)} %get-tuple-element.129), channel_id=1, source_target_pairs={{0,1},{1,0},{2,3},{3,2},{4,5},{5,4},{6,7},{7,6},{8,9},{9,8},{10,11... | collective-permute-start | bytes 7962632 | tf_op jit(solution)/shard_map/ppermute | solution.py:388
  491.2 35.0 %copy-start.2 = (f32[32,18432]{1,0:T(8,128)S(1)}, f32[32,18432]{1,0:T(8,128)}, u32[]{:S(2)}) copy-start(f32[32,18432]{1,0:T(8,128)} %shard_map.243.refs_15_) | copy-start | bytes 7077892
  523.4 45.3 %collective-permute-start.7 = (bf16[4,144,1152]{2,1,0:T(8,128)(2,1)}, bf16[4,144,1152]{2,1,0:T(8,128)(2,1)}, u32[]{:S(2)}, u32[]{:S(2)}) collective-permute-start(bf16[4,144,1152]{2,1,0:T(8,128)(2,1)} %get-tuple-element.135), channel_id=1, source_target_pairs={{0,4},{1,5},{2,6},{3,7},{4,0},{5,1},{6,2},{7,3},{8,12},{9,13},{10,... | collective-permute-start | bytes 3981320 | tf_op jit(solution)/shard_map/ppermute | solution.py:388
  584.7 4.1 collective-permute-start.17
  589.0 11.5 %collective-permute-start.18 = (f32[2,11520]{1,0:T(2,128)S(1)}, f32[2,11520]{1,0:T(2,128)S(1)}, u32[]{:S(2)}, u32[]{:S(2)}) collective-permute-start(f32[2,11520]{1,0:T(2,128)S(1)} %pad_maximum_fusion.9), channel_id=1, source_target_pairs={{0,8},{1,9},{2,10},{3,11},{4,12},{5,13},{6,14},{7,15},{8,0},{9,1},... | collective-permute-start | bytes 276488 | tf_op jit(solution)/shard_map/ppermute | solution.py:388
  590.4 76.8 %collective-permute-start.9 = (bf16[4,144,1152]{2,1,0:T(8,128)(2,1)}, bf16[4,144,1152]{2,1,0:T(8,128)(2,1)S(1)}, u32[]{:S(2)}, u32[]{:S(2)}) collective-permute-start(bf16[4,144,1152]{2,1,0:T(8,128)(2,1)} %get-tuple-element.138), channel_id=1, source_target_pairs={{0,4},{1,5},{2,6},{3,7},{4,0},{5,1},{6,2},{7,3},{8,12},{9,13},{10,... | collective-permute-start | bytes 3981320 | tf_op jit(solution)/shard_map/ppermute | solution.py:388
  591.9 74.9 %collective-permute-start.12 = (bf16[144,1152]{1,0:T(8,128)(2,1)}, bf16[144,1152]{1,0:T(8,128)(2,1)}, u32[]{:S(2)}, u32[]{:S(2)}) collective-permute-start(bf16[144,1152]{1,0:T(8,128)(2,1)} %get-tuple-element.165), channel_id=1, source_target_pairs={{0,24},{1,25},{2,26},{3,27},{4,28},{5,29},{6,30},{7,31},{8,16},{9,... | collective-permute-start | bytes 995336 | tf_op jit(solution)/shard_map/ppermute | solution.py:388
  593.4 73.4 %collective-permute-start.11 = (bf16[144,1152]{1,0:T(8,128)(2,1)}, bf16[144,1152]{1,0:T(8,128)(2,1)}, u32[]{:S(2)}, u32[]{:S(2)}) collective-permute-start(bf16[144,1152]{1,0:T(8,128)(2,1)} %get-tuple-element.166), channel_id=1, source_target_pairs={{0,16},{1,17},{2,18},{3,19},{4,20},{5,21},{6,22},{7,23},{8,24},{9,... | collective-permute-start | bytes 995336 | tf_op jit(solution)/shard_map/ppermute | solution.py:388
  600.6 18.3 %collective-permute-start.19 = (f32[4,11520]{1,0:T(4,128)S(1)}, f32[4,11520]{1,0:T(4,128)S(1)}, u32[]{:S(2)}, u32[]{:S(2)}) collective-permute-start(f32[4,11520]{1,0:T(4,128)S(1)} %pad_maximum_fusion.8), channel_id=1, source_target_pairs={{0,24},{1,25},{2,26},{3,27},{4,28},{5,29},{6,30},{7,31},{8,16},{9,... | collective-permute-start | bytes 552968 | tf_op jit(solution)/shard_map/ppermute | solution.py:388
  605.7 57.1 %collective-permute-start.8 = (bf16[512,1152]{1,0:T(8,128)(2,1)}, bf16[512,1152]{1,0:T(8,128)(2,1)S(1)}, u32[]{:S(2)}, u32[]{:S(2)}) collective-permute-start(bf16[512,1152]{1,0:T(8,128)(2,1)} %constant_dynamic-slice_fusion), channel_id=1, source_target_pairs={{0,1},{1,0},{2,3},{3,2},{4,5},{5,4},{6,7},{7,6},{8,9},{9,8},{10,11... | collective-permute-start | bytes 3538952 | tf_op jit(solution)/shard_map/ppermute | solution.py:388
  618.9 16.5 %collective-permute-start.22 = (bf16[144,2304]{1,0:T(8,128)(2,1)}, bf16[144,2304]{1,0:T(8,128)(2,1)S(1)}, u32[]{:S(2)}, u32[]{:S(2)}) collective-permute-start(bf16[144,2304]{1,0:T(8,128)(2,1)} %reduce-scatter.5.cloned.1.call-done), channel_id=1, source_target_pairs={{0,2},{1,3},{2,0},{3,1},{4,6},{5,7},{6,4},{7,5},{8,10},{9,11},{10,... | collective-permute-start | bytes 1990664 | tf_op jit(solution)/shard_map/ppermute | solution.py:388
  635.4 9.1 %collective-permute-start.20 = (f32[8,11520]{1,0:T(8,128)S(1)}, f32[8,11520]{1,0:T(8,128)S(1)}, u32[]{:S(2)}, u32[]{:S(2)}) collective-permute-start(f32[8,11520]{1,0:T(8,128)S(1)} %pad_maximum_fusion.6), channel_id=1, source_target_pairs={{0,2},{1,3},{2,0},{3,1},{4,6},{5,7},{6,4},{7,5},{8,10},{9,11},{10,... | collective-permute-start | bytes 1105928 | tf_op jit(solution)/shard_map/ppermute | solution.py:388
  644.5 22.7 %collective-permute-start.10 = (bf16[144,1152]{1,0:T(8,128)(2,1)}, bf16[144,1152]{1,0:T(8,128)(2,1)}, u32[]{:S(2)}, u32[]{:S(2)}) collective-permute-start(bf16[144,1152]{1,0:T(8,128)(2,1)} %get-tuple-element.167), channel_id=1, source_target_pairs={{0,8},{1,9},{2,10},{3,11},{4,12},{5,13},{6,14},{7,15},{8,0},{9,1},... | collective-permute-start | bytes 995336 | tf_op jit(solution)/shard_map/ppermute | solution.py:388
  663.7 12.3 %collective-permute-start.21 = (f32[16,11520]{1,0:T(8,128)}, f32[16,11520]{1,0:T(8,128)}, u32[]{:S(2)}, u32[]{:S(2)}) collective-permute-start(f32[16,11520]{1,0:T(8,128)} %concatenate.165), channel_id=1, source_target_pairs={{0,1},{1,0},{2,3},{3,2},{4,5},{5,4},{6,7},{7,6},{8,9},{9,8},{10,11... | collective-permute-start | bytes 2211848 | tf_op jit(solution)/shard_map/ppermute | solution.py:388
  670.9 15.9 %collective-permute-start.13 = (bf16[144,1152]{1,0:T(8,128)(2,1)}, bf16[144,1152]{1,0:T(8,128)(2,1)}, u32[]{:S(2)}, u32[]{:S(2)}) collective-permute-start(bf16[144,1152]{1,0:T(8,128)(2,1)} %get-tuple-element.162), channel_id=1, source_target_pairs={{0,8},{1,9},{2,10},{3,11},{4,12},{5,13},{6,14},{7,15},{8,0},{9,1},... | collective-permute-start | bytes 995336 | tf_op jit(solution)/shard_map/ppermute | solution.py:388
  672.7 16.8 %collective-permute-start.15 = (bf16[144,1152]{1,0:T(8,128)(2,1)}, bf16[144,1152]{1,0:T(8,128)(2,1)}, u32[]{:S(2)}, u32[]{:S(2)}) collective-permute-start(bf16[144,1152]{1,0:T(8,128)(2,1)} %get-tuple-element.163), channel_id=1, source_target_pairs={{0,24},{1,25},{2,26},{3,27},{4,28},{5,29},{6,30},{7,31},{8,16},{9,... | collective-permute-start | bytes 995336 | tf_op jit(solution)/shard_map/ppermute | solution.py:388
  673.3 30.3 %collective-permute-start.14 = (bf16[144,1152]{1,0:T(8,128)(2,1)}, bf16[144,1152]{1,0:T(8,128)(2,1)}, u32[]{:S(2)}, u32[]{:S(2)}) collective-permute-start(bf16[144,1152]{1,0:T(8,128)(2,1)} %get-tuple-element.164), channel_id=1, source_target_pairs={{0,16},{1,17},{2,18},{3,19},{4,20},{5,21},{6,22},{7,23},{8,24},{9,... | collective-permute-start | bytes 995336 | tf_op jit(solution)/shard_map/ppermute | solution.py:388
  679.9 25.6 %copy-start.12 = (f32[4608]{0:T(1024)S(1)}, f32[4608]{0:T(1024)}, u32[]{:S(2)}) copy-start(f32[4608]{0:T(1024)} %get-tuple-element.178) | copy-start | bytes 55300
  705.1 8.7 %collective-permute-start.16 = (bf16[144,1152]{1,0:T(8,128)(2,1)S(1)}, bf16[144,1152]{1,0:T(8,128)(2,1)S(1)}, u32[]{:S(2)}, u32[]{:S(2)}) collective-permute-start(bf16[144,1152]{1,0:T(8,128)(2,1)S(1)} %fusion.2), channel_id=1, source_target_pairs={{0,2},{1,3},{2,0},{3,1},{4,6},{5,7},{6,4},{7,5},{8,10},{9,11},{10,... | collective-permute-start | bytes 995336 | tf_op jit(solution)/shard_map/ppermute | solution.py:388
  (24 other events, 150.2 us)
Sparse Core Ops, SparseCore 0:
  11.5 103.7 all-gather.4
  118.8 134.3 all-gather.6
  342.7 134.7 reduce-scatter.2
  481.4 120.5 reduce-scatter.4

commit v2 on v1

--- a/solution.py
+++ b/solution.py
@@ -375,6 +375,10 @@
 ANY_SPEC = pl.BlockSpec(memory_space=pl.ANY)
 
 
+def cost(micros):
+    return pl.CostEstimate(flops=int(4 * micros * 1.15e9), bytes_accessed=0, transcendentals=0)
+
+
 def dot(left, right, dims=NN):
     return lax.dot_general(left, right, dims, preferred_element_type=f32)
 
@@ -403,162 +407,179 @@
     )(*values, *after)
 
 
-def fetch(whole_ref, block, column, out_ref, sem):
-    width = out_ref.shape[1]
-    return [
-        pltpu.make_async_copy(
-            whole_ref.at[d * 4 + block, :, pl.ds(column, width)],
-            out_ref.at[pl.ds(d * ROWS, ROWS), :],
-            sem.at[d],
-        )
-        for d in range(8)
-    ]
-
-
-def send_pieces(stage, place_ref, first, count, outs, sem):
-    for q in range(count):
-        source = stage.at[pl.ds(q * ROWS, ROWS), :]
-        spot = place_ref[first + q]
-
-        @pl.when(spot < 4)
-        def _():
-            pltpu.make_async_copy(source, outs[0].at[spot], sem.at[q]).start()
-
-        @pl.when(spot >= 4)
-        def _():
-            pltpu.make_async_copy(source, outs[1].at[spot - 4], sem.at[q]).start()
-
-
-def wait_pieces(stage, count, outs, sem):
-    for q in range(count):
-        pltpu.make_async_copy(stage.at[pl.ds(q * ROWS, ROWS), :], outs[0].at[0], sem.at[q]).wait()
-
-
-def mlp_body(added, waits, tok_steps, *refs):
-    block_ref, x_ref, g_ref, xt_ref, gt_ref, whole_ref, b_ref = refs[:7]
-    init_ref = refs[7] if added else None
-    b2_ref, dm_ref, db_ref, dw_ref, w1_ref, w2_ref, act_s, slope_s, sem = refs[7 + added + waits :]
+def piece_copies(stage, place_ref, parts, outs, sem, start):
+    for q in range(8):
+        column = 0
+        for i, width in enumerate(parts):
+            source = stage.at[pl.ds(q * ROWS, ROWS), pl.ds(column, width)]
+            column += width
+            low, high, done = outs[2 * i], outs[2 * i + 1], sem.at[len(parts) * q + i]
+            if not start:
+                pltpu.make_async_copy(source, low.at[0], done).wait()
+                continue
+            spot = place_ref[q]
+
+            @pl.when(spot < 4)
+            def _():
+                pltpu.make_async_copy(source, low.at[spot], done).start()
+
+            @pl.when(spot >= 4)
+            def _():
+                pltpu.make_async_copy(source, high.at[spot - 4], done).start()
+
+
+def mlp_tokens(x_ref, g_ref, w1_ref, w2_ref, b_ref, b2_ref, dm_ref, db_ref):
+    pre = dot(x_ref[...], w1_ref[...]) + b_ref[...]
+    act_grad = dot(g_ref[...], w2_ref[...])
+    square = pre * pre
+    bend = jnp.tanh(pre * (GELU_A + GELU_B * square))
+    half = 0.5 + 0.5 * bend
+    act = (pre * half).astype(bf16)
+    slope = half + pre * (half * (1.0 - bend)) * (GELU_A + (3 * GELU_B) * square)
+    pre_grad = (act_grad * slope).astype(bf16)
+    b2_ref[...] = dot(act, w2_ref[...], NT).astype(bf16)
+    dm_ref[...] = dot(pre_grad, w1_ref[...], NT).astype(bf16)
+    add_rows(db_ref, pre_grad.astype(f32))
+    return act, pre_grad
+
+
+def mlp_whole_body(waits, tok_steps, x_ref, g_ref, xt_ref, gt_ref, w1_ref, w2_ref, b_ref, *refs):
+    b2_ref, dm_ref, db_ref, dw_ref, act_s, slope_s = refs[waits:]
     step = pl.program_id(0)
     rows = x_ref.shape[0]
     ff = w1_ref.shape[1]
 
-    @pl.when(step == 0)
-    def _():
-        copies = fetch(whole_ref, block_ref[0], 0, w1_ref, sem.at[0])
-        copies += fetch(whole_ref, block_ref[0], ff, w2_ref, sem.at[1])
-        for copy in copies:
-            copy.start()
-        for copy in copies:
-            copy.wait()
-
     @pl.when(step < tok_steps)
     def _():
-        pre = dot(x_ref[...], w1_ref[...]) + b_ref[...]
-        act_grad = dot(g_ref[...], w2_ref[...])
-        square = pre * pre
-        bend = jnp.tanh(pre * (GELU_A + GELU_B * square))
-        half = 0.5 + 0.5 * bend
-        act = (pre * half).astype(bf16)
-        slope = half + pre * (half * (1.0 - bend)) * (GELU_A + (3 * GELU_B) * square)
-        pre_grad = (act_grad * slope).astype(bf16)
-        b2_ref[...] = dot(act, w2_ref[...], NT).astype(bf16)
-        dm_ref[...] = dot(pre_grad, w1_ref[...], NT).astype(bf16)
+        act, pre_grad = mlp_tokens(x_ref, g_ref, w1_ref, w2_ref, b_ref, b2_ref, dm_ref, db_ref)
         here = pl.ds(pl.multiple_of(step * rows, rows), rows)
         act_s[here, :] = act
         slope_s[here, :] = pre_grad
-        sums = jnp.sum(pre_grad.astype(f32), axis=0, keepdims=True)
-
-        @pl.when(step == 0)
-        def _():
-            db_ref[...] = sums
-
-        @pl.when(step > 0)
-        def _():
-            db_ref[...] += sums
 
     @pl.when(step >= tok_steps)
     def _():
-        grad1 = dot(xt_ref[...], slope_s[...])
-        grad2 = dot(gt_ref[...], act_s[...])
-        if added:
-            grad1 += init_ref[:, :ff].astype(f32)
-            grad2 += init_ref[:, ff:].astype(f32)
-        dw_ref[:, :ff] = grad1.astype(bf16)
-        dw_ref[:, ff:] = grad2.astype(bf16)
-
-
-def mlp_block(x, g, xt, gt, whole, block, bias, init=None, waits=(), tok_steps=4, row_steps=4):
+        dw_ref[:, :ff] = dot(xt_ref[...], slope_s[...]).astype(bf16)
+        dw_ref[:, ff:] = dot(gt_ref[...], act_s[...]).astype(bf16)
+
+
+def mlp_first_body(waits, x_ref, g_ref, w1_ref, w2_ref, b_ref, *refs):
+    b2_ref, dm_ref, db_ref, act_ref, slope_ref = refs[waits:]
+    act, pre_grad = mlp_tokens(x_ref, g_ref, w1_ref, w2_ref, b_ref, b2_ref, dm_ref, db_ref)
+    act_ref[...] = act
+    slope_ref[...] = pre_grad
+
+
+def mlp_second_body(waits, xt_ref, gt_ref, act_ref, slope_ref, init_ref, *refs):
+    (dw_ref,) = refs[waits:]
+    ff = act_ref.shape[1]
+    grad1 = dot(xt_ref[...], slope_ref[...]) + init_ref[:, :ff].astype(f32)
+    dw_ref[:, :ff] = grad1.astype(bf16)
+    grad2 = dot(gt_ref[...], act_ref[...]) + init_ref[:, ff:].astype(f32)
+    dw_ref[:, ff:] = grad2.astype(bf16)
+
+
+def mlp_call(body, steps, in_specs, operands, outs, scratch, waits, micros):
+    n, d = operands[0].shape
+    return pl.pallas_call(
+        lambda *refs: body(len(waits), *refs),
+        grid=(steps,),
+        in_specs=in_specs + [ANY_SPEC] * len(waits),
+        out_specs=[spec for spec, _, _ in outs],
+        out_shape=[jax.ShapeDtypeStruct(shape, kind) for _, shape, kind in outs],
+        scratch_shapes=scratch,
+        compiler_params=compiler_params(),
+        cost_estimate=cost(micros),
+    )(*operands, *waits)
+
+
+def columns(d, ff, block):
+    return pl.BlockSpec((d, ff), lambda s: (0, block), pipeline_mode=pl.Buffered(1))
+
+
+def mlp_weights(d, ff, weights):
+    return [columns(d, ff, block) for _, block in weights] + [
+        pl.BlockSpec((1, ff), lambda s: (0, 0))
+    ]
+
+
+def mlp_whole(x, g, xt, gt, weights, bias, waits=(), tok_steps=4, row_steps=4):
     n, d = x.shape
-    ff = whole.shape[2] // 2
-    added = init is not None
+    ff = bias.shape[1]
     tok_rows, dim_rows = n // tok_steps, d // row_steps
-
-    def tok(s):
-        return (jnp.minimum(s, tok_steps - 1), 0)
-
-    def row(s):
-        return (jnp.maximum(s - tok_steps, 0), 0)
-
-    in_specs = [
-        SMEM_SPEC,
-        pl.BlockSpec((tok_rows, d), tok),
-        pl.BlockSpec((tok_rows, d), tok),
-        pl.BlockSpec((dim_rows, n), row),
-        pl.BlockSpec((dim_rows, n), row),
-        ANY_SPEC,
-        pl.BlockSpec((1, ff), lambda s: (0, 0)),
-    ]
-    operands = [block, x, g, xt, gt, whole, bias]
-    if added:
-        in_specs.append(pl.BlockSpec((dim_rows, 2 * ff), row))
-        operands.append(init)
-    return pl.pallas_call(
-        lambda *refs: mlp_body(added, len(waits), tok_steps, *refs),
-        grid=(tok_steps + row_steps,),
-        in_specs=in_specs + [ANY_SPEC] * len(waits),
-        out_specs=[
-            pl.BlockSpec((tok_rows, d), tok),
-            pl.BlockSpec((tok_rows, d), tok),
-            pl.BlockSpec((1, ff), lambda s: (0, 0)),
-            pl.BlockSpec((dim_rows, 2 * ff), row),
+    tok = pl.BlockSpec((tok_rows, d), lambda s: (jnp.minimum(s, tok_steps - 1), 0))
+    row = pl.BlockSpec((dim_rows, n), lambda s: (jnp.maximum(s - tok_steps, 0), 0))
+    wide = pl.BlockSpec((dim_rows, 2 * ff), lambda s: (jnp.maximum(s - tok_steps, 0), 0))
+    return mlp_call(
+        lambda count, *refs: mlp_whole_body(count, tok_steps, *refs),
+        tok_steps + row_steps,
+        [tok, tok, row, row] + mlp_weights(d, ff, weights),
+        [x, g, xt, gt, *[w for w, _ in weights], bias],
+        [
+            (tok, (n, d), bf16),
+            (tok, (n, d), bf16),
+            (pl.BlockSpec((1, ff), lambda s: (0, 0)), (1, ff), f32),
+            (wide, (d, 2 * ff), bf16),
         ],
-        out_shape=[
-            jax.ShapeDtypeStruct((n, d), bf16),
-            jax.ShapeDtypeStruct((n, d), bf16),
-            jax.ShapeDtypeStruct((1, ff), f32),
-            jax.ShapeDtypeStruct((d, 2 * ff), bf16),
+        [pltpu.VMEM((n, ff), bf16), pltpu.VMEM((n, ff), bf16)],
+        waits,
+        27,
+    )
+
+
+def mlp_first(x, g, weights, bias, waits=(), steps=4):
+    n, d = x.shape
+    ff = bias.shape[1]
+    tok = pl.BlockSpec((n // steps, d), lambda s: (s, 0))
+    hid = pl.BlockSpec((n // steps, ff), lambda s: (s, 0))
+    return mlp_call(
+        mlp_first_body,
+        steps,
+        [tok, tok] + mlp_weights(d, ff, weights),
+        [x, g, *[w for w, _ in weights], bias],
+        [
+            (tok, (n, d), bf16),
+            (tok, (n, d), bf16),
+            (pl.BlockSpec((1, ff), lambda s: (0, 0)), (1, ff), f32),
+            (hid, (n, ff), bf16),
+            (hid, (n, ff), bf16),
         ],
-        scratch_shapes=[
-            pltpu.VMEM((d, ff), bf16),
-            pltpu.VMEM((d, ff), bf16),
-            pltpu.VMEM((n, ff), bf16),
-            pltpu.VMEM((n, ff), bf16),
-            pltpu.SemaphoreType.DMA((2, 8)),
-        ],
-        compiler_params=compiler_params(),
-        cost_estimate=pl.CostEstimate(
-            flops=12 * n * d * ff, bytes_accessed=30 << 20, transcendentals=n * ff
-        ),
-    )(*operands, *waits)
-
-
-def attend_fwd_body(
-    heads, lo_ref, hi_ref, block_ref, x_ref, whole_ref, b_ref, sc_ref, sr_ref, *refs
-):
-    qkv_ref, att_ref, lse_ref, part_ref, w_ref, qt_s, k_s, vt_s, ot_s, m_s, l_s, acc_s, sem = refs[-13:]
-    copies = fetch(whole_ref, block_ref[0], 0, w_ref, sem)
-    for copy in copies:
-        copy.start()
-    for copy in copies:
-        copy.wait()
+        [],
+        waits,
+        19,
+    )
+
+
+def mlp_second(xt, gt, act, slope, init, waits=(), steps=4):
+    d, n = xt.shape
+    ff = act.shape[1]
+    row = pl.BlockSpec((d // steps, n), lambda s: (s, 0))
+    wide = pl.BlockSpec((d // steps, 2 * ff), lambda s: (s, 0))
+    all_hid = pl.BlockSpec((n, ff), lambda s: (0, 0), pipeline_mode=pl.Buffered(1))
+    return mlp_call(
+        mlp_second_body,
+        steps,
+        [row, row, all_hid, all_hid, wide],
+        [xt, gt, act, slope, init],
+        [(wide, (d, 2 * ff), bf16)],
+        [],
+        waits,
+        12,
+    )[0]
+
+
+def attend_fwd_body(heads, lo_ref, hi_ref, x_ref, w_ref, b_ref, sc_ref, sr_ref, *refs):
+    qkv_any, att_ref, lse_ref, part_ref, qt_s, k_s, vt_s, ot_s, qkv_ref, sem = refs[-10:]
     n = x_ref.shape[0]
     e = heads * HD
     c = LOG2E / math.sqrt(HD)
     qkv = dot(x_ref[...], w_ref[:, : 3 * e]) + b_ref[...]
     qkv_ref[...] = qkv.astype(bf16)
+    save = pltpu.make_async_copy(qkv_ref, qkv_any, sem.at[0])
+    save.start()
     qt = qkv[:, :e].T
     vt = qkv[:, 2 * e :].T
-    for h in range(heads):
+    every = range(heads)
+    for h in every:
         qt_s[h] = qt[h * HD : (h + 1) * HD].astype(bf16)
         vt_s[h] = vt[h * HD : (h + 1) * HD].astype(bf16)
         k_s[h] = qkv[:, e + h * HD : e + (h + 1) * HD].astype(bf16)
@@ -566,46 +587,44 @@
     @pl.loop(0, n // QT)
     def _(i):
         qi = pl.ds(pl.multiple_of(i * QT, QT), QT)
-        m_s[...] = jnp.full(m_s.shape, masked_score, f32)
-        l_s[...] = jnp.zeros(l_s.shape, f32)
-        acc_s[...] = jnp.zeros(acc_s.shape, f32)
         seg_row = sr_ref[:1, qi]
-
-        @pl.loop(lo_ref[i], hi_ref[i])
-        def _(j):
-            kj = pl.ds(pl.multiple_of(j * QT, QT), QT)
-            same = sc_ref[kj, :1] == seg_row
-            for h in range(heads):
-                scores = jnp.where(same, dot(k_s[h, kj, :], qt_s[h, :, qi]), masked_score)
-                old = m_s[h]
-                top = jnp.maximum(old, jnp.max(scores, axis=0, keepdims=True))
-                fade = jnp.exp2((old - top) * c)
-                p = jnp.exp2((scores - top) * c)
-                l_s[h] = l_s[h] * fade + jnp.sum(p, axis=0, keepdims=True)
-                acc_s[h] = acc_s[h] * fade + dot(vt_s[h, :, kj], p.astype(bf16))
-                m_s[h] = top
-
-        for h in range(heads):
-            total = l_s[h]
-            ot_s[h * HD : (h + 1) * HD, qi] = acc_s[h] / total
-            lse_ref[h : h + 1, qi] = m_s[h] * c + jnp.log(total) * LOG2E
+        first = lo_ref[i]
+
+        def attend(count):
+            kk = pl.ds(pl.multiple_of(first * QT, QT), count * QT)
+            same = sc_ref[kk, :1] == seg_row
+            scores = [
+                jnp.where(same, dot(k_s[h, kk, :], qt_s[h, :, qi]), masked_score) for h in every
+            ]
+            tops = [jnp.max(v, axis=0, keepdims=True) for v in scores]
+            probs = [jnp.exp2((v - t) * c) for v, t in zip(scores, tops)]
+            totals = [jnp.sum(p, axis=0, keepdims=True) for p in probs]
+            mixed = [dot(vt_s[h, :, kk], probs[h].astype(bf16)) for h in every]
+            for h in every:
+                ot_s[h * HD : (h + 1) * HD, qi] = mixed[h] / totals[h]
+                lse_ref[h : h + 1, qi] = tops[h] * c + jnp.log(totals[h]) * LOG2E
+
+        for count in range(1, n // QT + 1):
+            pl.when(hi_ref[i] - first == count)(lambda count=count: attend(count))
 
     att = ot_s[...].T.astype(bf16)
     att_ref[...] = att
     part_ref[...] = dot(att, w_ref[:, 3 * e :], NT).astype(bf16)
-
-
-def attend_fwd(x, whole, block, bias, lo, hi, seg_col, seg_row, waits=()):
+    save.wait()
+
+
+def attend_fwd(x, w, bias, lo, hi, seg_col, seg_row, waits=()):
     n, d = x.shape
-    e = whole.shape[2] // 4
+    e = bias.shape[1] // 3
     heads = e // HD
     return pl.pallas_call(
         lambda *refs: attend_fwd_body(heads, *refs),
-        in_specs=[SMEM_SPEC] * 3
-        + [VMEM_SPEC, ANY_SPEC]
+        in_specs=[SMEM_SPEC] * 2
+        + [VMEM_SPEC, columns(d, 4 * e, w[1])]
         + [VMEM_SPEC] * 3
         + [ANY_SPEC] * len(waits),
-        out_specs=[VMEM_SPEC] * 4,
+        grid=(1,),
+        out_specs=[ANY_SPEC] + [VMEM_SPEC] * 3,
         out_shape=[
             jax.ShapeDtypeStruct((n, 3 * e), bf16),
             jax.ShapeDtypeStruct((n, e), bf16),
@@ -613,44 +632,45 @@
             jax.ShapeDtypeStruct((n, d), bf16),
         ],
         scratch_shapes=[
-            pltpu.VMEM((d, 4 * e), bf16),
             pltpu.VMEM((heads, HD, n), bf16),
             pltpu.VMEM((heads, n, HD), bf16),
             pltpu.VMEM((heads, HD, n), bf16),
             pltpu.VMEM((e, n), f32),
-            pltpu.VMEM((heads, 1, QT), f32),
-            pltpu.VMEM((heads, 1, QT), f32),
-            pltpu.VMEM((heads, HD, QT), f32),
-            pltpu.SemaphoreType.DMA((8,)),
+            pltpu.VMEM((n, 3 * e), bf16),
+            pltpu.SemaphoreType.DMA((1,)),
         ],
         compiler_params=compiler_params(),
-        cost_estimate=pl.CostEstimate(
-            flops=8 * n * d * e * 3, bytes_accessed=12 << 20, transcendentals=heads * n * n
-        ),
-    )(lo, hi, block, x, whole, bias, seg_col, seg_row, *waits)
-
-
-def attend_bwd_body(final, waits, heads, *refs):
-    (lo_ref, hi_ref, block_ref, place_ref, qkv_ref, att_ref, g_ref, gt_ref, xt_ref, whole_ref, lse_ref, sc_ref, sr_ref) = refs[:13]
-    init_ref = refs[13] if final else None
-    refs = refs[13 + final + waits :]
+        cost_estimate=cost(16),
+    )(lo, hi, x, w[0], bias, seg_col, seg_row, *waits)
+
+
+def attend_bwd_body(final, parts, waits, heads, *refs):
+    (lo_ref, hi_ref, place_ref, qkv_ref, att_ref, g_ref, gt_any, xt_any, w_ref, lse_ref, sc_ref, sr_ref) = refs[:12]
+    init_any = refs[12] if final else None
+    refs = refs[12 + final + waits :]
+    grads_any, db_ref = refs[:2]
+    refs = refs[2:]
+    if parts:
+        count = 2 * len(parts)
+        outs, (stage, sem), refs = refs[:count], refs[-2:], refs[count:-2]
+    else:
+        stage, refs = refs[0], refs[1:]
     if final:
-        dx_ref, db_ref = refs[:2]
-        outs, (stage, sem) = refs[2:4], refs[-2:]
-        refs = refs[4:-2]
-    else:
-        dx_ref, db_ref, stage = refs[:3]
-        refs = refs[3:]
-    qt_s, q_s, k_s, kt_s, v_s, do_s, dot_s, delta_s, dqt_s, dk_s, dv_s, w_ref, w_sem = refs
-    copies = fetch(whole_ref, block_ref[0], 0, w_ref, w_sem)
-    for copy in copies:
-        copy.start()
-    for copy in copies:
-        copy.wait()
+        init_ref, refs = refs[-1], refs[:-1]
+    qt_s, q_s, k_s, kt_s, v_s, do_s, dot_s, delta_s, dqt_s, dk_s, dv_s, xt_ref, gt_ref, grads_ref, own_sem = refs
+    loads = [
+        pltpu.make_async_copy(xt_any, xt_ref, own_sem.at[0]),
+        pltpu.make_async_copy(gt_any, gt_ref, own_sem.at[1]),
+    ]
+    if final:
+        loads.append(pltpu.make_async_copy(init_any, init_ref, own_sem.at[2]))
+    for load in loads:
+        load.start()
     n = g_ref.shape[0]
     e = heads * HD
     c = LOG2E / math.sqrt(HD)
     scale = 1.0 / math.sqrt(HD)
+    every = range(heads)
     out_grad = dot(g_ref[...], w_ref[:, 3 * e :]).astype(bf16).astype(f32)
     out_grad_t = out_grad.T
     qkv = qkv_ref[...].astype(f32)
@@ -658,7 +678,7 @@
     kt = qkv[:, e : 2 * e].T
     att = att_ref[...]
     products = out_grad_t * att.astype(f32).T
-    for h in range(heads):
+    for h in every:
         s = slice(h * HD, (h + 1) * HD)
         qt_s[h] = qt[s].astype(bf16)
         kt_s[h] = kt[s].astype(bf16)
@@ -668,80 +688,94 @@
         k_s[h] = qkv[:, e + h * HD : e + (h + 1) * HD].astype(bf16)
         v_s[h] = qkv[:, 2 * e + h * HD : 2 * e + (h + 1) * HD].astype(bf16)
         do_s[h] = out_grad[:, s].astype(bf16)
-    dqt_s[...] = jnp.zeros(dqt_s.shape, f32)
     dk_s[...] = jnp.zeros(dk_s.shape, f32)
     dv_s[...] = jnp.zeros(dv_s.shape, f32)
 
     @pl.loop(0, n // QT)
-    def _(j):
-        kj = pl.ds(pl.multiple_of(j * QT, QT), QT)
-        seg_col = sc_ref[kj, :1]
-
-        @pl.loop(lo_ref[j], hi_ref[j])
-        def _(i):
-            qi = pl.ds(pl.multiple_of(i * QT, QT), QT)
-            same = seg_col == sr_ref[:1, qi]
-            for h in range(heads):
-                scores = dot(k_s[h, kj, :], qt_s[h, :, qi])
-                p = jnp.where(same, jnp.exp2(scores * c - lse_ref[h : h + 1, qi]), 0.0)
-                p_grad = dot(v_s[h, kj, :], dot_s[h, :, qi])
-                s_grad = (p * (p_grad - delta_s[h, :, qi])).astype(bf16)
-                dv_s[h, kj, :] += dot(p.astype(bf16), do_s[h, qi, :])
-                dk_s[h, kj, :] += dot(s_grad, q_s[h, qi, :])
-                dqt_s[h, :, qi] += dot(kt_s[h, :, kj], s_grad)
-
-    dq = jnp.concatenate([dqt_s[h] for h in range(heads)], axis=0).T * scale
-    dk = [dk_s[h] * scale for h in range(heads)]
-    dv = [dv_s[h] for h in range(heads)]
+    def _(i):
+        qi = pl.ds(pl.multiple_of(i * QT, QT), QT)
+        seg_row = sr_ref[:1, qi]
+        first = lo_ref[i]
+
+        def attend(count):
+            kk = pl.ds(pl.multiple_of(first * QT, QT), count * QT)
+            same = sc_ref[kk, :1] == seg_row
+            scores = [dot(k_s[h, kk, :], qt_s[h, :, qi]) for h in every]
+            p_grads = [dot(v_s[h, kk, :], dot_s[h, :, qi]) for h in every]
+            probs = [
+                jnp.where(same, jnp.exp2(scores[h] * c - lse_ref[h : h + 1, qi]), 0.0) for h in every
+            ]
+            s_grads = [(probs[h] * (p_grads[h] - delta_s[h, :, qi])).astype(bf16) for h in every]
+            dv = [dot(probs[h].astype(bf16), do_s[h, qi, :]) for h in every]
+            dk = [dot(s_grads[h], q_s[h, qi, :]) for h in every]
+            dq = [dot(kt_s[h, :, kk], s_grads[h]) for h in every]
+            for h in every:
+                dv_s[h, kk, :] += dv[h]
+                dk_s[h, kk, :] += dk[h]
+                dqt_s[h, :, qi] = dq[h]
+
+        for count in range(1, n // QT + 1):
+            pl.when(hi_ref[i] - first == count)(lambda count=count: attend(count))
+
+    dq = jnp.concatenate([dqt_s[h] for h in every], axis=0).T * scale
+    dk = [dk_s[h] * scale for h in every]
+    dv = [dv_s[h] for h in every]
     grads = jnp.concatenate([dq] + dk + dv, axis=1).astype(bf16)
     db_ref[...] = jnp.sum(grads.astype(f32), axis=0, keepdims=True)
-    dx_ref[...] = dot(grads, w_ref[:, : 3 * e], NT).astype(bf16)
+    grads_ref[...] = grads
+    save = pltpu.make_async_copy(grads_ref, grads_any, own_sem.at[3])
+    save.start()
+    for load in loads:
+        load.wait()
     dw = jnp.concatenate([dot(xt_ref[...], grads), dot(gt_ref[...], att)], axis=1)
-    if not final:
-        stage[...] = dw.astype(bf16)
-    else:
-        stage[...] = (dw + init_ref[...].astype(f32)).astype(bf16)
-        send_pieces(stage, place_ref, 0, 8, outs, sem)
-        wait_pieces(stage, 8, outs, sem)
+    if final:
+        dw += init_ref[...].astype(f32)
+    stage[...] = dw.astype(bf16)
+    if parts:
+        piece_copies(stage, place_ref, parts, outs, sem, True)
+        piece_copies(stage, place_ref, parts, outs, sem, False)
+    save.wait()
 
 
 def attend_bwd(
-    qkv, att, g, gt, xt, whole, block, lse, lo, hi, seg_col, seg_row, place, init=None, waits=()
+    qkv, att, g, gt, xt, w, lse, lo, hi, seg_col, seg_row, place, init=None, parts=(), waits=()
 ):
     n, d = g.shape
-    e = whole.shape[2] // 4
+    e = att.shape[1]
     heads = e // HD
     final = init is not None
-    operands = [lo, hi, block, place, qkv, att, g, gt, xt, whole, lse, seg_col, seg_row]
-    in_specs = [SMEM_SPEC] * 4 + [VMEM_SPEC] * 5 + [ANY_SPEC] + [VMEM_SPEC] * 3
-    out_shape = [jax.ShapeDtypeStruct((n, d), bf16), jax.ShapeDtypeStruct((1, 3 * e), f32)]
-    out_specs = [VMEM_SPEC, VMEM_SPEC]
+    operands = [lo, hi, place, qkv, att, g, gt, xt, w[0], lse, seg_col, seg_row]
+    in_specs = [SMEM_SPEC] * 3 + [VMEM_SPEC] * 3 + [ANY_SPEC] * 2
+    in_specs += [columns(d, 4 * e, w[1])] + [VMEM_SPEC] * 3
+    out_shape = [jax.ShapeDtypeStruct((n, 3 * e), bf16), jax.ShapeDtypeStruct((1, 3 * e), f32)]
+    out_specs = [ANY_SPEC, VMEM_SPEC]
     tall, wide = (heads, n, HD), (heads, HD, n)
     scratch = [pltpu.VMEM(s, bf16) for s in (wide, tall, tall, wide, tall, tall, wide)]
     scratch += [pltpu.VMEM((heads, 1, n), f32)] + [pltpu.VMEM(s, f32) for s in (wide, tall, tall)]
-    scratch += [pltpu.VMEM((d, 4 * e), bf16), pltpu.SemaphoreType.DMA((8,))]
+    scratch += [pltpu.VMEM(s, bf16) for s in ((d, n), (d, n), (n, 3 * e))]
+    scratch += [pltpu.SemaphoreType.DMA((4,))]
     if final:
         operands.append(init)
-        in_specs.append(VMEM_SPEC)
-        out_shape += [jax.ShapeDtypeStruct((4, ROWS, 4 * e), bf16)] * 2
+        in_specs.append(ANY_SPEC)
+        scratch.append(pltpu.VMEM((d, 4 * e), bf16))
+    for width in parts:
+        out_shape += [jax.ShapeDtypeStruct((4, ROWS, width), bf16)] * 2
         out_specs += [ANY_SPEC] * 2
-        scratch += [pltpu.VMEM((d, 4 * e), bf16), pltpu.SemaphoreType.DMA((8,))]
+    if parts:
+        scratch += [pltpu.VMEM((d, 4 * e), bf16), pltpu.SemaphoreType.DMA((8 * len(parts),))]
     else:
         out_shape.append(jax.ShapeDtypeStruct((d, 4 * e), bf16))
         out_specs.append(VMEM_SPEC)
-    in_specs += [ANY_SPEC] * len(waits)
-    operands += waits
     return pl.pallas_call(
-        lambda *refs: attend_bwd_body(final, len(waits), heads, *refs),
-        in_specs=in_specs,
+        lambda *refs: attend_bwd_body(final, parts, len(waits), heads, *refs),
+        grid=(1,),
+        in_specs=in_specs + [ANY_SPEC] * len(waits),
         out_specs=out_specs,
         out_shape=out_shape,
         scratch_shapes=scratch,
         compiler_params=compiler_params(),
-        cost_estimate=pl.CostEstimate(
-            flops=16 * n * d * e * 3, bytes_accessed=20 << 20, transcendentals=heads * n * n
-        ),
-    )(*operands)
+        cost_estimate=cost(7),
+    )(*operands, *waits)
 
 
 def token_rows(mod_ref, block, sc_ref):
@@ -794,11 +828,14 @@
         acc_ref[...] += part
 
 
-def enter_body(x_ref, g_ref, mod_ref, sc_ref, a_ref, at_ref, bg_ref, bgt_ref, sum_ref):
+def enter_body(x_ref, mod_ref, sc_ref, a_ref, at_ref):
     normed, _ = normalize(x_ref[...].astype(f32))
     a = normed * (1.0 + token_rows(mod_ref, 1, sc_ref)) + token_rows(mod_ref, 0, sc_ref)
     a_ref[...] = a.astype(bf16)
     at_ref[...] = a.T.astype(bf16)
+
+
+def branch_body(g_ref, mod_ref, sc_ref, bg_ref, bgt_ref, sum_ref):
     bg = token_rows(mod_ref, 5, sc_ref) * g_ref[...].astype(f32)
     bg_ref[...] = bg.astype(bf16)
     bgt_ref[...] = bg.T.astype(bf16)
@@ -839,15 +876,40 @@
     )
 
 
-def leave_body(first_ref, last_ref, x_ref, hg_ref, d0, d1, d2, d3, mod_ref, sc_ref, out_ref, img_ref):
-    a_grad = d0[...].astype(f32) + d1[...].astype(f32) + d2[...].astype(f32) + d3[...].astype(f32)
+def back_body(q0, q1, q2, q3, w0, w1, w2, w3, *refs):
+    out_ref = refs[-1]
+    width = q0.shape[1]
+    total = dot(q0[...], w0[:, :width], NT)
+    for grads, w in ((q1, w1), (q2, w2), (q3, w3)):
+        total += dot(grads[...], w[:, :width], NT)
+    out_ref[...] = total
+
+
+def back_to_input(grads, weights, waits, steps=4):
+    n, width = grads[0].shape
+    d = weights[0][0].shape[0]
+    return pl.pallas_call(
+        back_body,
+        grid=(steps,),
+        in_specs=[pl.BlockSpec((n // steps, width), lambda s: (s, 0))] * 4
+        + [columns(d, width * 4 // 3, block) for _, block in weights]
+        + [ANY_SPEC] * len(waits),
+        out_specs=pl.BlockSpec((n // steps, d), lambda s: (s, 0)),
+        out_shape=jax.ShapeDtypeStruct((n, d), f32),
+        compiler_params=compiler_params(),
+        cost_estimate=cost(17),
+    )(*grads, *[w for w, _ in weights], *waits)
+
+
+def leave_body(first_ref, last_ref, x_ref, hg_ref, ag_ref, mod_ref, sc_ref, out_ref, img_ref):
+    a_grad = ag_ref[...]
     normed, inverse = normalize(x_ref[...].astype(f32))
     back = norm_back(normed, inverse, a_grad * (1.0 + token_rows(mod_ref, 1, sc_ref)))
     out_ref[...] = (hg_ref[...] + back).astype(bf16)
     add_images(img_ref, first_ref, last_ref, sc_ref, (a_grad, a_grad * normed))
 
 
-def by_rows(body_fn, scalars, operands, outs, waits=(), carried=()):
+def by_rows(body_fn, micros, scalars, operands, outs, waits=()):
     def spec(kind, shape):
         if kind == "t":
             return pl.BlockSpec((ET, shape[1]), lambda s: (s, 0))
@@ -856,36 +918,35 @@
         return pl.BlockSpec(shape, lambda s: (0, 0))
 
     n = operands[0][1].shape[0]
-    own_in, own_out = len(scalars) + len(operands), len(outs)
-    idle = len(waits) + len(carried)
+    own_in = len(scalars) + len(operands)
 
     def body(*refs):
-        body_fn(*refs[:own_in], *refs[own_in + idle : own_in + idle + own_out])
+        body_fn(*refs[:own_in], *refs[own_in + len(waits) :])
 
     return pl.pallas_call(
         body,
         grid=(n // ET,),
         in_specs=[SMEM_SPEC] * len(scalars)
         + [spec(k, v.shape) for k, v in operands]
-        + [ANY_SPEC] * idle,
-        out_specs=[spec(k, s) for k, s, _ in outs] + [ANY_SPEC] * len(carried),
-        out_shape=[jax.ShapeDtypeStruct(s, t) for _, s, t in outs]
-        + [jax.ShapeDtypeStruct(v.shape, v.dtype) for v in carried],
-        input_output_aliases={
-            own_in + len(waits) + i: own_out + i for i in range(len(carried))
-        },
+        + [ANY_SPEC] * len(waits),
+        out_specs=[spec(k, s) for k, s, _ in outs],
+        out_shape=[jax.ShapeDtypeStruct(s, t) for _, s, t in outs],
         compiler_params=compiler_params(),
-        cost_estimate=pl.CostEstimate(
-            flops=100 * n * 1152, bytes_accessed=24 << 20, transcendentals=n
-        ),
-    )(*scalars, *[v for _, v in operands], *waits, *carried)
-
-
-def trade_rows(values, core):
-    own = lax.dynamic_index_in_dim(values, core, 0, keepdims=False)
-    got = across(lax.dynamic_index_in_dim(values, 1 - core, 0, keepdims=False), CORE)
-    first = core == 0
-    return jnp.concatenate([jnp.where(first, own, got), jnp.where(first, got, own)])
+        cost_estimate=cost(micros),
+    )(*scalars, *[v for _, v in operands], *waits)
+
+
+class Row:
+    def __init__(self, values, core):
+        self.core = core
+        self.own = lax.dynamic_index_in_dim(values, core, 0, keepdims=False)
+        self.got = across(lax.dynamic_index_in_dim(values, 1 - core, 0, keepdims=False), CORE)
+
+    def whole(self):
+        first = self.core == 0
+        return jnp.concatenate(
+            [jnp.where(first, self.own, self.got), jnp.where(first, self.got, self.own)]
+        )
 
 
 def trade_back(row, core):
@@ -913,12 +974,27 @@
         return add_pieces(self.low, *self.got)
 
 
-def gather_all(values, dp_rank, tp_rank):
-    order = dp_rank * 4 + tp_rank + jnp.zeros((1,), jnp.int32)
-    for dp_mask, tp_mask in ((1, 0), (2, 0), (6, 0), (0, CHIP), (0, CORE)):
-        values = jnp.concatenate([values, swap(values, dp_mask, tp_mask)])
-        order = jnp.concatenate([order, order ^ (dp_mask * 4 + tp_mask)])
-    return values, order
+def lanes(values, rows):
+    values = values.reshape(rows, -1)
+    spare = -values.shape[1] % 128
+    return jnp.pad(values.astype(bf16), ((0, 0), (0, spare))).reshape(rows, -1, 128)
+
+
+def to_owners(grads, pieces, sums):
+    count, width = grads.shape
+    grads = lanes(grads.reshape(count, 4, width // 4).transpose(1, 0, 2), 4)
+    parts = [jnp.concatenate([grads] * 8)]
+    if pieces is not None:
+        parts.append(lanes(pieces, 32))
+    if sums:
+        sums = lanes(jnp.concatenate(sums, axis=1), 1)
+        parts.append(jnp.broadcast_to(sums, (32,) + sums.shape[1:]))
+    return lax.all_to_all(jnp.concatenate(parts, axis=1), AXES, 0, 0, tiled=True)
+
+
+def taken_apart(got, count, width):
+    rows = count * width // 128
+    return got[:, :rows].reshape(32 * count, width), got[:, rows:].reshape(32, -1)
 
 
 def row_body(
@@ -943,13 +1019,11 @@
     e, ff, mod_dev = w_qkv.shape[2], w_fc1.shape[1], w_ada.shape[1]
     flips = jnp.arange(8, dtype=jnp.int32) ^ dp_rank
     place = (flips & 1) * 4 + (flips >> 1)
-    blocks = [(tp_rank ^ k).reshape(1) for k in range(4)]
     att_shard = jnp.concatenate([w_qkv[0], w_qkv[1], w_qkv[2], w_out.T], axis=1)
     mlp_shard = jnp.concatenate([w_fc1, w_fc2.T], axis=1)
-    att_w = lax.all_gather(att_shard, AXES)
-    mlp_w = lax.all_gather(mlp_shard, AXES)
-    x = trade_rows(block_input, core)
-    g = trade_rows(cotangent, core)
+    near_att = lax.all_gather(att_shard, "dp", axis=0, tiled=True)
+    x = Row(block_input, core).whole()
+    g_row = Row(cotangent, core)
     seg = lax.dynamic_slice(segment_ids, (core, chip * PACK), (1, PACK))[0]
     seg_col = jnp.broadcast_to(seg[:, None], (PACK, 128))
     seg_row = jnp.broadcast_to(seg[None, :], (8, PACK))
@@ -962,30 +1036,55 @@
     lifted = lax.all_to_all(lifted.transpose(1, 0, 2), "dp", 0, 0)
     lifted = lifted.reshape(8, 2, 2, IMG_ROW, -1).transpose(0, 2, 1, 3, 4).reshape(32 * IMG_ROW, -1)
     mod_part = dot(lifted, w_ada).reshape(32, IMG_ROW, mod_dev)
-    mod_part = lax.all_to_all(mod_part, AXES, 0, 0).reshape(8, 4, IMG_ROW, mod_dev)
+    (mlp_shard,) = tie([mlp_shard], (mod_part,))
+    peer_shard = across(mlp_shard, CHIP)
+    (mod_part,) = tie([lax.all_to_all(mod_part, AXES, 0, 0)], (x,))
+    mod_part = mod_part.reshape(8, 4, IMG_ROW, mod_dev)
     modulation = jnp.sum(mod_part, axis=0).transpose(1, 0, 2).reshape(IMG_ROW, -1)
     modulation = modulation + ada_bias.astype(f32)
+    (peer_shard,) = tie([peer_shard], (modulation,))
+    far_w = lax.all_gather(peer_shard, "dp", axis=0, tiled=True)
+    near_w = lax.all_gather(mlp_shard, "dp", axis=0, tiled=True)
     row_f, row_b = ((PACK, d), f32), ((PACK, d), bf16)
     turned = ((d, PACK), bf16)
-    a, a_t, bg2, bg2_t, fc2_sum = by_rows(
+    a, a_t = by_rows(
         enter_body,
+        6,
         (),
-        [("t", x), ("t", g), ("w", modulation), ("t", seg_col)],
-        [("t", *row_b), ("T", *turned), ("t", *row_b), ("T", *turned), ("w", (1, d), f32)],
+        [("t", x), ("w", modulation), ("t", seg_col)],
+        [("t", *row_b), ("T", *turned)],
+        waits=(peer_shard,),
     )
     qkv_bias = jnp.stack([qv_bias[0], jnp.zeros_like(qv_bias[0]), qv_bias[1]]).astype(f32)
     kept = {}
 
     def forward(k, waits):
         bias = lax.dynamic_slice_in_dim(qkv_bias, (tp_rank ^ k) * e, e, 1).reshape(1, 3 * e)
-        kept[k] = attend_fwd(a, att_w, blocks[k], bias, lo, hi, seg_col, seg_row, waits)
+        kept[k] = attend_fwd(a, att_w[k], bias, lo, hi, seg_col, seg_row, waits)
         return (kept[k][2],)
 
-    after = ()
-    for k in range(4):
-        after = forward(k, after)
+    (near_att,) = tie([near_att], (a,))
+    att_w = [(v, 0) for v in (near_att, across(near_att, CORE), across(near_att, CHIP))]
+    after = forward(1, forward(0, ()))
+    (g_row.got,) = tie([g_row.got], after)
+    g = g_row.whole()
+    bg2, bg2_t, fc2_sum = by_rows(
+        branch_body,
+        6,
+        (),
+        [("t", g), ("w", modulation), ("t", seg_col)],
+        [("t", *row_b), ("T", *turned), ("w", (1, d), f32)],
+        waits=after,
+    )
+    (far_att,) = tie([att_w[2][0]], (fc2_sum,))
+    att_w[2:] = [(far_att, 0), (across(far_att, CORE), 0)]
+    after = forward(2, after)
+    (far_w,) = tie([far_w], after)
+    after = forward(3, after + (far_w,))
+    partner_w = across(far_w, CORE)
     hidden, branch1, m, m_t = by_rows(
         middle_body,
+        12,
         (),
         [("t", x)]
         + [("t", kept[k][3]) for k in range(4)]
@@ -995,43 +1094,48 @@
     done = {}
     fc1_f = fc1_bias.astype(f32)[None]
 
-    def feed_forward(k, init, waits):
-        bias = lax.dynamic_slice_in_dim(fc1_f, (tp_rank ^ k) * ff, ff, 1)
-        done[k] = mlp_block(m, bg2, m_t, bg2_t, mlp_w, blocks[k], bias, init, waits)
-        return (done[k][2],)
-
-    after = feed_forward(1, None, ())
+    def fc1_part(k):
+        return lax.dynamic_slice_in_dim(fc1_f, (tp_rank ^ k) * ff, ff, 1)
+
+    def halves(w):
+        return ((w, 0), (w, 1))
+
+    done[3] = mlp_whole(m, bg2, m_t, bg2_t, halves(partner_w), fc1_part(3))
+    init = across(done[3][3], CORE)
+    done[2] = mlp_first(m, bg2, halves(far_w), fc1_part(2), (done[3][2],))
+    (near_w,) = tie([near_w], (done[2][2],))
+    partner_w = across(near_w, CORE)
+    grad = mlp_second(m_t, bg2_t, *done[2][3:], init, (near_w,))
+    far_sum = lax.psum_scatter(grad, "dp", scatter_dimension=0, tiled=True)
+    done[1] = mlp_whole(m, bg2, m_t, bg2_t, halves(partner_w), fc1_part(1), (grad,))
     init = across(done[1][3], CORE)
-    after = feed_forward(3, None, after)
-    after = feed_forward(0, init, after)
-    init = across(done[3][3], CORE)
-    mlp_sum = {0: lax.psum_scatter(done[0][3], "dp", scatter_dimension=0, tiled=True)}
-    after = feed_forward(2, init, after)
-    mlp_sum[2] = lax.psum_scatter(done[2][3], "dp", scatter_dimension=0, tiled=True)
+    done[0] = mlp_first(m, bg2, halves(near_w), fc1_part(0), (done[1][2],))
+    grad = mlp_second(m_t, bg2_t, *done[0][3:], init)
+    near_sum = lax.psum_scatter(grad, "dp", scatter_dimension=0, tiled=True)
     block_output, hidden_grad, bg1, bg1_t, out_sum, img_late = by_rows(
         turn_body,
+        5,
         (first, last),
         [("t", hidden), ("t", branch1), ("t", g)]
         + [("t", done[k][0]) for k in range(4)]
         + [("t", done[k][1]) for k in range(4)]
         + [("w", modulation), ("t", seg_col), ("w", fc2_bias.astype(f32)[None])],
         [("t", *row_b), ("t", *row_f), ("t", *row_b), ("T", *turned), ("w", (1, d), f32), ("w", (IMG_ROW, 4 * d), f32)],
-        waits=after,
+        waits=(grad,),
     )
     fc1_sum = jnp.zeros((1, 4 * ff), f32)
     for k in range(4):
         fc1_sum = lax.dynamic_update_slice_in_dim(fc1_sum, done[k][2], (tp_rank ^ k) * ff, 1)
     late = jnp.concatenate([jnp.zeros((IMG_ROW, 2 * d), f32), img_late], axis=1)
-    late = late.reshape(IMG_ROW, 4, mod_dev).transpose(1, 0, 2).reshape(4, IMG_ROW * mod_dev)
-    sums = jnp.concatenate([jnp.sum(img_late, axis=0, keepdims=True), fc1_sum, fc2_sum, out_sum], axis=1)
-    late = jnp.concatenate([late, jnp.broadcast_to(sums, (4, sums.shape[1]))], axis=1)
-    late = lax.all_to_all(jnp.concatenate([late] * 8), AXES, 0, 0, tiled=True)
+    late_sums = [jnp.sum(img_late, axis=0, keepdims=True), fc1_sum, fc2_sum, out_sum]
+    late_sums = jnp.concatenate(late_sums, axis=1).reshape(32, -1)
+    late = to_owners(late, late_sums, [])
     back = {}
 
-    def backward(k, init, waits):
+    def backward(k, init, waits, parts=()):
         qkv, att, lse, _ = kept[k]
         back[k] = attend_bwd(
-            qkv, att, bg1, bg1_t, a_t, att_w, blocks[k], lse, lo, hi, seg_col, seg_row, place, init, waits
+            qkv, att, bg1, bg1_t, a_t, att_w[k], lse, lo, hi, seg_col, seg_row, place, init, parts, waits
         )
         return (back[k][1],)
 
@@ -1039,52 +1143,59 @@
     after = backward(1, None, ())
     init = across(back[1][2], CORE)
     (block_output,) = tie([block_output], after)
-    after = backward(3, None, after + (block_output,))
+    after = backward(3, None, after + (block_output, far_sum))
+    init, last_init = across(back[3][2], CORE), init
+    after = backward(2, init, after, (4 * e,))
     (late,) = tie([late], after)
-    after = backward(0, init, after + (late,))
-    init = across(back[3][2], CORE)
-    near = Scatter(*back[0][2:])
-    after = backward(2, init, after + (mlp_sum[0],))
-    (near.got,) = tie([near.got], after)
-    near.turn()
+    late_grads, late_sums = taken_apart(late, IMG_ROW, mod_dev)
     far = Scatter(*back[2][2:])
+    far_peer = across(far_sum, CHIP)
+    after = backward(0, last_init, after)
+    near_att = lax.psum_scatter(back[0][2], "dp", scatter_dimension=0, tiled=True)
+    far.got, far_peer = tie([far.got, far_peer], after)
+    far.turn()
+    a_grad = back_to_input([back[k][0] for k in range(4)], att_w, (far.low, near_sum))
+    far.got = tie(far.got, (a_grad,))
+    far_att = across(far.total().astype(bf16), CHIP)
     input_grad, img_early = by_rows(
         leave_body,
+        11,
         (first, last),
-        [("t", x), ("t", hidden_grad)]
-        + [("t", back[k][0]) for k in range(4)]
-        + [("w", modulation), ("t", seg_col)],
+        [("t", x), ("t", hidden_grad), ("t", a_grad), ("w", modulation), ("t", seg_col)],
         [("t", *row_b), ("w", (IMG_ROW, 2 * d), f32)],
-        waits=(near.low,),
-    )
-    mlp_total = mlp_sum[0].astype(f32) + across(mlp_sum[2], CHIP).astype(f32)
-    far.got, *near.got = tie([far.got] + near.got, (img_early,))
-    far.turn()
-    att_total = near.total() + across(far.total().astype(bf16), CHIP).astype(f32)
+    )
+    (far_att,) = tie([far_att], (img_early,))
+    att_total = near_att.astype(f32) + far_att.astype(f32)
+    near_sum = near_sum.astype(f32)
+    fc1_grad = near_sum[:, :ff]
+    fc2_grad = near_sum[:, ff:]
+    far_peer = far_peer.astype(f32)
+    fc1_grad, fc2_grad = fc1_grad + far_peer[:, :ff], fc2_grad + far_peer[:, ff:]
     qv_sum = jnp.zeros((2, 4 * e), f32)
     for k in range(4):
         grads = back[k][1].reshape(3, e)
         qv_sum = lax.dynamic_update_slice_in_dim(
             qv_sum, jnp.stack([grads[0], grads[2]]), (tp_rank ^ k) * e, 1
         )
-    all_b = jnp.concatenate([img_early.reshape(1, -1), qv_sum.reshape(1, -1)], axis=1)
-    all_b, order = gather_all(all_b, dp_rank, tp_rank)
-    early = 2 * d * IMG_ROW
-    own = IMG_ROW * mod_dev
+    early = jnp.concatenate([img_early, jnp.zeros((IMG_ROW, 4 * d), f32)], axis=1)
+    late_sums = jnp.sum(late_sums.astype(f32), axis=0, keepdims=True)
+    early_sums = [late_sums, jnp.sum(img_early, axis=0, keepdims=True), qv_sum.reshape(1, -1)]
+    early = to_owners(early, None, early_sums)
+    early_grads, early_sums = taken_apart(early, IMG_ROW, mod_dev)
+    share = late_sums.shape[1]
+    used = (5 * d + d + 4 * ff) // 32
+    late_sums = early_sums[:, :used].astype(f32).reshape(-1)
     late_bias, fc1_total, fc2_total, out_total = jnp.split(
-        jnp.sum(late[:, own:], axis=0), [4 * d, 4 * d + 4 * ff, 5 * d + 4 * ff]
-    )
-    qv_total = jnp.sum(all_b[:, early:], axis=0).reshape(2, -1)
-    all_b = all_b[:, :early].reshape(32 * IMG_ROW, 2 * d)
-    ada_total = jnp.concatenate([jnp.sum(all_b, axis=0), late_bias])
-    grad_b = lax.dynamic_slice_in_dim(
-        jnp.pad(all_b, ((0, 0), (0, 4 * d))), tp_rank * mod_dev, mod_dev, 1
-    )
-    lifted = lifted.astype(f32)
-    lifted_b = jnp.take(lifted.reshape(32, -1), order, axis=0).reshape(lifted.shape)
-    ada_grad = jnp.zeros((), f32)
-    for rows, grad in ((lifted, late[:, :own].reshape(32 * IMG_ROW, mod_dev)), (lifted_b, grad_b)):
-        ada_grad += lax.dot_general(rows, grad, (((0,), (0,)), ((), ())), precision=highest)
+        late_sums, [4 * d, 4 * d + 4 * ff, 5 * d + 4 * ff]
+    )
+    early_sums = jnp.sum(early_sums[:, share : share + 2 * d + 8 * e].astype(f32), axis=0)
+    early_bias, qv_total = jnp.split(early_sums, [2 * d])
+    qv_total = qv_total.reshape(2, -1)
+    ada_total = jnp.concatenate([early_bias, late_bias])
+    mod_grad = late_grads.astype(f32) + early_grads.astype(f32)
+    ada_grad = lax.dot_general(
+        lifted.astype(f32), mod_grad, (((0,), (0,)), ((), ())), precision=highest
+    )
     return (
         block_output,
         trade_back(input_grad, core),
@@ -1092,9 +1203,9 @@
         qv_total,
         att_total[:, 3 * e :].T,
         out_total,
-        mlp_total[:, :ff],
+        fc1_grad,
         fc1_total,
-        mlp_total[:, ff:].T,
+        fc2_grad.T,
         fc2_total,
         ada_grad,
         ada_total,

time: 729 us -> 624 us (0.86)
  waiting for transfers between devices: 179 us -> 131 us
  Pallas kernels: 385 us -> 346 us
  starting transfers between devices: 51.8 us -> 29.4 us
  blocking collectives: 0 us -> 13.7 us
  local copies, waits for them, and re-layouts: 57.4 us -> 47.9 us
    all_gather x2 -> x3, waiting for transfers between devices: 62.7 us -> 7.77 us  [the longest x1 7.75 us: row_body(): near_w = lax.all_gather(mlp_shard, 'dp', axis=0, tiled=True)]
    reduce_scatter x2 -> x3, waiting for transfers between devices: 0.01 us -> 48.5 us  [the longest x1 37.6 us: row_body(): near_sum = lax.psum_scatter(grad, 'dp', scatter_dimension=0, tiled=True)]
    ppermute x23 -> x20, waiting for transfers between devices: 74.5 us -> 27.6 us  [swap(): return lax.ppermute(values, AXES, pairs)]
    pallas_call x4, Pallas kernels: 88 us -> 57.2 us  [attend_fwd(): pl.pallas_call(lambda *refs: attend_fwd_body(heads, *refs), in_specs=[SME...]
    ppermute x23 -> x20, starting transfers between devices: 35.3 us -> 16.6 us  [swap(): return lax.ppermute(values, AXES, pairs)]
    all_to_all x0 -> x1, blocking collectives: none -> 13.7 us  [row_body(): lifted = lax.all_to_all(lifted.transpose(1, 0, 2), 'dp', 0, 0)]
    pallas_call x8 -> x11, Pallas kernels: 239 us -> 228 us  [the longest x6 117 us: mlp_call(): pl.pallas_call(lambda *refs: body(len(waits), *refs), grid=(steps,), in_s...]
    unnamed x56 -> x107, local copies, waits for them, and re-layouts: 9.43 us -> 15.7 us
  transfers between devices with their start and end apart: 30 -> 29, of which waited for: 15 -> 7; matrix products, arithmetic and copies ran while one was open for 10% -> 10% of each run, Pallas kernels for 49% -> 56%
where the time goes in v2:
time: 624 us; the launch traced here: 618 us
  Pallas kernels  346 us (55%)
  waiting for transfers between devices  131 us (21%)
  local copies, waits for them, and re-layouts  47.9 us (8%)
  other arithmetic  32.4 us (5%)
  starting transfers between devices  29.4 us (5%)
  between operations  15.4 us (2%)
  blocking collectives  13.7 us (2%)
    pallas_call x6, Pallas kernels, mlp_call(): pl.pallas_call(lambda *refs: body(len(waits), *refs), grid=(steps,), in_s...  117 us
    pallas_call x4, Pallas kernels, attend_bwd(): pl.pallas_call(lambda *refs: attend_bwd_body(final, parts, len(waits), he...  93.7 us
    pallas_call x5, Pallas kernels, by_rows(): pl.pallas_call(body, grid=(n // ET,), in_specs=[SMEM_SPEC] * len(scalars)...  61.1 us
    pallas_call x4, Pallas kernels, attend_fwd(): pl.pallas_call(lambda *refs: attend_fwd_body(heads, *refs), in_specs=[SME...  57.2 us
    reduce_scatter x1, waiting for transfers between devices, row_body(): near_sum = lax.psum_scatter(grad, 'dp', scatter_dimension=0, tiled=True)  37.6 us
    all_to_all x1, waiting for transfers between devices, row_body(): mod_part, = tie([lax.all_to_all(mod_part, AXES, 0, 0)], (x,))  33.5 us
    ppermute x20, waiting for transfers between devices, swap(): return lax.ppermute(values, AXES, pairs)  27.6 us
    pallas_call x1, Pallas kernels, back_to_input(): pl.pallas_call(back_body, grid=(steps,), in_specs=[pl.BlockSpec((n // ste...  17.6 us
  transfers between devices with their start and end apart: 29, of which 7 were waited for; matrix products, arithmetic and copies ran while one was open for 10% of the time, Pallas kernels for 56%

profile of v2, /device:TPU:0, one launch (start us, length us, event | category | flops | bytes accessed | tf_op | source)
XLA Modules:
  0.0 618.1 jit_solution(13396248569135849487)
XLA Ops:
  13.3 13.7 %all_to_all.20 = bf16[8,16,144]{2,1,0:T(8,128)(2,1)S(1)} all-to-all(bf16[8,16,144]{2,1,0:T(8,128)(2,1)S(1)} %copy.75), channel_id=1, replica_groups=mesh['dp'=8,'tp'=4] {'dp'}, dimensions={0} | all-to-all | bytes 73728 | tf_op jit(solution)/shard_map/all_to_all | solution.py:1036
  29.6 3.4 all-to-all-start.1
  38.8 33.5 %all-to-all-done.1.refs_0_ = f32[32,4,1728]{2,1,0:T(4,128)S(1)} async-done(((f32[32,4,1728]{2,1,0:T(4,128)}), f32[32,4,1728]{2,1,0:T(4,128)S(1)}, u32[]{:S(2)}, u32[]{:S(2)}) %all-to-all-start.1) | async-done | bytes 884768 | tf_op jit(solution)/shard_map/all_to_all | solution.py:1041
  88.5 7.9 %shard_map.232 = (bf16[1024,1152]{1,0:T(8,128)(2,1)}, bf16[1152,1024]{1,0:T(8,128)(2,1)}) custom-call(bf16[1024,1152]{1,0:T(8,128)(2,1)} %pad_maximum_fusion.refs_1_.refs_0_.refs_2_, f32[4,6912]{1,0:T(4,128)} %broadcast_add_fusion.refs_1_.refs_5_.refs_13_, s32[1024,128]{1,0:T(8,128)} %broadcast_in_dim.44.refs_2_.refs_5_.refs_6_.refs_14_.refs_10_, ...), custom_call_target="tpu_custom_call" | custom-call | flops 27599998976 | tf_op jit(solution)/shard_map/pallas_call | solution.py:926
  98.7 14.1 %shard_map.234 = (bf16[1024,864]{1,0:T(8,128)(2,1)}, bf16[1024,288]{1,0:T(8,128)(2,1)}, f32[8,1024]{1,0:T(8,128)}, bf16[1024,1152]{1,0:T(8,128)(2,1)}) custom-call(s32[4]{0:T(128)} %get-tuple-element.155.refs_0_, s32[4]{0:T(128)} %get-tuple-element.154.refs_1_, bf16[1024,1152]{1,0:T(8,128)(2,1)} %get-tuple-element.81.refs_1_.refs_2_, ...), custom_call_target="tpu_custom_call" | custom-call | flops 73600000000 | tf_op jit(solution)/shard_map/pallas_call | solution.py:620
  114.3 14.6 %shard_map.235 = (bf16[1024,864]{1,0:T(8,128)(2,1)}, bf16[1024,288]{1,0:T(8,128)(2,1)}, f32[8,1024]{1,0:T(8,128)}, bf16[1024,1152]{1,0:T(8,128)(2,1)}) custom-call(s32[4]{0:T(128)} %get-tuple-element.155.refs_0_, s32[4]{0:T(128)} %get-tuple-element.154.refs_1_, bf16[1024,1152]{1,0:T(8,128)(2,1)} %get-tuple-element.81.refs_1_.refs_2_, ...), custom_call_target="tpu_custom_call" | custom-call | flops 73600000000 | tf_op jit(solution)/shard_map/pallas_call | solution.py:620
  133.7 7.5 %shard_map.237 = (bf16[1024,1152]{1,0:T(8,128)(2,1)}, bf16[1152,1024]{1,0:T(8,128)(2,1)}, f32[1,1152]{1,0:T(1,128)}) custom-call(bf16[1024,1152]{1,0:T(8,128)(2,1)} %pad_maximum_fusion.1.refs_0_.refs_4_, f32[4,6912]{1,0:T(4,128)} %broadcast_add_fusion.refs_1_.refs_5_.refs_13_, s32[1024,128]{1,0:T(8,128)} %broadcast_in_dim.44.refs_2_.refs_5_.refs_6_.refs_14_.refs_10_, ...), custom_call_target="tpu_custom_call" | custom-call | flops 27599998976 | tf_op jit(solution)/shard_map/pallas_call | solution.py:926
  141.2 15.6 %collective-permute-done.3.refs_0_ = bf16[1152,1152]{1,0:T(8,128)(2,1)} collective-permute-done((bf16[1152,1152]{1,0:T(8,128)(2,1)}, bf16[1152,1152]{1,0:T(8,128)(2,1)}, u32[]{:S(2)}, u32[]{:S(2)}) %collective-permute-start.3) | collective-permute-done | bytes 2654240 | tf_op jit(solution)/shard_map/ppermute | solution.py:392
  156.8 14.3 %shard_map.239 = (bf16[1024,864]{1,0:T(8,128)(2,1)}, bf16[1024,288]{1,0:T(8,128)(2,1)}, f32[8,1024]{1,0:T(8,128)}, bf16[1024,1152]{1,0:T(8,128)(2,1)}) custom-call(s32[4]{0:T(128)} %get-tuple-element.155.refs_0_, s32[4]{0:T(128)} %get-tuple-element.154.refs_1_, bf16[1024,1152]{1,0:T(8,128)(2,1)} %get-tuple-element.81.refs_1_.refs_2_, ...), custom_call_target="tpu_custom_call" | custom-call | flops 73600000000 | tf_op jit(solution)/shard_map/pallas_call | solution.py:620
  171.7 14.3 %shard_map.241 = (bf16[1024,864]{1,0:T(8,128)(2,1)}, bf16[1024,288]{1,0:T(8,128)(2,1)}, f32[8,1024]{1,0:T(8,128)}, bf16[1024,1152]{1,0:T(8,128)(2,1)}) custom-call(s32[4]{0:T(128)} %get-tuple-element.155.refs_0_, s32[4]{0:T(128)} %get-tuple-element.154.refs_1_, bf16[1024,1152]{1,0:T(8,128)(2,1)} %get-tuple-element.81.refs_1_.refs_2_, ...), custom_call_target="tpu_custom_call" | custom-call | flops 73600000000 | tf_op jit(solution)/shard_map/pallas_call | solution.py:620
  186.0 12.7 %shard_map.242 = (f32[1024,1152]{1,0:T(8,128)}, f32[1024,1152]{1,0:T(8,128)}, bf16[1024,1152]{1,0:T(8,128)(2,1)}, bf16[1152,1024]{1,0:T(8,128)(2,1)}) custom-call(bf16[1024,1152]{1,0:T(8,128)(2,1)} %pad_maximum_fusion.refs_1_.refs_0_.refs_2_, bf16[1024,1152]{1,0:T(8,128)(2,1)} %get-tuple-element.82.refs_1_, bf16[1024,1152]{1,0:T(8,128)(2,1)} %get-tuple-element.84.refs_2_, ...), custom_call_target="tpu_custom_call" | custom-call | flops 55199997952 | tf_op jit(solution)/shard_map/pallas_call | solution.py:926
  201.1 26.9 %shard_map.243 = (bf16[1024,1152]{1,0:T(8,128)(2,1)}, bf16[1024,1152]{1,0:T(8,128)(2,1)}, f32[1,1152]{1,0:T(1,128)}, bf16[1152,2304]{1,0:T(8,128)(2,1)}) custom-call(bf16[1024,1152]{1,0:T(8,128)(2,1)} %get-tuple-element.92.refs_0_, bf16[1024,1152]{1,0:T(8,128)(2,1)} %get-tuple-element.93.refs_1_, bf16[1152,1024]{1,0:T(8,128)(2,1)} %get-tuple-element.94.refs_2_.refs_0_, ...), custom_call_target="tpu_custom_call" | custom-call | flops 124200001536 | tf_op jit(solution)/shard_map/pallas_call | solution.py:483
  228.0 19.7 %shard_map.244 = (bf16[1024,1152]{1,0:T(8,128)(2,1)}, bf16[1024,1152]{1,0:T(8,128)(2,1)}, f32[1,1152]{1,0:T(1,128)}, bf16[1024,1152]{1,0:T(8,128)(2,1)}, bf16[1024,1152]{1,0:T(8,128)(2,1)}) custom-call(bf16[1024,1152]{1,0:T(8,128)(2,1)} %get-tuple-element.92.refs_0_, bf16[1024,1152]{1,0:T(8,128)(2,1)} %get-tuple-element.93.refs_1_, ...), custom_call_target="tpu_custom_call" | custom-call | flops 87399997440 | tf_op jit(solution)/shard_map/pallas_call | solution.py:483
  247.7 7.7 %all-gather.8.cloned.1.call-done.refs_0_ = bf16[1152,2304]{1,0:T(8,128)(2,1)} async-done(((bf16[144,2304]{1,0:T(8,128)(2,1)}), bf16[1152,2304]{1,0:T(8,128)(2,1)}) %all-gather.8.cloned.1.call-update) | async-done | bytes 5308432 | tf_op jit(solution)/shard_map/all_gather | solution.py:1047
  259.9 11.8 %shard_map.246.refs_7_ = bf16[1152,2304]{1,0:T(8,128)(2,1)} custom-call(bf16[1152,1024]{1,0:T(8,128)(2,1)} %get-tuple-element.94.refs_2_.refs_0_, bf16[1152,1024]{1,0:T(8,128)(2,1)} %get-tuple-element.95.refs_3_.refs_1_, bf16[1024,1152]{1,0:T(8,128)(2,1)} %get-tuple-element.98.refs_2_, bf16[1024,1152]{1,0:T(8,128)(2,1)} %get-tuple-element.99.refs_3_, ...), custom_call_target="tpu_custom_call" | custom-call | flops 55199997952 | tf_op jit(solution)/shard_map/pallas_call | solution.py:483
  271.8 26.9 %shard_map.247 = (bf16[1024,1152]{1,0:T(8,128)(2,1)}, bf16[1024,1152]{1,0:T(8,128)(2,1)}, f32[1,1152]{1,0:T(1,128)}, bf16[1152,2304]{1,0:T(8,128)(2,1)}) custom-call(bf16[1024,1152]{1,0:T(8,128)(2,1)} %get-tuple-element.92.refs_0_, bf16[1024,1152]{1,0:T(8,128)(2,1)} %get-tuple-element.93.refs_1_, bf16[1152,1024]{1,0:T(8,128)(2,1)} %get-tuple-element.94.refs_2_.refs_0_, ...), custom_call_target="tpu_custom_call" | custom-call | flops 124200001536 | tf_op jit(solution)/shard_map/pallas_call | solution.py:483
  299.3 19.4 %shard_map.248 = (bf16[1024,1152]{1,0:T(8,128)(2,1)}, bf16[1024,1152]{1,0:T(8,128)(2,1)}, f32[1,1152]{1,0:T(1,128)}, bf16[1024,1152]{1,0:T(8,128)(2,1)}, bf16[1024,1152]{1,0:T(8,128)(2,1)}) custom-call(bf16[1024,1152]{1,0:T(8,128)(2,1)} %get-tuple-element.92.refs_0_, bf16[1024,1152]{1,0:T(8,128)(2,1)} %get-tuple-element.93.refs_1_, ...), custom_call_target="tpu_custom_call" | custom-call | flops 87399997440 | tf_op jit(solution)/shard_map/pallas_call | solution.py:483
  320.9 12.0 %shard_map.249.refs_16_ = bf16[1152,2304]{1,0:T(8,128)(2,1)} custom-call(bf16[1152,1024]{1,0:T(8,128)(2,1)} %get-tuple-element.94.refs_2_.refs_0_, bf16[1152,1024]{1,0:T(8,128)(2,1)} %get-tuple-element.95.refs_3_.refs_1_, bf16[1024,1152]{1,0:T(8,128)(2,1)} %get-tuple-element.110.refs_2_, bf16[1024,1152]{1,0:T(8,128)(2,1)} %get-tuple-element.111.refs_3_, ...), custom_call_target="tpu_custom_call" | custom-call | flops 55199997952 | tf_op jit(solution)/shard_map/pallas_call | solution.py:483
  332.9 21.6 %shard_map.250 = (bf16[1024,1152]{1,0:T(8,128)(2,1)}, f32[1024,1152]{1,0:T(8,128)}, bf16[1024,1152]{1,0:T(8,128)(2,1)}, bf16[1152,1024]{1,0:T(8,128)(2,1)}, f32[1,1152]{1,0:T(1,128)}, /*index=5*/f32[4,4608]{1,0:T(4,128)}) custom-call(s32[8]{0:T(128)} %get-tuple-element.153.refs_0_, s32[8]{0:T(128)} %get-tuple-element.152.refs_1_, ...), custom_call_target="tpu_custom_call" | custom-call | flops 23000000512 | tf_op jit(solution)/shard_map/pallas_call | solution.py:926
  356.2 23.2 %shard_map.251 = (bf16[1024,864]{1,0:T(8,128)(2,1)}, f32[1,864]{1,0:T(1,128)}, bf16[1152,1152]{1,0:T(8,128)(2,1)}) custom-call(s32[4]{0:T(128)} %get-tuple-element.155.refs_0_, s32[4]{0:T(128)} %get-tuple-element.154.refs_1_, s32[8]{0:T(128)} %shift-right-arithmetic_add_fusion.refs_2_, bf16[1024,864]{1,0:T(8,128)(2,1)} %get-tuple-element.114.refs_3_, ...), custom_call_target="tpu_custom_call" | custom-call | flops 32199999488 | tf_op jit(solution)/shard_map/pallas_call | solution.py:769
  381.6 23.2 %shard_map.253 = (bf16[1024,864]{1,0:T(8,128)(2,1)}, f32[1,864]{1,0:T(1,128)}, bf16[1152,1152]{1,0:T(8,128)(2,1)}) custom-call(s32[4]{0:T(128)} %get-tuple-element.155.refs_0_, s32[4]{0:T(128)} %get-tuple-element.154.refs_1_, s32[8]{0:T(128)} %shift-right-arithmetic_add_fusion.refs_2_, bf16[1024,864]{1,0:T(8,128)(2,1)} %get-tuple-element.126.refs_3_, ...), custom_call_target="tpu_custom_call" | custom-call | flops 32199999488 | tf_op jit(solution)/shard_map/pallas_call | solution.py:769
  407.2 5.8 all-to-all-start.2
  415.4 23.9 %shard_map.254 = (bf16[1024,864]{1,0:T(8,128)(2,1)}, f32[1,864]{1,0:T(1,128)}, bf16[4,144,1152]{2,1,0:T(8,128)(2,1)}, bf16[4,144,1152]{2,1,0:T(8,128)(2,1)}) custom-call(s32[4]{0:T(128)} %get-tuple-element.155.refs_0_, s32[4]{0:T(128)} %get-tuple-element.154.refs_1_, s32[8]{0:T(128)} %shift-right-arithmetic_add_fusion.refs_2_, ...), custom_call_target="tpu_custom_call" | custom-call | flops 32199999488 | tf_op jit(solution)/shard_map/pallas_call | solution.py:769
  439.2 3.0 collective-permute-start.13
  443.7 23.4 %shard_map.255 = (bf16[1024,864]{1,0:T(8,128)(2,1)}, f32[1,864]{1,0:T(1,128)}, bf16[1152,1152]{1,0:T(8,128)(2,1)}) custom-call(s32[4]{0:T(128)} %get-tuple-element.155.refs_0_, s32[4]{0:T(128)} %get-tuple-element.154.refs_1_, s32[8]{0:T(128)} %shift-right-arithmetic_add_fusion.refs_2_, bf16[1024,864]{1,0:T(8,128)(2,1)} %get-tuple-element.121.refs_3_, ...), custom_call_target="tpu_custom_call" | custom-call | flops 32199999488 | tf_op jit(solution)/shard_map/pallas_call | solution.py:769
  471.2 11.9 %collective-permute-done.13.refs_0_ = bf16[4,144,1152]{2,1,0:T(8,128)(2,1)S(1)} collective-permute-done((bf16[4,144,1152]{2,1,0:T(8,128)(2,1)}, bf16[4,144,1152]{2,1,0:T(8,128)(2,1)S(1)}, u32[]{:S(2)}, u32[]{:S(2)}) %collective-permute-start.13) | collective-permute-done | bytes 1327136 | tf_op jit(solution)/shard_map/ppermute | solution.py:392
  492.7 37.6 %reduce-scatter.6.cloned.1.call-done.refs_1_ = bf16[144,2304]{1,0:T(8,128)(2,1)} async-done(((bf16[1152,2304]{1,0:T(8,128)(2,1)}), bf16[144,2304]{1,0:T(8,128)(2,1)}) %reduce-scatter.6.cloned.1.call-update) | async-done | bytes 663568 | tf_op jit(solution)/shard_map/reduce_scatter | solution.py:1114
  530.3 17.6 %shard_map.257.refs_4_.refs_3_ = f32[1024,1152]{1,0:T(8,128)} custom-call(bf16[1024,864]{1,0:T(8,128)(2,1)} %get-tuple-element.132.q0, bf16[1024,864]{1,0:T(8,128)(2,1)} %get-tuple-element.133.q1, bf16[1024,864]{1,0:T(8,128)(2,1)} %get-tuple-element.134.q2, bf16[1024,864]{1,0:T(8,128)(2,1)} %get-tuple-element.135.q3, ...), custom_call_target="tpu_custom_call" | custom-call | flops 78199996416 | tf_op jit(solution)/shard_map/pallas_call | solution.py:891
  547.9 11.3 %shard_map.258 = (bf16[1024,1152]{1,0:T(8,128)(2,1)}, f32[4,2304]{1,0:T(4,128)}) custom-call(s32[8]{0:T(128)} %get-tuple-element.153.refs_0_, s32[8]{0:T(128)} %get-tuple-element.152.refs_1_, bf16[1024,1152]{1,0:T(8,128)(2,1)} %pad_maximum_fusion.refs_1_.refs_0_.refs_2_, f32[1024,1152]{1,0:T(8,128)} %get-tuple-element.120.refs_3_, ...), custom_call_target="tpu_custom_call" | custom-call | flops 50600001536 | tf_op jit(solution)/shard_map/pallas_call | solution.py:926
  568.7 3.0 all-to-all-start.3
  578.6 13.8 %all-to-all-done.3 = bf16[32,93,128]{2,1,0:T(8,128)(2,1)S(1)} async-done(((bf16[32,93,128]{2,1,0:T(8,128)(2,1)}), bf16[32,93,128]{2,1,0:T(8,128)(2,1)S(1)}, u32[]{:S(2)}, u32[]{:S(2)}) %all-to-all-start.3) | async-done | bytes 761888 | tf_op jit(solution)/shard_map/all_to_all | solution.py:992
  597.3 10.9 %reduce-scatter.8.cloned.1.call-done = bf16[144,1152]{1,0:T(8,128)(2,1)} async-done(((bf16[1152,1152]{1,0:T(8,128)(2,1)}), bf16[144,1152]{1,0:T(8,128)(2,1)}) %reduce-scatter.8.cloned.1.call-update) | async-done | bytes 331792 | tf_op jit(solution)/shard_map/reduce_scatter | solution.py:1154
  (290 shorter events, 96.5 us)
Async XLA Ops:
  7.2 89.3 %all-gather.4.cloned.1.call-start = ((), (), s32[]{:S(2)}) async-start(), calls=%async_computation.7 | async-start | bytes 2985984 | tf_op jit(solution)/shard_map/all_gather | solution.py:1024
  12.6 23.1 %collective-permute-start = (bf16[512,1152]{1,0:T(8,128)(2,1)}, bf16[512,1152]{1,0:T(8,128)(2,1)S(1)}, u32[]{:S(2)}, u32[]{:S(2)}) collective-permute-start(bf16[512,1152]{1,0:T(8,128)(2,1)} %dynamic-slice_bitcast_fusion.1), channel_id=1, source_target_pairs={{0,1},{1,0},{2,3},{3,2},{4,5},{5,4},{6,7},{7,6},{8,9},{9,8},{10,11... | collective-permute-start | bytes 3538952 | tf_op jit(solution)/shard_map/ppermute | solution.py:392
  29.6 42.8 %all-to-all-start.1 = ((f32[32,4,1728]{2,1,0:T(4,128)}), f32[32,4,1728]{2,1,0:T(4,128)S(1)}, u32[]{:S(2)}, u32[]{:S(2)}) async-start(f32[32,4,1728]{2,1,0:T(4,128)} %copy.78.refs_1_), calls=%async_computation.1 | async-start | bytes 1835008 | tf_op jit(solution)/shard_map/all_to_all | solution.py:1041
  33.0 138.1 %all-gather.6.cloned.1.call-start = ((), (), s32[]{:S(2)}) async-start(), calls=%async_computation.8 | async-start | bytes 5971968 | tf_op jit(solution)/shard_map/all_gather | solution.py:1046
  34.0 41.5 %collective-permute-start.1 = (bf16[144,2304]{1,0:T(8,128)(2,1)}, bf16[144,2304]{1,0:T(8,128)(2,1)S(1)}, u32[]{:S(2)}, u32[]{:S(2)}) collective-permute-start(bf16[144,2304]{1,0:T(8,128)(2,1)} %shard_map.230), channel_id=1, source_target_pairs={{0,2},{1,3},{2,0},{3,1},{4,6},{5,7},{6,4},{7,5},{8,10},{9,11},{10,... | collective-permute-start | bytes 1990664 | tf_op jit(solution)/shard_map/ppermute | solution.py:392
  76.4 179.0 %all-gather.8.cloned.1.call-start = ((), (), s32[]{:S(2)}) async-start(), calls=%async_computation.9 | async-start | bytes 5971968 | tf_op jit(solution)/shard_map/all_gather | solution.py:1047
  78.8 50.1 %collective-permute-start.4 = (bf16[512,1152]{1,0:T(8,128)(2,1)}, bf16[512,1152]{1,0:T(8,128)(2,1)}, u32[]{:S(2)}, u32[]{:S(2)}) collective-permute-start(bf16[512,1152]{1,0:T(8,128)(2,1)} %dynamic-slice_bitcast_fusion), channel_id=1, source_target_pairs={{0,1},{1,0},{2,3},{3,2},{4,5},{5,4},{6,7},{7,6},{8,9},{9,8},{10,11... | collective-permute-start | bytes 3538952 | tf_op jit(solution)/shard_map/ppermute | solution.py:392
  87.2 294.3 %reduce-scatter.4.cloned.1.call-start = ((), (), s32[]{:S(2)}) async-start(), calls=%async_computation.10 | async-start | bytes 5971968 | tf_op jit(solution)/shard_map/reduce_scatter | solution.py:1109
  96.5 60.3 %collective-permute-start.3 = (bf16[1152,1152]{1,0:T(8,128)(2,1)}, bf16[1152,1152]{1,0:T(8,128)(2,1)}, u32[]{:S(2)}, u32[]{:S(2)}) collective-permute-start(bf16[1152,1152]{1,0:T(8,128)(2,1)} %shard_map.233.refs_3_.refs_8_.w0), channel_id=1, source_target_pairs={{0,2},{1,3},{2,0},{3,1},{4,6},{5,7},{6,4},{7,5},{8,10},{9,11},{10,... | collective-permute-start | bytes 7962632 | tf_op jit(solution)/shard_map/ppermute | solution.py:392
  97.9 14.9 %collective-permute-start.2 = (bf16[1152,1152]{1,0:T(8,128)(2,1)}, bf16[1152,1152]{1,0:T(8,128)(2,1)S(1)}, u32[]{:S(2)}, u32[]{:S(2)}) collective-permute-start(bf16[1152,1152]{1,0:T(8,128)(2,1)} %shard_map.233.refs_3_.refs_8_.w0), channel_id=1, source_target_pairs={{0,1},{1,0},{2,3},{3,2},{4,5},{5,4},{6,7},{7,6},{8,9},{9,8},{10,11... | collective-permute-start | bytes 7962632 | tf_op jit(solution)/shard_map/ppermute | solution.py:392
  156.8 14.9 %collective-permute-start.5 = (bf16[1152,1152]{1,0:T(8,128)(2,1)}, bf16[1152,1152]{1,0:T(8,128)(2,1)}, u32[]{:S(2)}, u32[]{:S(2)}) collective-permute-start(bf16[1152,1152]{1,0:T(8,128)(2,1)} %shard_map.238.refs_3_.refs_8_.w2), channel_id=1, source_target_pairs={{0,1},{1,0},{2,3},{3,2},{4,5},{5,4},{6,7},{7,6},{8,9},{9,8},{10,11... | collective-permute-start | bytes 7962632 | tf_op jit(solution)/shard_map/ppermute | solution.py:392
  171.1 27.6 %collective-permute-start.6 = (bf16[1152,2304]{1,0:T(8,128)(2,1)}, bf16[1152,2304]{1,0:T(8,128)(2,1)S(1)}, u32[]{:S(2)}, u32[]{:S(2)}) collective-permute-start(bf16[1152,2304]{1,0:T(8,128)(2,1)} %shard_map.240.refs_8_.refs_2_.refs_3_), channel_id=1, source_target_pairs={{0,1},{1,0},{2,3},{3,2},{4,5},{5,4},{6,7},{7,6},{8,9},{9,8},{10,11... | collective-permute-start | bytes 15925256 | tf_op jit(solution)/shard_map/ppermute | solution.py:392
  228.0 32.0 %collective-permute-start.8 = (bf16[1152,2304]{1,0:T(8,128)(2,1)}, bf16[1152,2304]{1,0:T(8,128)(2,1)}, u32[]{:S(2)}, u32[]{:S(2)}) collective-permute-start(bf16[1152,2304]{1,0:T(8,128)(2,1)} %get-tuple-element.100), channel_id=1, source_target_pairs={{0,1},{1,0},{2,3},{3,2},{4,5},{5,4},{6,7},{7,6},{8,9},{9,8},{10,11... | collective-permute-start | bytes 15925256 | tf_op jit(solution)/shard_map/ppermute | solution.py:392
  255.4 16.4 %collective-permute-start.7 = (bf16[1152,2304]{1,0:T(8,128)(2,1)}, bf16[1152,2304]{1,0:T(8,128)(2,1)}, u32[]{:S(2)}, u32[]{:S(2)}) collective-permute-start(bf16[1152,2304]{1,0:T(8,128)(2,1)} %shard_map.245.refs_5_.refs_2_.refs_3_), channel_id=1, source_target_pairs={{0,1},{1,0},{2,3},{3,2},{4,5},{5,4},{6,7},{7,6},{8,9},{9,8},{10,11... | collective-permute-start | bytes 15925256 | tf_op jit(solution)/shard_map/ppermute | solution.py:392
  271.8 258.5 %reduce-scatter.6.cloned.1.call-start = ((), (), s32[]{:S(2)}) async-start(), calls=%async_computation.11 | async-start | bytes 5971968 | tf_op jit(solution)/shard_map/reduce_scatter | solution.py:1114
  298.8 19.9 %collective-permute-start.9 = (bf16[1152,2304]{1,0:T(8,128)(2,1)}, bf16[1152,2304]{1,0:T(8,128)(2,1)S(1)}, u32[]{:S(2)}, u32[]{:S(2)}) collective-permute-start(bf16[1152,2304]{1,0:T(8,128)(2,1)} %get-tuple-element.112), channel_id=1, source_target_pairs={{0,1},{1,0},{2,3},{3,2},{4,5},{5,4},{6,7},{7,6},{8,9},{9,8},{10,11... | collective-permute-start | bytes 15925256 | tf_op jit(solution)/shard_map/ppermute | solution.py:392
  355.9 23.4 %collective-permute-start.10 = (bf16[512,1152]{1,0:T(8,128)(2,1)S(1)}, bf16[512,1152]{1,0:T(8,128)(2,1)S(1)}, u32[]{:S(2)}, u32[]{:S(2)}) collective-permute-start(bf16[512,1152]{1,0:T(8,128)(2,1)S(1)} %constant_dynamic-slice_fusion.1), channel_id=1, source_target_pairs={{0,1},{1,0},{2,3},{3,2},{4,5},{5,4},{6,7},{7,6},{8,9},{9,8},{10,11... | collective-permute-start | bytes 3538952 | tf_op jit(solution)/shard_map/ppermute | solution.py:392
  381.6 23.8 %copy-start.23 = (f32[4,4608]{1,0:T(4,128)S(1)}, f32[4,4608]{1,0:T(4,128)}, u32[]{:S(2)}) copy-start(f32[4,4608]{1,0:T(4,128)} %get-tuple-element.146) | copy-start | bytes 221188
  381.6 24.2 %copy-start.29 = (bf16[1,1152]{1,0:T(2,128)(2,1)S(1)}, bf16[1,1152]{1,0:T(2,128)(2,1)}, u32[]{:S(2)}) copy-start(bf16[1,1152]{1,0:T(2,128)(2,1)} %convert.40) | copy-start | bytes 6916
  404.9 10.5 %collective-permute-start.12 = (bf16[1152,1152]{1,0:T(8,128)(2,1)}, bf16[1152,1152]{1,0:T(8,128)(2,1)}, u32[]{:S(2)}, u32[]{:S(2)}) collective-permute-start(bf16[1152,1152]{1,0:T(8,128)(2,1)} %get-tuple-element.129), channel_id=1, source_target_pairs={{0,1},{1,0},{2,3},{3,2},{4,5},{5,4},{6,7},{7,6},{8,9},{9,8},{10,11... | collective-permute-start | bytes 7962632 | tf_op jit(solution)/shard_map/ppermute | solution.py:392
  407.2 60.0 %all-to-all-start.2 = ((bf16[32,57,128]{2,1,0:T(8,128)(2,1)}), bf16[32,57,128]{2,1,0:T(8,128)(2,1)S(1)}, u32[]{:S(2)}, u32[]{:S(2)}) async-start(bf16[32,57,128]{2,1,0:T(8,128)(2,1)} %pad_maximum_fusion.7), calls=%async_computation.5 | async-start | bytes 1048576 | tf_op jit(solution)/shard_map/all_to_all | solution.py:992
  412.9 195.2 %reduce-scatter.8.cloned.1.call-start = ((), (), s32[]{:S(2)}) async-start(), calls=%async_computation.12 | async-start | bytes 2985984 | tf_op jit(solution)/shard_map/reduce_scatter | solution.py:1154
  413.0 29.2 %collective-permute-start.11 = (bf16[1152,1152]{1,0:T(8,128)(2,1)}, bf16[1152,1152]{1,0:T(8,128)(2,1)S(1)}, u32[]{:S(2)}, u32[]{:S(2)}) collective-permute-start(bf16[1152,1152]{1,0:T(8,128)(2,1)} %get-tuple-element.123), channel_id=1, source_target_pairs={{0,1},{1,0},{2,3},{3,2},{4,5},{5,4},{6,7},{7,6},{8,9},{9,8},{10,11... | collective-permute-start | bytes 7962632 | tf_op jit(solution)/shard_map/ppermute | solution.py:392
  413.5 57.6 %collective-permute-start.14 = (bf16[144,2304]{1,0:T(8,128)(2,1)}, bf16[144,2304]{1,0:T(8,128)(2,1)S(1)}, u32[]{:S(2)}, u32[]{:S(2)}) collective-permute-start(bf16[144,2304]{1,0:T(8,128)(2,1)} %reduce-scatter.4.cloned.1.call-done.refs_14_), channel_id=1, source_target_pairs={{0,2},{1,3},{2,0},{3,1},{4,6},{5,7},{6,4},{7,5},{8,10},{9,11},{10,... | collective-permute-start | bytes 1990664 | tf_op jit(solution)/shard_map/ppermute | solution.py:392
  439.2 43.8 %collective-permute-start.13 = (bf16[4,144,1152]{2,1,0:T(8,128)(2,1)}, bf16[4,144,1152]{2,1,0:T(8,128)(2,1)S(1)}, u32[]{:S(2)}, u32[]{:S(2)}) collective-permute-start(bf16[4,144,1152]{2,1,0:T(8,128)(2,1)} %get-tuple-element.137), channel_id=1, source_target_pairs={{0,4},{1,5},{2,6},{3,7},{4,0},{5,1},{6,2},{7,3},{8,12},{9,13},{10,... | collective-permute-start | bytes 3981320 | tf_op jit(solution)/shard_map/ppermute | solution.py:392
  443.7 26.5 %copy-start.33 = (f32[1,864]{1,0:T(1,128)S(1)}, f32[1,864]{1,0:T(1,128)}, u32[]{:S(2)}) copy-start(f32[1,864]{1,0:T(1,128)} %get-tuple-element.131.refs_13_.refs_1_) | copy-start | bytes 10372
  488.3 72.1 %collective-permute-start.18 = (bf16[144,1152]{1,0:T(8,128)(2,1)}, bf16[144,1152]{1,0:T(8,128)(2,1)S(1)}, u32[]{:S(2)}, u32[]{:S(2)}) collective-permute-start(bf16[144,1152]{1,0:T(8,128)(2,1)} %get-tuple-element.168), channel_id=1, source_target_pairs={{0,24},{1,25},{2,26},{3,27},{4,28},{5,29},{6,30},{7,31},{8,16},{9,... | collective-permute-start | bytes 995336 | tf_op jit(solution)/shard_map/ppermute | solution.py:392
  491.3 69.2 %collective-permute-start.17 = (bf16[144,1152]{1,0:T(8,128)(2,1)}, bf16[144,1152]{1,0:T(8,128)(2,1)S(1)}, u32[]{:S(2)}, u32[]{:S(2)}) collective-permute-start(bf16[144,1152]{1,0:T(8,128)(2,1)} %get-tuple-element.169), channel_id=1, source_target_pairs={{0,16},{1,17},{2,18},{3,19},{4,20},{5,21},{6,22},{7,23},{8,24},{9,... | collective-permute-start | bytes 995336 | tf_op jit(solution)/shard_map/ppermute | solution.py:392
  491.3 69.2 %collective-permute-start.16 = (bf16[144,1152]{1,0:T(8,128)(2,1)}, bf16[144,1152]{1,0:T(8,128)(2,1)}, u32[]{:S(2)}, u32[]{:S(2)}) collective-permute-start(bf16[144,1152]{1,0:T(8,128)(2,1)} %get-tuple-element.170), channel_id=1, source_target_pairs={{0,8},{1,9},{2,10},{3,11},{4,12},{5,13},{6,14},{7,15},{8,0},{9,1},... | collective-permute-start | bytes 995336 | tf_op jit(solution)/shard_map/ppermute | solution.py:392
  563.5 10.5 %collective-permute-start.19 = (bf16[144,1152]{1,0:T(8,128)(2,1)}, bf16[144,1152]{1,0:T(8,128)(2,1)S(1)}, u32[]{:S(2)}, u32[]{:S(2)}) collective-permute-start(bf16[144,1152]{1,0:T(8,128)(2,1)} %add_convert_fusion), channel_id=1, source_target_pairs={{0,2},{1,3},{2,0},{3,1},{4,6},{5,7},{6,4},{7,5},{8,10},{9,11},{10,... | collective-permute-start | bytes 995336 | tf_op jit(solution)/shard_map/ppermute | solution.py:392
  567.3 7.5 %collective-permute-start.15 = (bf16[512,1152]{1,0:T(8,128)(2,1)}, bf16[512,1152]{1,0:T(8,128)(2,1)}, u32[]{:S(2)}, u32[]{:S(2)}) collective-permute-start(bf16[512,1152]{1,0:T(8,128)(2,1)} %constant_dynamic-slice_fusion), channel_id=1, source_target_pairs={{0,1},{1,0},{2,3},{3,2},{4,5},{5,4},{6,7},{7,6},{8,9},{9,8},{10,11... | collective-permute-start | bytes 3538952 | tf_op jit(solution)/shard_map/ppermute | solution.py:392
  568.7 23.7 %all-to-all-start.3 = ((bf16[32,93,128]{2,1,0:T(8,128)(2,1)}), bf16[32,93,128]{2,1,0:T(8,128)(2,1)S(1)}, u32[]{:S(2)}, u32[]{:S(2)}) async-start(bf16[32,93,128]{2,1,0:T(8,128)(2,1)} %pad_maximum_fusion.4), calls=%async_computation.6 | async-start | bytes 1572864 | tf_op jit(solution)/shard_map/all_to_all | solution.py:992
  (42 other events, 331.8 us)
Sparse Core Ops, SparseCore 0:
  10.4 67.8 all-gather.3
  81.0 86.3 all-gather.5
  170.1 85.2 all-gather.7
  271.9 102.5 reduce-scatter.3
  378.3 151.9 reduce-scatter.5
  533.8 74.3 reduce-scatter.7

commit v3 on v2

--- a/solution.py
+++ b/solution.py
@@ -897,7 +897,7 @@
         out_specs=pl.BlockSpec((n // steps, d), lambda s: (s, 0)),
         out_shape=jax.ShapeDtypeStruct((n, d), f32),
         compiler_params=compiler_params(),
-        cost_estimate=cost(17),
+        cost_estimate=cost(1),
     )(*grads, *[w for w, _ in weights], *waits)
 
 
@@ -1033,12 +1033,25 @@
     small = seg.reshape(-1, ET)
     first, last = small[:, 0], small[:, -1]
     lifted = smooth_gate(conditioning.astype(f32)).astype(bf16).reshape(-1, 8, w_ada.shape[0])
-    lifted = lax.all_to_all(lifted.transpose(1, 0, 2), "dp", 0, 0)
+    (lifted,) = tie([lifted.transpose(1, 0, 2)], (att_shard,))
+    lifted = lax.all_to_all(lifted, "dp", 0, 0)
     lifted = lifted.reshape(8, 2, 2, IMG_ROW, -1).transpose(0, 2, 1, 3, 4).reshape(32 * IMG_ROW, -1)
     mod_part = dot(lifted, w_ada).reshape(32, IMG_ROW, mod_dev)
     (mlp_shard,) = tie([mlp_shard], (mod_part,))
     peer_shard = across(mlp_shard, CHIP)
-    (mod_part,) = tie([lax.all_to_all(mod_part, AXES, 0, 0)], (x,))
+    qkv_bias = jnp.stack([qv_bias[0], jnp.zeros_like(qv_bias[0]), qv_bias[1]]).astype(f32)
+    qkv_bias = [
+        lax.dynamic_slice_in_dim(qkv_bias, (tp_rank ^ k) * e, e, 1).reshape(1, 3 * e)
+        for k in range(4)
+    ]
+    fc1_part = [
+        lax.dynamic_slice_in_dim(fc1_bias.astype(f32)[None], (tp_rank ^ k) * ff, ff, 1)
+        for k in range(4)
+    ]
+    out_bias_row, fc2_bias_row = out_bias.astype(f32)[None], fc2_bias.astype(f32)[None]
+    ready = (x, seg_col, seg_row, lo, hi, first, last, g_row.own, out_bias_row, fc2_bias_row)
+    ready += tuple(qkv_bias) + tuple(fc1_part)
+    (mod_part,) = tie([lax.all_to_all(mod_part, AXES, 0, 0)], ready)
     mod_part = mod_part.reshape(8, 4, IMG_ROW, mod_dev)
     modulation = jnp.sum(mod_part, axis=0).transpose(1, 0, 2).reshape(IMG_ROW, -1)
     modulation = modulation + ada_bias.astype(f32)
@@ -1055,15 +1068,13 @@
         [("t", *row_b), ("T", *turned)],
         waits=(peer_shard,),
     )
-    qkv_bias = jnp.stack([qv_bias[0], jnp.zeros_like(qv_bias[0]), qv_bias[1]]).astype(f32)
     kept = {}
 
     def forward(k, waits):
-        bias = lax.dynamic_slice_in_dim(qkv_bias, (tp_rank ^ k) * e, e, 1).reshape(1, 3 * e)
-        kept[k] = attend_fwd(a, att_w[k], bias, lo, hi, seg_col, seg_row, waits)
+        kept[k] = attend_fwd(a, att_w[k], qkv_bias[k], lo, hi, seg_col, seg_row, waits)
         return (kept[k][2],)
 
-    (near_att,) = tie([near_att], (a,))
+    (near_att,) = tie([near_att], (modulation,))
     att_w = [(v, 0) for v in (near_att, across(near_att, CORE), across(near_att, CHIP))]
     after = forward(1, forward(0, ()))
     (g_row.got,) = tie([g_row.got], after)
@@ -1088,28 +1099,23 @@
         (),
         [("t", x)]
         + [("t", kept[k][3]) for k in range(4)]
-        + [("w", modulation), ("t", seg_col), ("w", out_bias.astype(f32)[None])],
+        + [("w", modulation), ("t", seg_col), ("w", out_bias_row)],
         [("t", *row_f), ("t", *row_f), ("t", *row_b), ("T", *turned)],
     )
     done = {}
-    fc1_f = fc1_bias.astype(f32)[None]
-
-    def fc1_part(k):
-        return lax.dynamic_slice_in_dim(fc1_f, (tp_rank ^ k) * ff, ff, 1)
-
     def halves(w):
         return ((w, 0), (w, 1))
 
-    done[3] = mlp_whole(m, bg2, m_t, bg2_t, halves(partner_w), fc1_part(3))
+    done[3] = mlp_whole(m, bg2, m_t, bg2_t, halves(partner_w), fc1_part[3])
     init = across(done[3][3], CORE)
-    done[2] = mlp_first(m, bg2, halves(far_w), fc1_part(2), (done[3][2],))
+    done[2] = mlp_first(m, bg2, halves(far_w), fc1_part[2], (done[3][2],))
     (near_w,) = tie([near_w], (done[2][2],))
     partner_w = across(near_w, CORE)
     grad = mlp_second(m_t, bg2_t, *done[2][3:], init, (near_w,))
     far_sum = lax.psum_scatter(grad, "dp", scatter_dimension=0, tiled=True)
-    done[1] = mlp_whole(m, bg2, m_t, bg2_t, halves(partner_w), fc1_part(1), (grad,))
+    done[1] = mlp_whole(m, bg2, m_t, bg2_t, halves(partner_w), fc1_part[1], (grad,))
     init = across(done[1][3], CORE)
-    done[0] = mlp_first(m, bg2, halves(near_w), fc1_part(0), (done[1][2],))
+    done[0] = mlp_first(m, bg2, halves(near_w), fc1_part[0], (done[1][2],))
     grad = mlp_second(m_t, bg2_t, *done[0][3:], init)
     near_sum = lax.psum_scatter(grad, "dp", scatter_dimension=0, tiled=True)
     block_output, hidden_grad, bg1, bg1_t, out_sum, img_late = by_rows(
@@ -1119,7 +1125,7 @@
         [("t", hidden), ("t", branch1), ("t", g)]
         + [("t", done[k][0]) for k in range(4)]
         + [("t", done[k][1]) for k in range(4)]
-        + [("w", modulation), ("t", seg_col), ("w", fc2_bias.astype(f32)[None])],
+        + [("w", modulation), ("t", seg_col), ("w", fc2_bias_row)],
         [("t", *row_b), ("t", *row_f), ("t", *row_b), ("T", *turned), ("w", (1, d), f32), ("w", (IMG_ROW, 4 * d), f32)],
         waits=(grad,),
     )
@@ -1150,22 +1156,24 @@
     late_grads, late_sums = taken_apart(late, IMG_ROW, mod_dev)
     far = Scatter(*back[2][2:])
     far_peer = across(far_sum, CHIP)
-    after = backward(0, last_init, after)
-    near_att = lax.psum_scatter(back[0][2], "dp", scatter_dimension=0, tiled=True)
+    after = backward(0, last_init, after, (4 * e,))
     far.got, far_peer = tie([far.got, far_peer], after)
     far.turn()
-    a_grad = back_to_input([back[k][0] for k in range(4)], att_w, (far.low, near_sum))
-    far.got = tie(far.got, (a_grad,))
-    far_att = across(far.total().astype(bf16), CHIP)
+    near = Scatter(*back[0][2:])
+    a_grad = back_to_input([back[k][0] for k in range(4)], att_w, (far.low,))
+    (near.got,) = tie([near.got], (a_grad,))
+    near.turn()
     input_grad, img_early = by_rows(
         leave_body,
-        11,
+        1,
         (first, last),
         [("t", x), ("t", hidden_grad), ("t", a_grad), ("w", modulation), ("t", seg_col)],
         [("t", *row_b), ("w", (IMG_ROW, 2 * d), f32)],
-    )
-    (far_att,) = tie([far_att], (img_early,))
-    att_total = near_att.astype(f32) + far_att.astype(f32)
+        waits=(near.low, near_sum),
+    )
+    far.got = tie(far.got, (img_early,))
+    far_att = across(far.total().astype(bf16), CHIP)
+    att_total = near.total() + far_att.astype(f32)
     near_sum = near_sum.astype(f32)
     fc1_grad = near_sum[:, :ff]
     fc2_grad = near_sum[:, ff:]

time: 624 us -> 621 us (level)
  starting transfers between devices: 29.4 us -> 44.5 us
  waiting for transfers between devices: 131 us -> 116 us
  blocking collectives: 13.7 us -> 0 us
  Pallas kernels: 346 us -> 356 us
    reduce_scatter x1, waiting for transfers between devices: 37.6 us -> 12.9 us  [row_body(): near_sum = lax.psum_scatter(grad, 'dp', scatter_dimension=0, tiled=True)]
    ppermute x20 -> x24, waiting for transfers between devices: 27.6 us -> 42.8 us  [swap(): return lax.ppermute(values, AXES, pairs)]
    all_to_all x1 -> x0, blocking collectives: 13.7 us -> none  [row_body(): lifted = lax.all_to_all(lifted.transpose(1, 0, 2), 'dp', 0, 0)]
    reduce_scatter x1 -> x0, waiting for transfers between devices: 10.9 us -> none  [row_body(): lax.psum_scatter(back[0][2], 'dp', scatter_dimension=0, tiled=True)]
    all_to_all x1 -> x2, starting transfers between devices: 3.42 us -> 13.4 us  [the longest x1 7.25 us: row_body(): lifted = lax.all_to_all(lifted, 'dp', 0, 0)]
    pallas_call x4, Pallas kernels: 93.7 us -> 100 us  [attend_bwd(): pl.pallas_call(lambda *refs: attend_bwd_body(final, parts, len(waits), he...]
    all_to_all x1 -> x2, waiting for transfers between devices: 33.5 us -> 32.5 us  [the longest x1 32.5 us: row_body(): mod_part, = tie([lax.all_to_all(mod_part, AXES, 0, 0)], ready)]
    unnamed x107 -> x99, local copies, waits for them, and re-layouts: 15.7 us -> 14.7 us
  transfers between devices with their start and end apart: 29 -> 33, of which waited for: 7 -> 8; matrix products, arithmetic and copies ran while one was open for 10% -> 10% of each run, Pallas kernels for 56% -> 54%
where the time goes in v3:
time: 621 us; the launch traced here: 615 us
  Pallas kernels  356 us (57%)
  waiting for transfers between devices  116 us (19%)
  local copies, waits for them, and re-layouts  45.9 us (7%)
  starting transfers between devices  44.5 us (7%)
  other arithmetic  36.1 us (6%)
  between operations  15 us (2%)
    pallas_call x6, Pallas kernels, mlp_call(): pl.pallas_call(lambda *refs: body(len(waits), *refs), grid=(steps,), in_s...  117 us
    pallas_call x4, Pallas kernels, attend_bwd(): pl.pallas_call(lambda *refs: attend_bwd_body(final, parts, len(waits), he...  100 us
    pallas_call x5, Pallas kernels, by_rows(): pl.pallas_call(body, grid=(n // ET,), in_specs=[SMEM_SPEC] * len(scalars)...  60.6 us
    pallas_call x4, Pallas kernels, attend_fwd(): pl.pallas_call(lambda *refs: attend_fwd_body(heads, *refs), in_specs=[SME...  60.4 us
    ppermute x24, waiting for transfers between devices, swap(): return lax.ppermute(values, AXES, pairs)  42.8 us
    all_to_all x1, waiting for transfers between devices, row_body(): mod_part, = tie([lax.all_to_all(mod_part, AXES, 0, 0)], ready)  32.5 us
    pallas_call x1, Pallas kernels, back_to_input(): pl.pallas_call(back_body, grid=(steps,), in_specs=[pl.BlockSpec((n // ste...  17.7 us
    ppermute x24, starting transfers between devices, swap(): return lax.ppermute(values, AXES, pairs)  17.2 us
  transfers between devices with their start and end apart: 33, of which 8 were waited for; matrix products, arithmetic and copies ran while one was open for 10% of the time, Pallas kernels for 54%

profile of v3, /device:TPU:0, one launch (start us, length us, event | category | flops | bytes accessed | tf_op | source)
XLA Modules:
  0.0 614.9 jit_solution(9071002637814606775)
XLA Ops:
  12.0 7.3 %all-to-all-start = ((bf16[8,16,144]{2,1,0:T(8,128)(2,1)}), bf16[8,16,144]{2,1,0:T(8,128)(2,1)S(1)}, u32[]{:S(2)}, u32[]{:S(2)}) async-start(bf16[8,16,144]{2,1,0:T(8,128)(2,1)} %shard_map.229), calls=%async_computation | async-start | bytes 131072 | tf_op jit(solution)/shard_map/all_to_all | solution.py:1037
  31.9 6.1 all-to-all-start.1
  38.9 3.4 dynamic-slice_bitcast_fusion
  48.0 32.5 %all-to-all-done.1.refs_0_ = f32[32,4,1728]{2,1,0:T(4,128)S(1)} async-done(((f32[32,4,1728]{2,1,0:T(4,128)}), f32[32,4,1728]{2,1,0:T(4,128)S(1)}, u32[]{:S(2)}, u32[]{:S(2)}) %all-to-all-start.1) | async-done | bytes 884768 | tf_op jit(solution)/shard_map/all_to_all | solution.py:1054
  86.3 8.0 %shard_map.233 = (bf16[1024,1152]{1,0:T(8,128)(2,1)}, bf16[1152,1024]{1,0:T(8,128)(2,1)}) custom-call(bf16[1024,1152]{1,0:T(8,128)(2,1)} %pad_maximum_fusion.refs_1_.refs_0_.refs_2_, f32[4,6912]{1,0:T(4,128)} %broadcast_add_fusion.refs_1_.refs_5_.refs_13_, s32[1024,128]{1,0:T(8,128)} %broadcast_in_dim.47.refs_2_.refs_5_.refs_6_.refs_14_.refs_10_, ...), custom_call_target="tpu_custom_call" | custom-call | flops 27599998976 | tf_op jit(solution)/shard_map/pallas_call | solution.py:926
  96.0 14.8 %shard_map.235 = (bf16[1024,864]{1,0:T(8,128)(2,1)}, bf16[1024,288]{1,0:T(8,128)(2,1)}, f32[8,1024]{1,0:T(8,128)}, bf16[1024,1152]{1,0:T(8,128)(2,1)}) custom-call(s32[4]{0:T(128)} %get-tuple-element.157.refs_4_.refs_0_, s32[4]{0:T(128)} %get-tuple-element.156.refs_5_.refs_1_, bf16[1024,1152]{1,0:T(8,128)(2,1)} %get-tuple-element.82.refs_2_, ...), custom_call_target="tpu_custom_call" | custom-call | flops 73600000000 | tf_op jit(solution)/shard_map/pallas_call | solution.py:620
  112.4 15.3 %shard_map.236 = (bf16[1024,864]{1,0:T(8,128)(2,1)}, bf16[1024,288]{1,0:T(8,128)(2,1)}, f32[8,1024]{1,0:T(8,128)}, bf16[1024,1152]{1,0:T(8,128)(2,1)}) custom-call(s32[4]{0:T(128)} %get-tuple-element.157.refs_4_.refs_0_, s32[4]{0:T(128)} %get-tuple-element.156.refs_5_.refs_1_, bf16[1024,1152]{1,0:T(8,128)(2,1)} %get-tuple-element.82.refs_2_, ...), custom_call_target="tpu_custom_call" | custom-call | flops 73600000000 | tf_op jit(solution)/shard_map/pallas_call | solution.py:620
  132.1 7.5 %shard_map.238 = (bf16[1024,1152]{1,0:T(8,128)(2,1)}, bf16[1152,1024]{1,0:T(8,128)(2,1)}, f32[1,1152]{1,0:T(1,128)}) custom-call(bf16[1024,1152]{1,0:T(8,128)(2,1)} %pad_maximum_fusion.1.refs_0_.refs_4_, f32[4,6912]{1,0:T(4,128)} %broadcast_add_fusion.refs_1_.refs_5_.refs_13_, s32[1024,128]{1,0:T(8,128)} %broadcast_in_dim.47.refs_2_.refs_5_.refs_6_.refs_14_.refs_10_, ...), custom_call_target="tpu_custom_call" | custom-call | flops 27599998976 | tf_op jit(solution)/shard_map/pallas_call | solution.py:926
  139.5 14.5 %collective-permute-done.3.refs_0_ = bf16[1152,1152]{1,0:T(8,128)(2,1)} collective-permute-done((bf16[1152,1152]{1,0:T(8,128)(2,1)}, bf16[1152,1152]{1,0:T(8,128)(2,1)}, u32[]{:S(2)}, u32[]{:S(2)}) %collective-permute-start.3) | collective-permute-done | bytes 2654240 | tf_op jit(solution)/shard_map/ppermute | solution.py:392
  154.0 15.2 %shard_map.240 = (bf16[1024,864]{1,0:T(8,128)(2,1)}, bf16[1024,288]{1,0:T(8,128)(2,1)}, f32[8,1024]{1,0:T(8,128)}, bf16[1024,1152]{1,0:T(8,128)(2,1)}) custom-call(s32[4]{0:T(128)} %get-tuple-element.157.refs_4_.refs_0_, s32[4]{0:T(128)} %get-tuple-element.156.refs_5_.refs_1_, bf16[1024,1152]{1,0:T(8,128)(2,1)} %get-tuple-element.82.refs_2_, ...), custom_call_target="tpu_custom_call" | custom-call | flops 73600000000 | tf_op jit(solution)/shard_map/pallas_call | solution.py:620
  173.8 15.0 %shard_map.242 = (bf16[1024,864]{1,0:T(8,128)(2,1)}, bf16[1024,288]{1,0:T(8,128)(2,1)}, f32[8,1024]{1,0:T(8,128)}, bf16[1024,1152]{1,0:T(8,128)(2,1)}) custom-call(s32[4]{0:T(128)} %get-tuple-element.157.refs_4_.refs_0_, s32[4]{0:T(128)} %get-tuple-element.156.refs_5_.refs_1_, bf16[1024,1152]{1,0:T(8,128)(2,1)} %get-tuple-element.82.refs_2_, ...), custom_call_target="tpu_custom_call" | custom-call | flops 73600000000 | tf_op jit(solution)/shard_map/pallas_call | solution.py:620
  188.8 12.7 %shard_map.243 = (f32[1024,1152]{1,0:T(8,128)}, f32[1024,1152]{1,0:T(8,128)}, bf16[1024,1152]{1,0:T(8,128)(2,1)}, bf16[1152,1024]{1,0:T(8,128)(2,1)}) custom-call(bf16[1024,1152]{1,0:T(8,128)(2,1)} %pad_maximum_fusion.refs_1_.refs_0_.refs_2_, bf16[1024,1152]{1,0:T(8,128)(2,1)} %get-tuple-element.83.refs_1_, bf16[1024,1152]{1,0:T(8,128)(2,1)} %get-tuple-element.85.refs_2_, ...), custom_call_target="tpu_custom_call" | custom-call | flops 55199997952 | tf_op jit(solution)/shard_map/pallas_call | solution.py:926
  201.5 26.9 %shard_map.244 = (bf16[1024,1152]{1,0:T(8,128)(2,1)}, bf16[1024,1152]{1,0:T(8,128)(2,1)}, f32[1,1152]{1,0:T(1,128)}, bf16[1152,2304]{1,0:T(8,128)(2,1)}) custom-call(bf16[1024,1152]{1,0:T(8,128)(2,1)} %get-tuple-element.93.refs_0_, bf16[1024,1152]{1,0:T(8,128)(2,1)} %get-tuple-element.94.refs_1_, bf16[1152,1024]{1,0:T(8,128)(2,1)} %get-tuple-element.95.refs_2_.refs_0_, ...), custom_call_target="tpu_custom_call" | custom-call | flops 124200001536 | tf_op jit(solution)/shard_map/pallas_call | solution.py:483
  228.4 19.7 %shard_map.245 = (bf16[1024,1152]{1,0:T(8,128)(2,1)}, bf16[1024,1152]{1,0:T(8,128)(2,1)}, f32[1,1152]{1,0:T(1,128)}, bf16[1024,1152]{1,0:T(8,128)(2,1)}, bf16[1024,1152]{1,0:T(8,128)(2,1)}) custom-call(bf16[1024,1152]{1,0:T(8,128)(2,1)} %get-tuple-element.93.refs_0_, bf16[1024,1152]{1,0:T(8,128)(2,1)} %get-tuple-element.94.refs_1_, ...), custom_call_target="tpu_custom_call" | custom-call | flops 87399997440 | tf_op jit(solution)/shard_map/pallas_call | solution.py:483
  248.1 12.1 %all-gather.8.cloned.1.call-done.refs_0_ = bf16[1152,2304]{1,0:T(8,128)(2,1)} async-done(((bf16[144,2304]{1,0:T(8,128)(2,1)}), bf16[1152,2304]{1,0:T(8,128)(2,1)}) %all-gather.8.cloned.1.call-update) | async-done | bytes 5308432 | tf_op jit(solution)/shard_map/all_gather | solution.py:1060
  262.4 11.8 %shard_map.247.refs_7_ = bf16[1152,2304]{1,0:T(8,128)(2,1)} custom-call(bf16[1152,1024]{1,0:T(8,128)(2,1)} %get-tuple-element.95.refs_2_.refs_0_, bf16[1152,1024]{1,0:T(8,128)(2,1)} %get-tuple-element.96.refs_3_.refs_1_, bf16[1024,1152]{1,0:T(8,128)(2,1)} %get-tuple-element.99.refs_2_, bf16[1024,1152]{1,0:T(8,128)(2,1)} %get-tuple-element.100.refs_3_, ...), custom_call_target="tpu_custom_call" | custom-call | flops 55199997952 | tf_op jit(solution)/shard_map/pallas_call | solution.py:483
  274.3 26.9 %shard_map.248 = (bf16[1024,1152]{1,0:T(8,128)(2,1)}, bf16[1024,1152]{1,0:T(8,128)(2,1)}, f32[1,1152]{1,0:T(1,128)}, bf16[1152,2304]{1,0:T(8,128)(2,1)}) custom-call(bf16[1024,1152]{1,0:T(8,128)(2,1)} %get-tuple-element.93.refs_0_, bf16[1024,1152]{1,0:T(8,128)(2,1)} %get-tuple-element.94.refs_1_, bf16[1152,1024]{1,0:T(8,128)(2,1)} %get-tuple-element.95.refs_2_.refs_0_, ...), custom_call_target="tpu_custom_call" | custom-call | flops 124200001536 | tf_op jit(solution)/shard_map/pallas_call | solution.py:483
  301.4 19.4 %shard_map.249 = (bf16[1024,1152]{1,0:T(8,128)(2,1)}, bf16[1024,1152]{1,0:T(8,128)(2,1)}, f32[1,1152]{1,0:T(1,128)}, bf16[1024,1152]{1,0:T(8,128)(2,1)}, bf16[1024,1152]{1,0:T(8,128)(2,1)}) custom-call(bf16[1024,1152]{1,0:T(8,128)(2,1)} %get-tuple-element.93.refs_0_, bf16[1024,1152]{1,0:T(8,128)(2,1)} %get-tuple-element.94.refs_1_, ...), custom_call_target="tpu_custom_call" | custom-call | flops 87399997440 | tf_op jit(solution)/shard_map/pallas_call | solution.py:483
  323.1 12.0 %shard_map.250.refs_16_ = bf16[1152,2304]{1,0:T(8,128)(2,1)} custom-call(bf16[1152,1024]{1,0:T(8,128)(2,1)} %get-tuple-element.95.refs_2_.refs_0_, bf16[1152,1024]{1,0:T(8,128)(2,1)} %get-tuple-element.96.refs_3_.refs_1_, bf16[1024,1152]{1,0:T(8,128)(2,1)} %get-tuple-element.111.refs_2_, bf16[1024,1152]{1,0:T(8,128)(2,1)} %get-tuple-element.112.refs_3_, ...), custom_call_target="tpu_custom_call" | custom-call | flops 55199997952 | tf_op jit(solution)/shard_map/pallas_call | solution.py:483
  335.1 21.5 %shard_map.251 = (bf16[1024,1152]{1,0:T(8,128)(2,1)}, f32[1024,1152]{1,0:T(8,128)}, bf16[1024,1152]{1,0:T(8,128)(2,1)}, bf16[1152,1024]{1,0:T(8,128)(2,1)}, f32[1,1152]{1,0:T(1,128)}, /*index=5*/f32[4,4608]{1,0:T(4,128)}) custom-call(s32[8]{0:T(128)} %get-tuple-element.155.refs_6_.refs_0_, s32[8]{0:T(128)} %get-tuple-element.154.refs_7_.refs_1_, ...), custom_call_target="tpu_custom_call" | custom-call | flops 23000000512 | tf_op jit(solution)/shard_map/pallas_call | solution.py:926
  358.4 24.7 %shard_map.252 = (bf16[1024,864]{1,0:T(8,128)(2,1)}, f32[1,864]{1,0:T(1,128)}, bf16[1152,1152]{1,0:T(8,128)(2,1)}) custom-call(s32[4]{0:T(128)} %get-tuple-element.157.refs_4_.refs_0_, s32[4]{0:T(128)} %get-tuple-element.156.refs_5_.refs_1_, s32[8]{0:T(128)} %shift-right-arithmetic_add_fusion.refs_2_, bf16[1024,864]{1,0:T(8,128)(2,1)} %get-tuple-element.115.refs_3_, ...), custom_call_target="tpu_custom_call" | custom-call | flops 32199999488 | tf_op jit(solution)/shard_map/pallas_call | solution.py:769
  385.3 24.7 %shard_map.254 = (bf16[1024,864]{1,0:T(8,128)(2,1)}, f32[1,864]{1,0:T(1,128)}, bf16[1152,1152]{1,0:T(8,128)(2,1)}) custom-call(s32[4]{0:T(128)} %get-tuple-element.157.refs_4_.refs_0_, s32[4]{0:T(128)} %get-tuple-element.156.refs_5_.refs_1_, s32[8]{0:T(128)} %shift-right-arithmetic_add_fusion.refs_2_, bf16[1024,864]{1,0:T(8,128)(2,1)} %get-tuple-element.127.refs_3_, ...), custom_call_target="tpu_custom_call" | custom-call | flops 32199999488 | tf_op jit(solution)/shard_map/pallas_call | solution.py:769
  412.9 3.5 all-to-all-start.2
  420.4 25.3 %shard_map.255 = (bf16[1024,864]{1,0:T(8,128)(2,1)}, f32[1,864]{1,0:T(1,128)}, bf16[4,144,1152]{2,1,0:T(8,128)(2,1)}, bf16[4,144,1152]{2,1,0:T(8,128)(2,1)}) custom-call(s32[4]{0:T(128)} %get-tuple-element.157.refs_4_.refs_0_, s32[4]{0:T(128)} %get-tuple-element.156.refs_5_.refs_1_, s32[8]{0:T(128)} %shift-right-arithmetic_add_fusion.refs_2_, ...), custom_call_target="tpu_custom_call" | custom-call | flops 32199999488 | tf_op jit(solution)/shard_map/pallas_call | solution.py:769
  447.3 25.6 %shard_map.256 = (bf16[1024,864]{1,0:T(8,128)(2,1)}, f32[1,864]{1,0:T(1,128)}, bf16[4,144,1152]{2,1,0:T(8,128)(2,1)}, bf16[4,144,1152]{2,1,0:T(8,128)(2,1)}) custom-call(s32[4]{0:T(128)} %get-tuple-element.157.refs_4_.refs_0_, s32[4]{0:T(128)} %get-tuple-element.156.refs_5_.refs_1_, s32[8]{0:T(128)} %shift-right-arithmetic_add_fusion.refs_2_, ...), custom_call_target="tpu_custom_call" | custom-call | flops 32199999488 | tf_op jit(solution)/shard_map/pallas_call | solution.py:769
  476.8 17.8 %collective-permute-done.13.refs_0_ = bf16[4,144,1152]{2,1,0:T(8,128)(2,1)S(1)} collective-permute-done((bf16[4,144,1152]{2,1,0:T(8,128)(2,1)}, bf16[4,144,1152]{2,1,0:T(8,128)(2,1)S(1)}, u32[]{:S(2)}, u32[]{:S(2)}) %collective-permute-start.13) | collective-permute-done | bytes 1327136 | tf_op jit(solution)/shard_map/ppermute | solution.py:392
  505.1 17.7 %shard_map.258.refs_1_.refs_4_ = f32[1024,1152]{1,0:T(8,128)} custom-call(bf16[1024,864]{1,0:T(8,128)(2,1)} %get-tuple-element.133.q0, bf16[1024,864]{1,0:T(8,128)(2,1)} %get-tuple-element.134.q1, bf16[1024,864]{1,0:T(8,128)(2,1)} %get-tuple-element.135.q2, bf16[1024,864]{1,0:T(8,128)(2,1)} %get-tuple-element.136.q3, ...), custom_call_target="tpu_custom_call" | custom-call | flops 4600000000 | tf_op jit(solution)/shard_map/pallas_call | solution.py:891
  522.8 10.5 %collective-permute-done.15.refs_0_ = bf16[4,144,1152]{2,1,0:T(8,128)(2,1)S(1)} collective-permute-done((bf16[4,144,1152]{2,1,0:T(8,128)(2,1)}, bf16[4,144,1152]{2,1,0:T(8,128)(2,1)S(1)}, u32[]{:S(2)}, u32[]{:S(2)}) %collective-permute-start.15) | collective-permute-done | bytes 1327136 | tf_op jit(solution)/shard_map/ppermute | solution.py:392
  540.0 12.9 %reduce-scatter.5.cloned.1.call-done.refs_8_ = bf16[144,2304]{1,0:T(8,128)(2,1)} async-done(((bf16[1152,2304]{1,0:T(8,128)(2,1)}), bf16[144,2304]{1,0:T(8,128)(2,1)}) %reduce-scatter.5.cloned.1.call-update) | async-done | bytes 663568 | tf_op jit(solution)/shard_map/reduce_scatter | solution.py:1120
  552.9 11.0 %shard_map.260 = (bf16[1024,1152]{1,0:T(8,128)(2,1)}, f32[4,2304]{1,0:T(4,128)}) custom-call(s32[8]{0:T(128)} %get-tuple-element.155.refs_6_.refs_0_, s32[8]{0:T(128)} %get-tuple-element.154.refs_7_.refs_1_, bf16[1024,1152]{1,0:T(8,128)(2,1)} %pad_maximum_fusion.refs_1_.refs_0_.refs_2_, f32[1024,1152]{1,0:T(8,128)} %get-tuple-element.121.refs_3_, ...), custom_call_target="tpu_custom_call" | custom-call | flops 4600000000 | tf_op jit(solution)/shard_map/pallas_call | solution.py:926
  571.7 9.9 %all-to-all-start.3 = ((bf16[32,93,128]{2,1,0:T(8,128)(2,1)}), bf16[32,93,128]{2,1,0:T(8,128)(2,1)S(1)}, u32[]{:S(2)}, u32[]{:S(2)}) async-start(bf16[32,93,128]{2,1,0:T(8,128)(2,1)} %pad_maximum_fusion.4), calls=%async_computation.5 | async-start | bytes 1572864 | tf_op jit(solution)/shard_map/all_to_all | solution.py:992
  590.4 11.8 %all-to-all-done.3 = bf16[32,93,128]{2,1,0:T(8,128)(2,1)S(1)} async-done(((bf16[32,93,128]{2,1,0:T(8,128)(2,1)}), bf16[32,93,128]{2,1,0:T(8,128)(2,1)S(1)}, u32[]{:S(2)}, u32[]{:S(2)}) %all-to-all-start.3) | async-done | bytes 761888 | tf_op jit(solution)/shard_map/all_to_all | solution.py:992
  (290 shorter events, 101.9 us)
Async XLA Ops:
  7.2 87.0 %all-gather.4.cloned.1.call-start = ((), (), s32[]{:S(2)}) async-start(), calls=%async_computation.6 | async-start | bytes 2985984 | tf_op jit(solution)/shard_map/all_gather | solution.py:1024
  12.0 18.0 %all-to-all-start = ((bf16[8,16,144]{2,1,0:T(8,128)(2,1)}), bf16[8,16,144]{2,1,0:T(8,128)(2,1)S(1)}, u32[]{:S(2)}, u32[]{:S(2)}) async-start(bf16[8,16,144]{2,1,0:T(8,128)(2,1)} %shard_map.229), calls=%async_computation | async-start | bytes 131072 | tf_op jit(solution)/shard_map/all_to_all | solution.py:1037
  20.4 24.5 %collective-permute-start = (bf16[512,1152]{1,0:T(8,128)(2,1)}, bf16[512,1152]{1,0:T(8,128)(2,1)S(1)}, u32[]{:S(2)}, u32[]{:S(2)}) collective-permute-start(bf16[512,1152]{1,0:T(8,128)(2,1)} %dynamic-slice_bitcast_fusion.2), channel_id=1, source_target_pairs={{0,1},{1,0},{2,3},{3,2},{4,5},{5,4},{6,7},{7,6},{8,9},{9,8},{10,11... | collective-permute-start | bytes 3538952 | tf_op jit(solution)/shard_map/ppermute | solution.py:392
  31.9 48.6 %all-to-all-start.1 = ((f32[32,4,1728]{2,1,0:T(4,128)}), f32[32,4,1728]{2,1,0:T(4,128)S(1)}, u32[]{:S(2)}, u32[]{:S(2)}) async-start(f32[32,4,1728]{2,1,0:T(4,128)} %copy.73.refs_1_), calls=%async_computation.1 | async-start | bytes 1835008 | tf_op jit(solution)/shard_map/all_to_all | solution.py:1054
  38.1 134.1 %all-gather.6.cloned.1.call-start = ((), (), s32[]{:S(2)}) async-start(), calls=%async_computation.7 | async-start | bytes 5971968 | tf_op jit(solution)/shard_map/all_gather | solution.py:1059
  43.1 41.2 %collective-permute-start.1 = (bf16[144,2304]{1,0:T(8,128)(2,1)}, bf16[144,2304]{1,0:T(8,128)(2,1)S(1)}, u32[]{:S(2)}, u32[]{:S(2)}) collective-permute-start(bf16[144,2304]{1,0:T(8,128)(2,1)} %shard_map.231), channel_id=1, source_target_pairs={{0,2},{1,3},{2,0},{3,1},{4,6},{5,7},{6,4},{7,5},{8,10},{9,11},{10,... | collective-permute-start | bytes 1990664 | tf_op jit(solution)/shard_map/ppermute | solution.py:392
  85.2 175.0 %all-gather.8.cloned.1.call-start = ((), (), s32[]{:S(2)}) async-start(), calls=%async_computation.8 | async-start | bytes 5971968 | tf_op jit(solution)/shard_map/all_gather | solution.py:1060
  85.2 42.5 %collective-permute-start.4 = (bf16[512,1152]{1,0:T(8,128)(2,1)}, bf16[512,1152]{1,0:T(8,128)(2,1)}, u32[]{:S(2)}, u32[]{:S(2)}) collective-permute-start(bf16[512,1152]{1,0:T(8,128)(2,1)} %get-tuple-element.178), channel_id=1, source_target_pairs={{0,1},{1,0},{2,3},{3,2},{4,5},{5,4},{6,7},{7,6},{8,9},{9,8},{10,11... | collective-permute-start | bytes 3538952 | tf_op jit(solution)/shard_map/ppermute | solution.py:392
  85.9 299.4 %reduce-scatter.3.cloned.1.call-start = ((), (), s32[]{:S(2)}) async-start(), calls=%async_computation.9 | async-start | bytes 5971968 | tf_op jit(solution)/shard_map/reduce_scatter | solution.py:1115
  94.3 59.8 %collective-permute-start.3 = (bf16[1152,1152]{1,0:T(8,128)(2,1)}, bf16[1152,1152]{1,0:T(8,128)(2,1)}, u32[]{:S(2)}, u32[]{:S(2)}) collective-permute-start(bf16[1152,1152]{1,0:T(8,128)(2,1)} %shard_map.234.refs_3_.refs_8_.w0), channel_id=1, source_target_pairs={{0,2},{1,3},{2,0},{3,1},{4,6},{5,7},{6,4},{7,5},{8,10},{9,11},{10,... | collective-permute-start | bytes 7962632 | tf_op jit(solution)/shard_map/ppermute | solution.py:392
  96.0 14.8 %collective-permute-start.2 = (bf16[1152,1152]{1,0:T(8,128)(2,1)}, bf16[1152,1152]{1,0:T(8,128)(2,1)S(1)}, u32[]{:S(2)}, u32[]{:S(2)}) collective-permute-start(bf16[1152,1152]{1,0:T(8,128)(2,1)} %shard_map.234.refs_3_.refs_8_.w0), channel_id=1, source_target_pairs={{0,1},{1,0},{2,3},{3,2},{4,5},{5,4},{6,7},{7,6},{8,9},{9,8},{10,11... | collective-permute-start | bytes 7962632 | tf_op jit(solution)/shard_map/ppermute | solution.py:392
  154.0 18.2 %collective-permute-start.5 = (bf16[1152,1152]{1,0:T(8,128)(2,1)}, bf16[1152,1152]{1,0:T(8,128)(2,1)S(1)}, u32[]{:S(2)}, u32[]{:S(2)}) collective-permute-start(bf16[1152,1152]{1,0:T(8,128)(2,1)} %shard_map.239.refs_3_.refs_8_.w2), channel_id=1, source_target_pairs={{0,1},{1,0},{2,3},{3,2},{4,5},{5,4},{6,7},{7,6},{8,9},{9,8},{10,11... | collective-permute-start | bytes 7962632 | tf_op jit(solution)/shard_map/ppermute | solution.py:392
  172.2 29.3 %collective-permute-start.6 = (bf16[1152,2304]{1,0:T(8,128)(2,1)}, bf16[1152,2304]{1,0:T(8,128)(2,1)}, u32[]{:S(2)}, u32[]{:S(2)}) collective-permute-start(bf16[1152,2304]{1,0:T(8,128)(2,1)} %shard_map.241.refs_8_.refs_2_.refs_3_), channel_id=1, source_target_pairs={{0,1},{1,0},{2,3},{3,2},{4,5},{5,4},{6,7},{7,6},{8,9},{9,8},{10,11... | collective-permute-start | bytes 15925256 | tf_op jit(solution)/shard_map/ppermute | solution.py:392
  228.4 34.0 %collective-permute-start.8 = (bf16[1152,2304]{1,0:T(8,128)(2,1)}, bf16[1152,2304]{1,0:T(8,128)(2,1)}, u32[]{:S(2)}, u32[]{:S(2)}) collective-permute-start(bf16[1152,2304]{1,0:T(8,128)(2,1)} %get-tuple-element.101), channel_id=1, source_target_pairs={{0,1},{1,0},{2,3},{3,2},{4,5},{5,4},{6,7},{7,6},{8,9},{9,8},{10,11... | collective-permute-start | bytes 15925256 | tf_op jit(solution)/shard_map/ppermute | solution.py:392
  260.3 14.0 %collective-permute-start.7 = (bf16[1152,2304]{1,0:T(8,128)(2,1)}, bf16[1152,2304]{1,0:T(8,128)(2,1)}, u32[]{:S(2)}, u32[]{:S(2)}) collective-permute-start(bf16[1152,2304]{1,0:T(8,128)(2,1)} %shard_map.246.refs_5_.refs_2_.refs_3_), channel_id=1, source_target_pairs={{0,1},{1,0},{2,3},{3,2},{4,5},{5,4},{6,7},{7,6},{8,9},{9,8},{10,11... | collective-permute-start | bytes 15925256 | tf_op jit(solution)/shard_map/ppermute | solution.py:392
  274.2 278.7 %reduce-scatter.5.cloned.1.call-start = ((), (), s32[]{:S(2)}) async-start(), calls=%async_computation.10 | async-start | bytes 5971968 | tf_op jit(solution)/shard_map/reduce_scatter | solution.py:1120
  301.2 19.6 %collective-permute-start.9 = (bf16[1152,2304]{1,0:T(8,128)(2,1)}, bf16[1152,2304]{1,0:T(8,128)(2,1)S(1)}, u32[]{:S(2)}, u32[]{:S(2)}) collective-permute-start(bf16[1152,2304]{1,0:T(8,128)(2,1)} %get-tuple-element.113), channel_id=1, source_target_pairs={{0,1},{1,0},{2,3},{3,2},{4,5},{5,4},{6,7},{7,6},{8,9},{9,8},{10,11... | collective-permute-start | bytes 15925256 | tf_op jit(solution)/shard_map/ppermute | solution.py:392
  358.0 25.1 %collective-permute-start.10 = (bf16[512,1152]{1,0:T(8,128)(2,1)S(1)}, bf16[512,1152]{1,0:T(8,128)(2,1)S(1)}, u32[]{:S(2)}, u32[]{:S(2)}) collective-permute-start(bf16[512,1152]{1,0:T(8,128)(2,1)S(1)} %constant_dynamic-slice_fusion.1), channel_id=1, source_target_pairs={{0,1},{1,0},{2,3},{3,2},{4,5},{5,4},{6,7},{7,6},{8,9},{9,8},{10,11... | collective-permute-start | bytes 3538952 | tf_op jit(solution)/shard_map/ppermute | solution.py:392
  410.0 8.8 %collective-permute-start.12 = (bf16[1152,1152]{1,0:T(8,128)(2,1)}, bf16[1152,1152]{1,0:T(8,128)(2,1)S(1)}, u32[]{:S(2)}, u32[]{:S(2)}) collective-permute-start(bf16[1152,1152]{1,0:T(8,128)(2,1)} %get-tuple-element.130), channel_id=1, source_target_pairs={{0,1},{1,0},{2,3},{3,2},{4,5},{5,4},{6,7},{7,6},{8,9},{9,8},{10,11... | collective-permute-start | bytes 7962632 | tf_op jit(solution)/shard_map/ppermute | solution.py:392
  412.9 60.8 %all-to-all-start.2 = ((bf16[32,57,128]{2,1,0:T(8,128)(2,1)}), bf16[32,57,128]{2,1,0:T(8,128)(2,1)}, u32[]{:S(2)}, u32[]{:S(2)}) async-start(bf16[32,57,128]{2,1,0:T(8,128)(2,1)} %pad_maximum_fusion.7), calls=%async_computation.4 | async-start | bytes 1048576 | tf_op jit(solution)/shard_map/all_to_all | solution.py:992
  416.4 29.4 %collective-permute-start.11 = (bf16[1152,1152]{1,0:T(8,128)(2,1)}, bf16[1152,1152]{1,0:T(8,128)(2,1)S(1)}, u32[]{:S(2)}, u32[]{:S(2)}) collective-permute-start(bf16[1152,1152]{1,0:T(8,128)(2,1)} %get-tuple-element.124), channel_id=1, source_target_pairs={{0,1},{1,0},{2,3},{3,2},{4,5},{5,4},{6,7},{7,6},{8,9},{9,8},{10,11... | collective-permute-start | bytes 7962632 | tf_op jit(solution)/shard_map/ppermute | solution.py:392
  416.8 60.0 %collective-permute-start.14 = (bf16[144,2304]{1,0:T(8,128)(2,1)}, bf16[144,2304]{1,0:T(8,128)(2,1)}, u32[]{:S(2)}, u32[]{:S(2)}) collective-permute-start(bf16[144,2304]{1,0:T(8,128)(2,1)} %reduce-scatter.3.cloned.1.call-done.refs_14_), channel_id=1, source_target_pairs={{0,2},{1,3},{2,0},{3,1},{4,6},{5,7},{6,4},{7,5},{8,10},{9,11},{10,... | collective-permute-start | bytes 1990664 | tf_op jit(solution)/shard_map/ppermute | solution.py:392
  445.7 49.0 %collective-permute-start.13 = (bf16[4,144,1152]{2,1,0:T(8,128)(2,1)}, bf16[4,144,1152]{2,1,0:T(8,128)(2,1)S(1)}, u32[]{:S(2)}, u32[]{:S(2)}) collective-permute-start(bf16[4,144,1152]{2,1,0:T(8,128)(2,1)} %get-tuple-element.138), channel_id=1, source_target_pairs={{0,4},{1,5},{2,6},{3,7},{4,0},{5,1},{6,2},{7,3},{8,12},{9,13},{10,... | collective-permute-start | bytes 3981320 | tf_op jit(solution)/shard_map/ppermute | solution.py:392
  472.9 60.4 %collective-permute-start.15 = (bf16[4,144,1152]{2,1,0:T(8,128)(2,1)}, bf16[4,144,1152]{2,1,0:T(8,128)(2,1)S(1)}, u32[]{:S(2)}, u32[]{:S(2)}) collective-permute-start(bf16[4,144,1152]{2,1,0:T(8,128)(2,1)} %get-tuple-element.142), channel_id=1, source_target_pairs={{0,4},{1,5},{2,6},{3,7},{4,0},{5,1},{6,2},{7,3},{8,12},{9,13},{10,... | collective-permute-start | bytes 3981320 | tf_op jit(solution)/shard_map/ppermute | solution.py:392
  500.7 64.4 %collective-permute-start.22 = (bf16[144,1152]{1,0:T(8,128)(2,1)}, bf16[144,1152]{1,0:T(8,128)(2,1)S(1)}, u32[]{:S(2)}, u32[]{:S(2)}) collective-permute-start(bf16[144,1152]{1,0:T(8,128)(2,1)} %get-tuple-element.172), channel_id=1, source_target_pairs={{0,24},{1,25},{2,26},{3,27},{4,28},{5,29},{6,30},{7,31},{8,16},{9,... | collective-permute-start | bytes 995336 | tf_op jit(solution)/shard_map/ppermute | solution.py:392
  502.0 63.3 %collective-permute-start.21 = (bf16[144,1152]{1,0:T(8,128)(2,1)}, bf16[144,1152]{1,0:T(8,128)(2,1)S(1)}, u32[]{:S(2)}, u32[]{:S(2)}) collective-permute-start(bf16[144,1152]{1,0:T(8,128)(2,1)} %get-tuple-element.173), channel_id=1, source_target_pairs={{0,16},{1,17},{2,18},{3,19},{4,20},{5,21},{6,22},{7,23},{8,24},{9,... | collective-permute-start | bytes 995336 | tf_op jit(solution)/shard_map/ppermute | solution.py:392
  502.0 63.3 %collective-permute-start.20 = (bf16[144,1152]{1,0:T(8,128)(2,1)}, bf16[144,1152]{1,0:T(8,128)(2,1)}, u32[]{:S(2)}, u32[]{:S(2)}) collective-permute-start(bf16[144,1152]{1,0:T(8,128)(2,1)} %get-tuple-element.174), channel_id=1, source_target_pairs={{0,8},{1,9},{2,10},{3,11},{4,12},{5,13},{6,14},{7,15},{8,0},{9,1},... | collective-permute-start | bytes 995336 | tf_op jit(solution)/shard_map/ppermute | solution.py:392
  537.2 47.5 %collective-permute-start.17 = (bf16[144,1152]{1,0:T(8,128)(2,1)S(1)}, bf16[144,1152]{1,0:T(8,128)(2,1)}, u32[]{:S(2)}, u32[]{:S(2)}) collective-permute-start(bf16[144,1152]{1,0:T(8,128)(2,1)S(1)} %get-tuple-element.168), channel_id=1, source_target_pairs={{0,8},{1,9},{2,10},{3,11},{4,12},{5,13},{6,14},{7,15},{8,0},{9,1},... | collective-permute-start | bytes 995336 | tf_op jit(solution)/shard_map/ppermute | solution.py:392
  538.0 46.8 %collective-permute-start.19 = (bf16[144,1152]{1,0:T(8,128)(2,1)S(1)}, bf16[144,1152]{1,0:T(8,128)(2,1)}, u32[]{:S(2)}, u32[]{:S(2)}) collective-permute-start(bf16[144,1152]{1,0:T(8,128)(2,1)S(1)} %get-tuple-element.169), channel_id=1, source_target_pairs={{0,24},{1,25},{2,26},{3,27},{4,28},{5,29},{6,30},{7,31},{8,16},{9,... | collective-permute-start | bytes 995336 | tf_op jit(solution)/shard_map/ppermute | solution.py:392
  565.1 19.6 %collective-permute-start.18 = (bf16[144,1152]{1,0:T(8,128)(2,1)S(1)}, bf16[144,1152]{1,0:T(8,128)(2,1)}, u32[]{:S(2)}, u32[]{:S(2)}) collective-permute-start(bf16[144,1152]{1,0:T(8,128)(2,1)S(1)} %get-tuple-element.170), channel_id=1, source_target_pairs={{0,16},{1,17},{2,18},{3,19},{4,20},{5,21},{6,22},{7,23},{8,24},{9,... | collective-permute-start | bytes 995336 | tf_op jit(solution)/shard_map/ppermute | solution.py:392
  568.3 16.4 %collective-permute-start.23 = (bf16[144,1152]{1,0:T(8,128)(2,1)}, bf16[144,1152]{1,0:T(8,128)(2,1)S(1)}, u32[]{:S(2)}, u32[]{:S(2)}) collective-permute-start(bf16[144,1152]{1,0:T(8,128)(2,1)} %add_convert_fusion), channel_id=1, source_target_pairs={{0,2},{1,3},{2,0},{3,1},{4,6},{5,7},{6,4},{7,5},{8,10},{9,11},{10,... | collective-permute-start | bytes 995336 | tf_op jit(solution)/shard_map/ppermute | solution.py:392
  571.7 30.5 %all-to-all-start.3 = ((bf16[32,93,128]{2,1,0:T(8,128)(2,1)}), bf16[32,93,128]{2,1,0:T(8,128)(2,1)S(1)}, u32[]{:S(2)}, u32[]{:S(2)}) async-start(bf16[32,93,128]{2,1,0:T(8,128)(2,1)} %pad_maximum_fusion.4), calls=%async_computation.5 | async-start | bytes 1572864 | tf_op jit(solution)/shard_map/all_to_all | solution.py:992
  (42 other events, 288.5 us)
Sparse Core Ops, SparseCore 0:
  10.5 72.7 all-gather.3
  86.1 86.0 all-gather.5
  175.0 85.2 all-gather.7
  274.3 102.3 reduce-scatter.2
  410.4 142.4 reduce-scatter.4

commit v4 on v3

--- a/solution.py
+++ b/solution.py
@@ -774,7 +774,7 @@
         out_shape=out_shape,
         scratch_shapes=scratch,
         compiler_params=compiler_params(),
-        cost_estimate=cost(7),
+        cost_estimate=cost(1),
     )(*operands, *waits)
 
 

time: 621 us -> 596 us (0.960)
  waiting for transfers between devices: 116 us -> 106 us
  Pallas kernels: 356 us -> 348 us
    reduce_scatter x1, waiting for transfers between devices: 12.9 us -> 2.59 us  [row_body(): near_sum = lax.psum_scatter(grad, 'dp', scatter_dimension=0, tiled=True)]
    all_to_all x2, waiting for transfers between devices: 11.8 us -> 2.76 us  [to_owners(): lax.all_to_all(jnp.concatenate(parts, axis=1), AXES, 0, 0, tiled=True)]
    ppermute x24, waiting for transfers between devices: 42.8 us -> 51 us  [swap(): return lax.ppermute(values, AXES, pairs)]
    unnamed x99 -> x95, local copies, waits for them, and re-layouts: 14.7 us -> 12.3 us
  transfers between devices with their start and end apart: 33 -> 33, of which waited for: 8 -> 9; matrix products, arithmetic and copies ran while one was open for 10% -> 10% of each run, Pallas kernels for 54% -> 59%
where the time goes in v4:
time: 596 us; the launch traced here: 591 us
  Pallas kernels  348 us (58%)
  waiting for transfers between devices  106 us (18%)
  local copies, waits for them, and re-layouts  43.4 us (7%)
  starting transfers between devices  41.3 us (7%)
  other arithmetic  35.5 us (6%)
  between operations  15 us (3%)
    pallas_call x6, Pallas kernels, mlp_call(): pl.pallas_call(lambda *refs: body(len(waits), *refs), grid=(steps,), in_s...  117 us
    pallas_call x4, Pallas kernels, attend_bwd(): pl.pallas_call(lambda *refs: attend_bwd_body(final, parts, len(waits), he...  94.9 us
    pallas_call x5, Pallas kernels, by_rows(): pl.pallas_call(body, grid=(n // ET,), in_specs=[SMEM_SPEC] * len(scalars)...  61 us
    pallas_call x4, Pallas kernels, attend_fwd(): pl.pallas_call(lambda *refs: attend_fwd_body(heads, *refs), in_specs=[SME...  57.4 us
    ppermute x24, waiting for transfers between devices, swap(): return lax.ppermute(values, AXES, pairs)  51 us
    all_to_all x1, waiting for transfers between devices, row_body(): mod_part, = tie([lax.all_to_all(mod_part, AXES, 0, 0)], ready)  32.5 us
    pallas_call x1, Pallas kernels, back_to_input(): pl.pallas_call(back_body, grid=(steps,), in_specs=[pl.BlockSpec((n // ste...  17.8 us
    ppermute x24, starting transfers between devices, swap(): return lax.ppermute(values, AXES, pairs)  17.5 us
  transfers between devices with their start and end apart: 33, of which 9 were waited for; matrix products, arithmetic and copies ran while one was open for 10% of the time, Pallas kernels for 59%

profile of v4, /device:TPU:0, one launch (start us, length us, event | category | flops | bytes accessed | tf_op | source)
XLA Modules:
  0.0 590.6 jit_solution(12175422968765012431)
XLA Ops:
  12.0 7.3 %all-to-all-start = ((bf16[8,16,144]{2,1,0:T(8,128)(2,1)}), bf16[8,16,144]{2,1,0:T(8,128)(2,1)S(1)}, u32[]{:S(2)}, u32[]{:S(2)}) async-start(bf16[8,16,144]{2,1,0:T(8,128)(2,1)} %shard_map.229), calls=%async_computation | async-start | bytes 131072 | tf_op jit(solution)/shard_map/all_to_all | solution.py:1037
  32.0 6.1 %all-to-all-start.1 = ((f32[32,4,1728]{2,1,0:T(4,128)}), f32[32,4,1728]{2,1,0:T(4,128)S(1)}, u32[]{:S(2)}, u32[]{:S(2)}) async-start(f32[32,4,1728]{2,1,0:T(4,128)} %copy.73.refs_1_), calls=%async_computation.1 | async-start | bytes 1835008 | tf_op jit(solution)/shard_map/all_to_all | solution.py:1054
  48.0 32.5 %all-to-all-done.1.refs_0_ = f32[32,4,1728]{2,1,0:T(4,128)S(1)} async-done(((f32[32,4,1728]{2,1,0:T(4,128)}), f32[32,4,1728]{2,1,0:T(4,128)S(1)}, u32[]{:S(2)}, u32[]{:S(2)}) %all-to-all-start.1) | async-done | bytes 884768 | tf_op jit(solution)/shard_map/all_to_all | solution.py:1054
  86.3 8.0 %shard_map.233 = (bf16[1024,1152]{1,0:T(8,128)(2,1)}, bf16[1152,1024]{1,0:T(8,128)(2,1)}) custom-call(bf16[1024,1152]{1,0:T(8,128)(2,1)} %pad_maximum_fusion.refs_1_.refs_0_.refs_2_, f32[4,6912]{1,0:T(4,128)} %broadcast_add_fusion.refs_1_.refs_5_.refs_13_, s32[1024,128]{1,0:T(8,128)} %broadcast_in_dim.47.refs_2_.refs_5_.refs_6_.refs_14_.refs_10_, ...), custom_call_target="tpu_custom_call" | custom-call | flops 27599998976 | tf_op jit(solution)/shard_map/pallas_call | solution.py:926
  96.1 14.1 %shard_map.235 = (bf16[1024,864]{1,0:T(8,128)(2,1)}, bf16[1024,288]{1,0:T(8,128)(2,1)}, f32[8,1024]{1,0:T(8,128)}, bf16[1024,1152]{1,0:T(8,128)(2,1)}) custom-call(s32[4]{0:T(128)} %get-tuple-element.157.refs_4_.refs_0_, s32[4]{0:T(128)} %get-tuple-element.156.refs_5_.refs_1_, bf16[1024,1152]{1,0:T(8,128)(2,1)} %get-tuple-element.82.refs_2_, ...), custom_call_target="tpu_custom_call" | custom-call | flops 73600000000 | tf_op jit(solution)/shard_map/pallas_call | solution.py:620
  111.8 14.6 %shard_map.236 = (bf16[1024,864]{1,0:T(8,128)(2,1)}, bf16[1024,288]{1,0:T(8,128)(2,1)}, f32[8,1024]{1,0:T(8,128)}, bf16[1024,1152]{1,0:T(8,128)(2,1)}) custom-call(s32[4]{0:T(128)} %get-tuple-element.157.refs_4_.refs_0_, s32[4]{0:T(128)} %get-tuple-element.156.refs_5_.refs_1_, bf16[1024,1152]{1,0:T(8,128)(2,1)} %get-tuple-element.82.refs_2_, ...), custom_call_target="tpu_custom_call" | custom-call | flops 73600000000 | tf_op jit(solution)/shard_map/pallas_call | solution.py:620
  130.8 7.5 %shard_map.238 = (bf16[1024,1152]{1,0:T(8,128)(2,1)}, bf16[1152,1024]{1,0:T(8,128)(2,1)}, f32[1,1152]{1,0:T(1,128)}) custom-call(bf16[1024,1152]{1,0:T(8,128)(2,1)} %pad_maximum_fusion.1.refs_0_.refs_4_, f32[4,6912]{1,0:T(4,128)} %broadcast_add_fusion.refs_1_.refs_5_.refs_13_, s32[1024,128]{1,0:T(8,128)} %broadcast_in_dim.47.refs_2_.refs_5_.refs_6_.refs_14_.refs_10_, ...), custom_call_target="tpu_custom_call" | custom-call | flops 27599998976 | tf_op jit(solution)/shard_map/pallas_call | solution.py:926
  138.3 15.8 %collective-permute-done.3.refs_0_ = bf16[1152,1152]{1,0:T(8,128)(2,1)} collective-permute-done((bf16[1152,1152]{1,0:T(8,128)(2,1)}, bf16[1152,1152]{1,0:T(8,128)(2,1)}, u32[]{:S(2)}, u32[]{:S(2)}) %collective-permute-start.3) | collective-permute-done | bytes 2654240 | tf_op jit(solution)/shard_map/ppermute | solution.py:392
  154.1 14.4 %shard_map.240 = (bf16[1024,864]{1,0:T(8,128)(2,1)}, bf16[1024,288]{1,0:T(8,128)(2,1)}, f32[8,1024]{1,0:T(8,128)}, bf16[1024,1152]{1,0:T(8,128)(2,1)}) custom-call(s32[4]{0:T(128)} %get-tuple-element.157.refs_4_.refs_0_, s32[4]{0:T(128)} %get-tuple-element.156.refs_5_.refs_1_, bf16[1024,1152]{1,0:T(8,128)(2,1)} %get-tuple-element.82.refs_2_, ...), custom_call_target="tpu_custom_call" | custom-call | flops 73600000000 | tf_op jit(solution)/shard_map/pallas_call | solution.py:620
  168.5 3.7 all-gather.6.cloned.1.call-done.refs_0_
  173.8 14.3 %shard_map.242 = (bf16[1024,864]{1,0:T(8,128)(2,1)}, bf16[1024,288]{1,0:T(8,128)(2,1)}, f32[8,1024]{1,0:T(8,128)}, bf16[1024,1152]{1,0:T(8,128)(2,1)}) custom-call(s32[4]{0:T(128)} %get-tuple-element.157.refs_4_.refs_0_, s32[4]{0:T(128)} %get-tuple-element.156.refs_5_.refs_1_, bf16[1024,1152]{1,0:T(8,128)(2,1)} %get-tuple-element.82.refs_2_, ...), custom_call_target="tpu_custom_call" | custom-call | flops 73600000000 | tf_op jit(solution)/shard_map/pallas_call | solution.py:620
  188.1 12.7 %shard_map.243 = (f32[1024,1152]{1,0:T(8,128)}, f32[1024,1152]{1,0:T(8,128)}, bf16[1024,1152]{1,0:T(8,128)(2,1)}, bf16[1152,1024]{1,0:T(8,128)(2,1)}) custom-call(bf16[1024,1152]{1,0:T(8,128)(2,1)} %pad_maximum_fusion.refs_1_.refs_0_.refs_2_, bf16[1024,1152]{1,0:T(8,128)(2,1)} %get-tuple-element.83.refs_1_, bf16[1024,1152]{1,0:T(8,128)(2,1)} %get-tuple-element.85.refs_2_, ...), custom_call_target="tpu_custom_call" | custom-call | flops 55199997952 | tf_op jit(solution)/shard_map/pallas_call | solution.py:926
  200.8 26.9 %shard_map.244 = (bf16[1024,1152]{1,0:T(8,128)(2,1)}, bf16[1024,1152]{1,0:T(8,128)(2,1)}, f32[1,1152]{1,0:T(1,128)}, bf16[1152,2304]{1,0:T(8,128)(2,1)}) custom-call(bf16[1024,1152]{1,0:T(8,128)(2,1)} %get-tuple-element.93.refs_0_, bf16[1024,1152]{1,0:T(8,128)(2,1)} %get-tuple-element.94.refs_1_, bf16[1152,1024]{1,0:T(8,128)(2,1)} %get-tuple-element.95.refs_2_.refs_0_, ...), custom_call_target="tpu_custom_call" | custom-call | flops 124200001536 | tf_op jit(solution)/shard_map/pallas_call | solution.py:483
  228.2 19.7 %shard_map.245 = (bf16[1024,1152]{1,0:T(8,128)(2,1)}, bf16[1024,1152]{1,0:T(8,128)(2,1)}, f32[1,1152]{1,0:T(1,128)}, bf16[1024,1152]{1,0:T(8,128)(2,1)}, bf16[1024,1152]{1,0:T(8,128)(2,1)}) custom-call(bf16[1024,1152]{1,0:T(8,128)(2,1)} %get-tuple-element.93.refs_0_, bf16[1024,1152]{1,0:T(8,128)(2,1)} %get-tuple-element.94.refs_1_, ...), custom_call_target="tpu_custom_call" | custom-call | flops 87399997440 | tf_op jit(solution)/shard_map/pallas_call | solution.py:483
  247.9 12.4 %all-gather.8.cloned.1.call-done.refs_0_ = bf16[1152,2304]{1,0:T(8,128)(2,1)} async-done(((bf16[144,2304]{1,0:T(8,128)(2,1)}), bf16[1152,2304]{1,0:T(8,128)(2,1)}) %all-gather.8.cloned.1.call-update) | async-done | bytes 5308432 | tf_op jit(solution)/shard_map/all_gather | solution.py:1060
  260.3 11.8 %shard_map.247.refs_7_ = bf16[1152,2304]{1,0:T(8,128)(2,1)} custom-call(bf16[1152,1024]{1,0:T(8,128)(2,1)} %get-tuple-element.95.refs_2_.refs_0_, bf16[1152,1024]{1,0:T(8,128)(2,1)} %get-tuple-element.96.refs_3_.refs_1_, bf16[1024,1152]{1,0:T(8,128)(2,1)} %get-tuple-element.99.refs_2_, bf16[1024,1152]{1,0:T(8,128)(2,1)} %get-tuple-element.100.refs_3_, ...), custom_call_target="tpu_custom_call" | custom-call | flops 55199997952 | tf_op jit(solution)/shard_map/pallas_call | solution.py:483
  272.2 27.0 %shard_map.248 = (bf16[1024,1152]{1,0:T(8,128)(2,1)}, bf16[1024,1152]{1,0:T(8,128)(2,1)}, f32[1,1152]{1,0:T(1,128)}, bf16[1152,2304]{1,0:T(8,128)(2,1)}) custom-call(bf16[1024,1152]{1,0:T(8,128)(2,1)} %get-tuple-element.93.refs_0_, bf16[1024,1152]{1,0:T(8,128)(2,1)} %get-tuple-element.94.refs_1_, bf16[1152,1024]{1,0:T(8,128)(2,1)} %get-tuple-element.95.refs_2_.refs_0_, ...), custom_call_target="tpu_custom_call" | custom-call | flops 124200001536 | tf_op jit(solution)/shard_map/pallas_call | solution.py:483
  299.7 19.4 %shard_map.249 = (bf16[1024,1152]{1,0:T(8,128)(2,1)}, bf16[1024,1152]{1,0:T(8,128)(2,1)}, f32[1,1152]{1,0:T(1,128)}, bf16[1024,1152]{1,0:T(8,128)(2,1)}, bf16[1024,1152]{1,0:T(8,128)(2,1)}) custom-call(bf16[1024,1152]{1,0:T(8,128)(2,1)} %get-tuple-element.93.refs_0_, bf16[1024,1152]{1,0:T(8,128)(2,1)} %get-tuple-element.94.refs_1_, ...), custom_call_target="tpu_custom_call" | custom-call | flops 87399997440 | tf_op jit(solution)/shard_map/pallas_call | solution.py:483
  321.5 11.9 %shard_map.250.refs_16_ = bf16[1152,2304]{1,0:T(8,128)(2,1)} custom-call(bf16[1152,1024]{1,0:T(8,128)(2,1)} %get-tuple-element.95.refs_2_.refs_0_, bf16[1152,1024]{1,0:T(8,128)(2,1)} %get-tuple-element.96.refs_3_.refs_1_, bf16[1024,1152]{1,0:T(8,128)(2,1)} %get-tuple-element.111.refs_2_, bf16[1024,1152]{1,0:T(8,128)(2,1)} %get-tuple-element.112.refs_3_, ...), custom_call_target="tpu_custom_call" | custom-call | flops 55199997952 | tf_op jit(solution)/shard_map/pallas_call | solution.py:483
  333.4 21.6 %shard_map.251 = (bf16[1024,1152]{1,0:T(8,128)(2,1)}, f32[1024,1152]{1,0:T(8,128)}, bf16[1024,1152]{1,0:T(8,128)(2,1)}, bf16[1152,1024]{1,0:T(8,128)(2,1)}, f32[1,1152]{1,0:T(1,128)}, /*index=5*/f32[4,4608]{1,0:T(4,128)}) custom-call(s32[8]{0:T(128)} %get-tuple-element.155.refs_6_.refs_0_, s32[8]{0:T(128)} %get-tuple-element.154.refs_7_.refs_1_, ...), custom_call_target="tpu_custom_call" | custom-call | flops 23000000512 | tf_op jit(solution)/shard_map/pallas_call | solution.py:926
  357.8 23.2 %shard_map.252 = (bf16[1024,864]{1,0:T(8,128)(2,1)}, f32[1,864]{1,0:T(1,128)}, bf16[1152,1152]{1,0:T(8,128)(2,1)}) custom-call(s32[4]{0:T(128)} %get-tuple-element.157.refs_4_.refs_0_, s32[4]{0:T(128)} %get-tuple-element.156.refs_5_.refs_1_, s32[8]{0:T(128)} %shift-right-arithmetic_add_fusion.refs_2_, bf16[1024,864]{1,0:T(8,128)(2,1)} %get-tuple-element.115.refs_3_, ...), custom_call_target="tpu_custom_call" | custom-call | flops 4600000000 | tf_op jit(solution)/shard_map/pallas_call | solution.py:769
  383.3 23.7 %shard_map.254 = (bf16[1024,864]{1,0:T(8,128)(2,1)}, f32[1,864]{1,0:T(1,128)}, bf16[1152,1152]{1,0:T(8,128)(2,1)}) custom-call(s32[4]{0:T(128)} %get-tuple-element.157.refs_4_.refs_0_, s32[4]{0:T(128)} %get-tuple-element.156.refs_5_.refs_1_, s32[8]{0:T(128)} %shift-right-arithmetic_add_fusion.refs_2_, bf16[1024,864]{1,0:T(8,128)(2,1)} %get-tuple-element.127.refs_3_, ...), custom_call_target="tpu_custom_call" | custom-call | flops 4600000000 | tf_op jit(solution)/shard_map/pallas_call | solution.py:769
  409.6 5.6 all-to-all-start.2
  418.7 23.9 %shard_map.255 = (bf16[1024,864]{1,0:T(8,128)(2,1)}, f32[1,864]{1,0:T(1,128)}, bf16[4,144,1152]{2,1,0:T(8,128)(2,1)}, bf16[4,144,1152]{2,1,0:T(8,128)(2,1)}) custom-call(s32[4]{0:T(128)} %get-tuple-element.157.refs_4_.refs_0_, s32[4]{0:T(128)} %get-tuple-element.156.refs_5_.refs_1_, s32[8]{0:T(128)} %shift-right-arithmetic_add_fusion.refs_2_, ...), custom_call_target="tpu_custom_call" | custom-call | flops 4600000000 | tf_op jit(solution)/shard_map/pallas_call | solution.py:769
  444.6 24.0 %shard_map.256 = (bf16[1024,864]{1,0:T(8,128)(2,1)}, f32[1,864]{1,0:T(1,128)}, bf16[4,144,1152]{2,1,0:T(8,128)(2,1)}, bf16[4,144,1152]{2,1,0:T(8,128)(2,1)}) custom-call(s32[4]{0:T(128)} %get-tuple-element.157.refs_4_.refs_0_, s32[4]{0:T(128)} %get-tuple-element.156.refs_5_.refs_1_, s32[8]{0:T(128)} %shift-right-arithmetic_add_fusion.refs_2_, ...), custom_call_target="tpu_custom_call" | custom-call | flops 4600000000 | tf_op jit(solution)/shard_map/pallas_call | solution.py:769
  472.1 13.3 %collective-permute-done.13.refs_0_ = bf16[4,144,1152]{2,1,0:T(8,128)(2,1)S(1)} collective-permute-done((bf16[4,144,1152]{2,1,0:T(8,128)(2,1)}, bf16[4,144,1152]{2,1,0:T(8,128)(2,1)S(1)}, u32[]{:S(2)}, u32[]{:S(2)}) %collective-permute-start.13) | collective-permute-done | bytes 1327136 | tf_op jit(solution)/shard_map/ppermute | solution.py:392
  491.5 4.0 collective-permute-start.22
  496.1 17.8 %shard_map.258.refs_1_.refs_4_ = f32[1024,1152]{1,0:T(8,128)} custom-call(bf16[1024,864]{1,0:T(8,128)(2,1)} %get-tuple-element.133.q0, bf16[1024,864]{1,0:T(8,128)(2,1)} %get-tuple-element.134.q1, bf16[1024,864]{1,0:T(8,128)(2,1)} %get-tuple-element.135.q2, bf16[1024,864]{1,0:T(8,128)(2,1)} %get-tuple-element.136.q3, ...), custom_call_target="tpu_custom_call" | custom-call | flops 4600000000 | tf_op jit(solution)/shard_map/pallas_call | solution.py:891
  513.9 4.9 collective-permute-done.15.refs_0_
  527.3 11.2 %shard_map.260 = (bf16[1024,1152]{1,0:T(8,128)(2,1)}, f32[4,2304]{1,0:T(4,128)}) custom-call(s32[8]{0:T(128)} %get-tuple-element.155.refs_6_.refs_0_, s32[8]{0:T(128)} %get-tuple-element.154.refs_7_.refs_1_, bf16[1024,1152]{1,0:T(8,128)(2,1)} %pad_maximum_fusion.refs_1_.refs_0_.refs_2_, f32[1024,1152]{1,0:T(8,128)} %get-tuple-element.121.refs_3_, ...), custom_call_target="tpu_custom_call" | custom-call | flops 4600000000 | tf_op jit(solution)/shard_map/pallas_call | solution.py:926
  545.3 4.2 all-to-all-start.3
  552.7 16.9 %collective-permute-done.18 = bf16[144,1152]{1,0:T(8,128)(2,1)} collective-permute-done((bf16[144,1152]{1,0:T(8,128)(2,1)S(1)}, bf16[144,1152]{1,0:T(8,128)(2,1)}, u32[]{:S(2)}, u32[]{:S(2)}) %collective-permute-start.18) | collective-permute-done | bytes 331808 | tf_op jit(solution)/shard_map/ppermute | solution.py:392
  (286 shorter events, 100.9 us)
Async XLA Ops:
  7.2 87.1 %all-gather.4.cloned.1.call-start = ((), (), s32[]{:S(2)}) async-start(), calls=%async_computation.6 | async-start | bytes 2985984 | tf_op jit(solution)/shard_map/all_gather | solution.py:1024
  12.0 18.0 %all-to-all-start = ((bf16[8,16,144]{2,1,0:T(8,128)(2,1)}), bf16[8,16,144]{2,1,0:T(8,128)(2,1)S(1)}, u32[]{:S(2)}, u32[]{:S(2)}) async-start(bf16[8,16,144]{2,1,0:T(8,128)(2,1)} %shard_map.229), calls=%async_computation | async-start | bytes 131072 | tf_op jit(solution)/shard_map/all_to_all | solution.py:1037
  20.3 24.6 %collective-permute-start = (bf16[512,1152]{1,0:T(8,128)(2,1)}, bf16[512,1152]{1,0:T(8,128)(2,1)S(1)}, u32[]{:S(2)}, u32[]{:S(2)}) collective-permute-start(bf16[512,1152]{1,0:T(8,128)(2,1)} %dynamic-slice_bitcast_fusion.2), channel_id=1, source_target_pairs={{0,1},{1,0},{2,3},{3,2},{4,5},{5,4},{6,7},{7,6},{8,9},{9,8},{10,11... | collective-permute-start | bytes 3538952 | tf_op jit(solution)/shard_map/ppermute | solution.py:392
  32.0 48.6 %all-to-all-start.1 = ((f32[32,4,1728]{2,1,0:T(4,128)}), f32[32,4,1728]{2,1,0:T(4,128)S(1)}, u32[]{:S(2)}, u32[]{:S(2)}) async-start(f32[32,4,1728]{2,1,0:T(4,128)} %copy.73.refs_1_), calls=%async_computation.1 | async-start | bytes 1835008 | tf_op jit(solution)/shard_map/all_to_all | solution.py:1054
  38.1 134.1 %all-gather.6.cloned.1.call-start = ((), (), s32[]{:S(2)}) async-start(), calls=%async_computation.7 | async-start | bytes 5971968 | tf_op jit(solution)/shard_map/all_gather | solution.py:1059
  43.1 41.2 %collective-permute-start.1 = (bf16[144,2304]{1,0:T(8,128)(2,1)}, bf16[144,2304]{1,0:T(8,128)(2,1)S(1)}, u32[]{:S(2)}, u32[]{:S(2)}) collective-permute-start(bf16[144,2304]{1,0:T(8,128)(2,1)} %shard_map.231), channel_id=1, source_target_pairs={{0,2},{1,3},{2,0},{3,1},{4,6},{5,7},{6,4},{7,5},{8,10},{9,11},{10,... | collective-permute-start | bytes 1990664 | tf_op jit(solution)/shard_map/ppermute | solution.py:392
  85.3 175.1 %all-gather.8.cloned.1.call-start = ((), (), s32[]{:S(2)}) async-start(), calls=%async_computation.8 | async-start | bytes 5971968 | tf_op jit(solution)/shard_map/all_gather | solution.py:1060
  85.3 41.1 %collective-permute-start.4 = (bf16[512,1152]{1,0:T(8,128)(2,1)}, bf16[512,1152]{1,0:T(8,128)(2,1)}, u32[]{:S(2)}, u32[]{:S(2)}) collective-permute-start(bf16[512,1152]{1,0:T(8,128)(2,1)} %get-tuple-element.178), channel_id=1, source_target_pairs={{0,1},{1,0},{2,3},{3,2},{4,5},{5,4},{6,7},{7,6},{8,9},{9,8},{10,11... | collective-permute-start | bytes 3538952 | tf_op jit(solution)/shard_map/ppermute | solution.py:392
  86.0 297.2 %reduce-scatter.3.cloned.1.call-start = ((), (), s32[]{:S(2)}) async-start(), calls=%async_computation.9 | async-start | bytes 5971968 | tf_op jit(solution)/shard_map/reduce_scatter | solution.py:1115
  94.3 59.8 %collective-permute-start.3 = (bf16[1152,1152]{1,0:T(8,128)(2,1)}, bf16[1152,1152]{1,0:T(8,128)(2,1)}, u32[]{:S(2)}, u32[]{:S(2)}) collective-permute-start(bf16[1152,1152]{1,0:T(8,128)(2,1)} %shard_map.234.refs_3_.refs_8_.w0), channel_id=1, source_target_pairs={{0,2},{1,3},{2,0},{3,1},{4,6},{5,7},{6,4},{7,5},{8,10},{9,11},{10,... | collective-permute-start | bytes 7962632 | tf_op jit(solution)/shard_map/ppermute | solution.py:392
  96.1 14.1 %collective-permute-start.2 = (bf16[1152,1152]{1,0:T(8,128)(2,1)}, bf16[1152,1152]{1,0:T(8,128)(2,1)S(1)}, u32[]{:S(2)}, u32[]{:S(2)}) collective-permute-start(bf16[1152,1152]{1,0:T(8,128)(2,1)} %shard_map.234.refs_3_.refs_8_.w0), channel_id=1, source_target_pairs={{0,1},{1,0},{2,3},{3,2},{4,5},{5,4},{6,7},{7,6},{8,9},{9,8},{10,11... | collective-permute-start | bytes 7962632 | tf_op jit(solution)/shard_map/ppermute | solution.py:392
  154.1 18.2 %collective-permute-start.5 = (bf16[1152,1152]{1,0:T(8,128)(2,1)}, bf16[1152,1152]{1,0:T(8,128)(2,1)S(1)}, u32[]{:S(2)}, u32[]{:S(2)}) collective-permute-start(bf16[1152,1152]{1,0:T(8,128)(2,1)} %shard_map.239.refs_3_.refs_8_.w2), channel_id=1, source_target_pairs={{0,1},{1,0},{2,3},{3,2},{4,5},{5,4},{6,7},{7,6},{8,9},{9,8},{10,11... | collective-permute-start | bytes 7962632 | tf_op jit(solution)/shard_map/ppermute | solution.py:392
  172.3 28.5 %collective-permute-start.6 = (bf16[1152,2304]{1,0:T(8,128)(2,1)}, bf16[1152,2304]{1,0:T(8,128)(2,1)}, u32[]{:S(2)}, u32[]{:S(2)}) collective-permute-start(bf16[1152,2304]{1,0:T(8,128)(2,1)} %shard_map.241.refs_8_.refs_2_.refs_3_), channel_id=1, source_target_pairs={{0,1},{1,0},{2,3},{3,2},{4,5},{5,4},{6,7},{7,6},{8,9},{9,8},{10,11... | collective-permute-start | bytes 15925256 | tf_op jit(solution)/shard_map/ppermute | solution.py:392
  227.7 32.6 %collective-permute-start.8 = (bf16[1152,2304]{1,0:T(8,128)(2,1)}, bf16[1152,2304]{1,0:T(8,128)(2,1)}, u32[]{:S(2)}, u32[]{:S(2)}) collective-permute-start(bf16[1152,2304]{1,0:T(8,128)(2,1)} %get-tuple-element.101), channel_id=1, source_target_pairs={{0,1},{1,0},{2,3},{3,2},{4,5},{5,4},{6,7},{7,6},{8,9},{9,8},{10,11... | collective-permute-start | bytes 15925256 | tf_op jit(solution)/shard_map/ppermute | solution.py:392
  260.3 11.9 %collective-permute-start.7 = (bf16[1152,2304]{1,0:T(8,128)(2,1)}, bf16[1152,2304]{1,0:T(8,128)(2,1)}, u32[]{:S(2)}, u32[]{:S(2)}) collective-permute-start(bf16[1152,2304]{1,0:T(8,128)(2,1)} %shard_map.246.refs_5_.refs_2_.refs_3_), channel_id=1, source_target_pairs={{0,1},{1,0},{2,3},{3,2},{4,5},{5,4},{6,7},{7,6},{8,9},{9,8},{10,11... | collective-permute-start | bytes 15925256 | tf_op jit(solution)/shard_map/ppermute | solution.py:392
  272.2 255.2 %reduce-scatter.5.cloned.1.call-start = ((), (), s32[]{:S(2)}) async-start(), calls=%async_computation.10 | async-start | bytes 5971968 | tf_op jit(solution)/shard_map/reduce_scatter | solution.py:1120
  299.2 19.9 %collective-permute-start.9 = (bf16[1152,2304]{1,0:T(8,128)(2,1)}, bf16[1152,2304]{1,0:T(8,128)(2,1)S(1)}, u32[]{:S(2)}, u32[]{:S(2)}) collective-permute-start(bf16[1152,2304]{1,0:T(8,128)(2,1)} %get-tuple-element.113), channel_id=1, source_target_pairs={{0,1},{1,0},{2,3},{3,2},{4,5},{5,4},{6,7},{7,6},{8,9},{9,8},{10,11... | collective-permute-start | bytes 15925256 | tf_op jit(solution)/shard_map/ppermute | solution.py:392
  356.5 24.6 %collective-permute-start.10 = (bf16[512,1152]{1,0:T(8,128)(2,1)S(1)}, bf16[512,1152]{1,0:T(8,128)(2,1)S(1)}, u32[]{:S(2)}, u32[]{:S(2)}) collective-permute-start(bf16[512,1152]{1,0:T(8,128)(2,1)S(1)} %constant_dynamic-slice_fusion.1), channel_id=1, source_target_pairs={{0,1},{1,0},{2,3},{3,2},{4,5},{5,4},{6,7},{7,6},{8,9},{9,8},{10,11... | collective-permute-start | bytes 3538952 | tf_op jit(solution)/shard_map/ppermute | solution.py:392
  407.7 36.9 %collective-permute-start.11 = (bf16[1152,1152]{1,0:T(8,128)(2,1)}, bf16[1152,1152]{1,0:T(8,128)(2,1)}, u32[]{:S(2)}, u32[]{:S(2)}) collective-permute-start(bf16[1152,1152]{1,0:T(8,128)(2,1)} %get-tuple-element.124), channel_id=1, source_target_pairs={{0,1},{1,0},{2,3},{3,2},{4,5},{5,4},{6,7},{7,6},{8,9},{9,8},{10,11... | collective-permute-start | bytes 7962632 | tf_op jit(solution)/shard_map/ppermute | solution.py:392
  409.6 59.3 %all-to-all-start.2 = ((bf16[32,57,128]{2,1,0:T(8,128)(2,1)}), bf16[32,57,128]{2,1,0:T(8,128)(2,1)}, u32[]{:S(2)}, u32[]{:S(2)}) async-start(bf16[32,57,128]{2,1,0:T(8,128)(2,1)} %pad_maximum_fusion.7), calls=%async_computation.4 | async-start | bytes 1048576 | tf_op jit(solution)/shard_map/all_to_all | solution.py:992
  415.3 56.8 %collective-permute-start.14 = (bf16[144,2304]{1,0:T(8,128)(2,1)}, bf16[144,2304]{1,0:T(8,128)(2,1)}, u32[]{:S(2)}, u32[]{:S(2)}) collective-permute-start(bf16[144,2304]{1,0:T(8,128)(2,1)} %reduce-scatter.3.cloned.1.call-done.refs_14_), channel_id=1, source_target_pairs={{0,2},{1,3},{2,0},{3,1},{4,6},{5,7},{6,4},{7,5},{8,10},{9,11},{10,... | collective-permute-start | bytes 1990664 | tf_op jit(solution)/shard_map/ppermute | solution.py:392
  442.6 42.8 %collective-permute-start.13 = (bf16[4,144,1152]{2,1,0:T(8,128)(2,1)}, bf16[4,144,1152]{2,1,0:T(8,128)(2,1)S(1)}, u32[]{:S(2)}, u32[]{:S(2)}) collective-permute-start(bf16[4,144,1152]{2,1,0:T(8,128)(2,1)} %get-tuple-element.138), channel_id=1, source_target_pairs={{0,4},{1,5},{2,6},{3,7},{4,0},{5,1},{6,2},{7,3},{8,12},{9,13},{10,... | collective-permute-start | bytes 3981320 | tf_op jit(solution)/shard_map/ppermute | solution.py:392
  468.7 50.1 %collective-permute-start.15 = (bf16[4,144,1152]{2,1,0:T(8,128)(2,1)}, bf16[4,144,1152]{2,1,0:T(8,128)(2,1)S(1)}, u32[]{:S(2)}, u32[]{:S(2)}) collective-permute-start(bf16[4,144,1152]{2,1,0:T(8,128)(2,1)} %get-tuple-element.142), channel_id=1, source_target_pairs={{0,4},{1,5},{2,6},{3,7},{4,0},{5,1},{6,2},{7,3},{8,12},{9,13},{10,... | collective-permute-start | bytes 3981320 | tf_op jit(solution)/shard_map/ppermute | solution.py:392
  491.5 48.2 %collective-permute-start.22 = (bf16[144,1152]{1,0:T(8,128)(2,1)}, bf16[144,1152]{1,0:T(8,128)(2,1)S(1)}, u32[]{:S(2)}, u32[]{:S(2)}) collective-permute-start(bf16[144,1152]{1,0:T(8,128)(2,1)} %get-tuple-element.172), channel_id=1, source_target_pairs={{0,24},{1,25},{2,26},{3,27},{4,28},{5,29},{6,30},{7,31},{8,16},{9,... | collective-permute-start | bytes 995336 | tf_op jit(solution)/shard_map/ppermute | solution.py:392
  495.5 44.4 %collective-permute-start.21 = (bf16[144,1152]{1,0:T(8,128)(2,1)}, bf16[144,1152]{1,0:T(8,128)(2,1)S(1)}, u32[]{:S(2)}, u32[]{:S(2)}) collective-permute-start(bf16[144,1152]{1,0:T(8,128)(2,1)} %get-tuple-element.173), channel_id=1, source_target_pairs={{0,16},{1,17},{2,18},{3,19},{4,20},{5,21},{6,22},{7,23},{8,24},{9,... | collective-permute-start | bytes 995336 | tf_op jit(solution)/shard_map/ppermute | solution.py:392
  495.5 44.4 %collective-permute-start.20 = (bf16[144,1152]{1,0:T(8,128)(2,1)}, bf16[144,1152]{1,0:T(8,128)(2,1)}, u32[]{:S(2)}, u32[]{:S(2)}) collective-permute-start(bf16[144,1152]{1,0:T(8,128)(2,1)} %get-tuple-element.174), channel_id=1, source_target_pairs={{0,8},{1,9},{2,10},{3,11},{4,12},{5,13},{6,14},{7,15},{8,0},{9,1},... | collective-permute-start | bytes 995336 | tf_op jit(solution)/shard_map/ppermute | solution.py:392
  522.7 30.0 %collective-permute-start.17 = (bf16[144,1152]{1,0:T(8,128)(2,1)S(1)}, bf16[144,1152]{1,0:T(8,128)(2,1)}, u32[]{:S(2)}, u32[]{:S(2)}) collective-permute-start(bf16[144,1152]{1,0:T(8,128)(2,1)S(1)} %get-tuple-element.168), channel_id=1, source_target_pairs={{0,8},{1,9},{2,10},{3,11},{4,12},{5,13},{6,14},{7,15},{8,0},{9,1},... | collective-permute-start | bytes 995336 | tf_op jit(solution)/shard_map/ppermute | solution.py:392
  522.7 30.0 %collective-permute-start.19 = (bf16[144,1152]{1,0:T(8,128)(2,1)S(1)}, bf16[144,1152]{1,0:T(8,128)(2,1)}, u32[]{:S(2)}, u32[]{:S(2)}) collective-permute-start(bf16[144,1152]{1,0:T(8,128)(2,1)S(1)} %get-tuple-element.169), channel_id=1, source_target_pairs={{0,24},{1,25},{2,26},{3,27},{4,28},{5,29},{6,30},{7,31},{8,16},{9,... | collective-permute-start | bytes 995336 | tf_op jit(solution)/shard_map/ppermute | solution.py:392
  539.8 29.8 %collective-permute-start.18 = (bf16[144,1152]{1,0:T(8,128)(2,1)S(1)}, bf16[144,1152]{1,0:T(8,128)(2,1)}, u32[]{:S(2)}, u32[]{:S(2)}) collective-permute-start(bf16[144,1152]{1,0:T(8,128)(2,1)S(1)} %get-tuple-element.170), channel_id=1, source_target_pairs={{0,16},{1,17},{2,18},{3,19},{4,20},{5,21},{6,22},{7,23},{8,24},{9,... | collective-permute-start | bytes 995336 | tf_op jit(solution)/shard_map/ppermute | solution.py:392
  542.8 26.8 %collective-permute-start.23 = (bf16[144,1152]{1,0:T(8,128)(2,1)}, bf16[144,1152]{1,0:T(8,128)(2,1)S(1)}, u32[]{:S(2)}, u32[]{:S(2)}) collective-permute-start(bf16[144,1152]{1,0:T(8,128)(2,1)} %add_convert_fusion), channel_id=1, source_target_pairs={{0,2},{1,3},{2,0},{3,1},{4,6},{5,7},{6,4},{7,5},{8,10},{9,11},{10,... | collective-permute-start | bytes 995336 | tf_op jit(solution)/shard_map/ppermute | solution.py:392
  545.3 32.6 %all-to-all-start.3 = ((bf16[32,93,128]{2,1,0:T(8,128)(2,1)}), bf16[32,93,128]{2,1,0:T(8,128)(2,1)S(1)}, u32[]{:S(2)}, u32[]{:S(2)}) async-start(bf16[32,93,128]{2,1,0:T(8,128)(2,1)} %pad_maximum_fusion.4), calls=%async_computation.5 | async-start | bytes 1572864 | tf_op jit(solution)/shard_map/all_to_all | solution.py:992
  551.1 22.0 %collective-permute-start.16 = (bf16[512,1152]{1,0:T(8,128)(2,1)S(1)}, bf16[512,1152]{1,0:T(8,128)(2,1)S(1)}, u32[]{:S(2)}, u32[]{:S(2)}) collective-permute-start(bf16[512,1152]{1,0:T(8,128)(2,1)S(1)} %constant_dynamic-slice_fusion), channel_id=1, source_target_pairs={{0,1},{1,0},{2,3},{3,2},{4,5},{5,4},{6,7},{7,6},{8,9},{9,8},{10,11... | collective-permute-start | bytes 3538952 | tf_op jit(solution)/shard_map/ppermute | solution.py:392
  (40 other events, 399.7 us)
Sparse Core Ops, SparseCore 0:
  10.5 72.8 all-gather.3
  86.2 86.0 all-gather.5
  175.0 85.2 all-gather.7
  272.3 102.5 reduce-scatter.2
  378.7 148.5 reduce-scatter.4
